TPU v7x, 32 devices: a whole 2x2x4 slice. The times are simulated.
32 devices in a mesh: section: 2 (over core), seq: 4 (over y, x), wt: 4 (over z).
Axes of the slice: x: 2, y: 2, z: 4, core: 2. Of those that a mesh axis runs over, the one named last changes fastest.
Arguments:
- tokens: float32 [2, 4, 512, 1536], P(None, 'wt', 'seq'), may hold values from -6 to 6
- cotangent: float32 [2, 4, 512, 1536], P(None, 'wt', 'seq'), may hold values from -6 to 6
- norm_gain: float32 [2, 1536], P('section'), may hold values from 0.5 to 1.5
- w_in: bfloat16 [2, 1536, 6448], P('section', 'wt'), may hold values from -0.15625 to 0.15625
- conv_w: float32 [2, 4, 3328], P('section'), may hold values from -3 to 3
- conv_b: float32 [2, 3328], P('section'), may hold values from -2 to 2
- dt_bias: float32 [2, 48], P('section'), may hold values from -5 to -1
- a_log: float32 [2, 48], P('section'), may hold values from -2 to 1.5
- skip_d: float32 [2, 48], P('section'), may hold values from 0.5 to 1.5
- gate_gain: float32 [2, 3072], P('section'), may hold values from 0.5 to 1.5
- w_out: bfloat16 [2, 3072, 1536], P('section', 'wt'), may hold values from -0.109375 to 0.109375
Outputs:
- section_out: float32 [2, 2, 4, 512, 1536], P('section', None, 'wt', 'seq')
- input_grad: float32 [2, 2, 4, 512, 1536], P('section', None, 'wt', 'seq')
- g_norm_gain: float32 [2, 1536], P('section')
- g_w_in: float32 [2, 1536, 6448], P('section', 'wt')
- g_conv_w: float32 [2, 4, 3328], P('section')
- g_conv_b: float32 [2, 3328], P('section')
- g_dt_bias: float32 [2, 48], P('section')
- g_a_log: float32 [2, 48], P('section')
- g_skip_d: float32 [2, 48], P('section')
- g_gate_gain: float32 [2, 3072], P('section')
- g_w_out: float32 [2, 3072, 1536], P('section', 'wt')
All inputs are finite; a program needn't handle non-finite values.
Results may differ from a plain program's by a relative error of at most 0.019.
Values may be sent and summed in bfloat16 or wider, within the bound.
A program may use at most 384 MiB of HBM per device.

v0:
```python
import jax
import jax.numpy as jnp
from jax import lax
from jax.sharding import PartitionSpec as P

D = 1536
HEADS = 48
HEAD_DIM = 64
STATE = 128
KERNEL = 4
SPAN = 256
INNER = 3072
CONV = 3328


EPSILON = 1e-05
EXACT_DOT = lax.Precision.HIGHEST


def passed_along(block, axis, distance):
    devices = range(lax.axis_size(axis))
    route = [(i - distance, i) for i in devices if i - distance in devices]
    return lax.ppermute(block, axis, route)


def silu_slope(values):
    sigma = jax.nn.sigmoid(values)
    return sigma * (1.0 + values * (1.0 - sigma))


def conv_silu(seq_in, kernel_w, conv_bias):
    length = seq_in.shape[0]
    padded = jnp.concatenate([jnp.zeros((KERNEL - 1, seq_in.shape[1]), jnp.float32), seq_in], 0)
    conv_sum = conv_bias[None, :] + jnp.zeros_like(seq_in)
    for k in range(KERNEL):
        conv_sum = conv_sum + kernel_w[k][None, :] * padded[k : k + length]
    return jax.nn.silu(conv_sum)


def mixer(x_raw, bc_raw, dt_raw, conv_wx, conv_bx, conv_wbc, conv_bbc, dt_bias, a_log, skip_d):
    x_conv = conv_silu(x_raw, conv_wx, conv_bx)
    bc_conv = conv_silu(bc_raw, conv_wbc, conv_bbc)
    head_count = dt_bias.shape[0]
    length = x_conv.shape[0]
    blocks = length // SPAN
    step_size = jax.nn.softplus(dt_raw + dt_bias[None, :])
    step_rate = -step_size * jnp.exp(a_log)[None, :]
    x_blocks = x_conv.reshape(blocks, SPAN, head_count, HEAD_DIM)
    b_blocks = bc_conv[:, :STATE].reshape(blocks, SPAN, STATE)
    c_blocks = bc_conv[:, STATE:].reshape(blocks, SPAN, STATE)
    step_blocks = step_size.reshape(blocks, SPAN, head_count)
    cum_rate = jnp.cumsum(step_rate.reshape(blocks, SPAN, head_count), axis=1)
    scores = jnp.einsum("ctn,csn->cts", c_blocks, b_blocks, precision=EXACT_DOT)
    row_ids = lax.broadcasted_iota(jnp.int32, (SPAN, SPAN), 0)
    col_ids = lax.broadcasted_iota(jnp.int32, (SPAN, SPAN), 1)
    causal = (row_ids >= col_ids)[None, :, :, None]
    rate_diff = cum_rate[:, :, None, :] - cum_rate[:, None, :, :]
    decay_mat = jnp.where(causal, jnp.exp(jnp.where(causal, rate_diff, 0.0)), 0.0)
    mix_weight = scores[:, :, :, None] * decay_mat * step_blocks[:, None, :, :]
    y_inner = jnp.einsum("ctsh,cshp->cthp", mix_weight, x_blocks, precision=EXACT_DOT)
    last_rate = cum_rate[:, -1, :]
    tail_weight = jnp.exp(last_rate[:, None, :] - cum_rate) * step_blocks
    states = jnp.einsum(
        "csn,cshp->chnp", b_blocks, x_blocks * tail_weight[:, :, :, None], precision=EXACT_DOT
    )

    def advance(carried, scan_item):
        block_state, block_rate = scan_item
        return (carried * jnp.exp(block_rate)[:, None, None] + block_state, carried)

    _, before = lax.scan(
        advance, jnp.zeros((head_count, STATE, HEAD_DIM), jnp.float32), (states, last_rate)
    )
    y_outer = (
        jnp.einsum("ctn,chnp->cthp", c_blocks, before, precision=EXACT_DOT)
        * jnp.exp(cum_rate)[:, :, :, None]
    )
    y_total = y_inner + y_outer + skip_d[None, None, :, None] * x_blocks
    return y_total.reshape(length, head_count * HEAD_DIM)


def outer_rows(left, right):
    return lax.dot_general(
        left, right, (((0,), (0,)), ((), ())), preferred_element_type=jnp.float32
    )


def local(
    tokens, cotangent, norm_gain, w_in, conv_w, conv_b, dt_bias, a_log, skip_d, gate_gain, w_out
):
    first_section = lax.axis_index("section") == 0
    micro_count = tokens.shape[0]
    tok_rows = tokens.shape[2]
    group_size = lax.axis_size("seq")
    heads_here = HEADS // group_size
    head_start = lax.axis_index("seq") * heads_here
    chan_start = head_start * HEAD_DIM
    chan_count = heads_here * HEAD_DIM
    gain_in = norm_gain[0]
    gain_gate = gate_gain[0]
    conv_here = conv_w[0]
    bias_here = conv_b[0]
    head_params = (
        lax.dynamic_slice_in_dim(conv_here, chan_start, chan_count, 1),
        lax.dynamic_slice_in_dim(bias_here, chan_start, chan_count, 0),
        conv_here[:, INNER:],
        bias_here[INNER:],
        lax.dynamic_slice_in_dim(dt_bias[0], head_start, heads_here, 0),
        lax.dynamic_slice_in_dim(a_log[0], head_start, heads_here, 0),
        lax.dynamic_slice_in_dim(skip_d[0], head_start, heads_here, 0),
    )
    in_full, out_full = (
        lax.all_gather(w_in, "wt", axis=1, tiled=True),
        lax.all_gather(w_out, "wt", axis=1, tiled=True),
    )
    in_weight = in_full[0]
    out_weight = out_full[0]
    received = jnp.zeros((tok_rows, D), jnp.float32)
    outs_list = []
    saves = []
    for step_index in range(micro_count + 1):
        own_in = tokens[min(step_index, micro_count - 1), 0]
        h_in = jnp.where(first_section, own_in, received)
        forward_inv_rms = lax.rsqrt(jnp.mean(h_in * h_in, axis=-1, keepdims=True) + EPSILON)
        forward_normed_in = (h_in * forward_inv_rms * gain_in[None, :]).astype(jnp.bfloat16)
        projected = jnp.dot(
            forward_normed_in, in_weight, preferred_element_type=jnp.float32
        ).astype(jnp.bfloat16)
        forward_gate_raw = projected[:, :INNER]
        forward_x_heads = lax.all_to_all(
            projected[:, INNER : 2 * INNER], "seq", split_axis=1, concat_axis=0, tiled=True
        )
        forward_dt_heads = lax.all_to_all(
            projected[:, 2 * INNER + 2 * STATE :], "seq", split_axis=1, concat_axis=0, tiled=True
        )
        forward_bc_whole = lax.all_gather(
            projected[:, 2 * INNER : 2 * INNER + 2 * STATE], "seq", axis=0, tiled=True
        )
        mixed = mixer(
            forward_x_heads.astype(jnp.float32),
            forward_bc_whole.astype(jnp.float32),
            forward_dt_heads.astype(jnp.float32),
            *head_params
        ).astype(jnp.bfloat16)
        forward_mixed_tok = lax.all_to_all(mixed, "seq", split_axis=0, concat_axis=1, tiled=True)
        forward_gate_act = jax.nn.silu(forward_gate_raw.astype(jnp.float32))
        forward_v = forward_mixed_tok.astype(jnp.float32) * forward_gate_act
        forward_inv_rms2 = lax.rsqrt(
            jnp.mean(forward_v * forward_v, axis=-1, keepdims=True) + EPSILON
        )
        forward_normed_out = (forward_v * forward_inv_rms2 * gain_gate[None, :]).astype(
            jnp.bfloat16
        )
        h_out = h_in + jnp.dot(forward_normed_out, out_weight, preferred_element_type=jnp.float32)
        h_out, saved = (
            h_out,
            (
                h_in,
                forward_normed_in,
                forward_gate_raw,
                forward_x_heads,
                forward_dt_heads,
                forward_bc_whole,
                forward_mixed_tok,
                forward_normed_out,
            ),
        )
        outs_list.append(h_out)
        saves.append(saved)
        if step_index < micro_count:
            received = passed_along(h_out, "section", 1)
    again_in, again_out = (
        lax.all_gather(w_in, "wt", axis=1, tiled=True),
        lax.all_gather(w_out, "wt", axis=1, tiled=True),
    )
    back_weights = (again_in[0], again_out[0])
    piece_list = []
    acc_norm = jnp.zeros((D,), jnp.float32)
    acc_gate = jnp.zeros((INNER,), jnp.float32)
    acc_conv_w = jnp.zeros((KERNEL, CONV), jnp.float32)
    acc_conv_b = jnp.zeros((CONV,), jnp.float32)
    acc_dt_bias = jnp.zeros((HEADS,), jnp.float32)
    acc_a_log = jnp.zeros((HEADS,), jnp.float32)
    acc_skip = jnp.zeros((HEADS,), jnp.float32)
    received = jnp.zeros((tok_rows, D), jnp.float32)
    d_list = []
    for step_index in range(micro_count + 1):
        if step_index < micro_count:
            own_grad = cotangent[step_index, 0]
        else:
            own_grad = jnp.zeros((tok_rows, D), jnp.float32)
        out_grad = jnp.where(first_section, received, own_grad)
        saved = jax.tree.map(
            lambda lower_val, upper_val: jnp.where(first_section, lower_val, upper_val),
            saves[max(step_index - 1, 0)],
            saves[min(step_index + 1, micro_count)],
        )
        backward_h_in, normed_in, gate_raw, x_heads, dt_heads, bc_whole, mixed_tok, normed_out = (
            saved
        )
        in_weight_b, out_weight_b = back_weights
        out_grad_b = out_grad.astype(jnp.bfloat16)
        d_normed = lax.dot_general(
            out_grad_b, out_weight_b, (((1,), (1,)), ((), ())), preferred_element_type=jnp.float32
        )
        gate_in = gate_raw.astype(jnp.float32)
        gate_act = jax.nn.silu(gate_in)
        mixed_f = mixed_tok.astype(jnp.float32)
        v = mixed_f * gate_act
        inv_rms2 = lax.rsqrt(jnp.mean(v * v, axis=-1, keepdims=True) + EPSILON)
        normed2 = v * inv_rms2
        g_gate = jnp.sum(d_normed * normed2, axis=0)
        d_scaled = d_normed * gain_gate[None, :]
        d_v = inv_rms2 * (d_scaled - normed2 * jnp.mean(d_scaled * normed2, axis=-1, keepdims=True))
        d_mixed = (d_v * gate_act).astype(jnp.bfloat16)
        d_gate = d_v * mixed_f * silu_slope(gate_in)
        d_heads = lax.all_to_all(d_mixed, "seq", split_axis=1, concat_axis=0, tiled=True)
        _, pull = jax.vjp(
            mixer,
            x_heads.astype(jnp.float32),
            bc_whole.astype(jnp.float32),
            dt_heads.astype(jnp.float32),
            *head_params
        )
        grads = pull(d_heads.astype(jnp.float32))
        d_x_tok = lax.all_to_all(
            grads[0].astype(jnp.bfloat16), "seq", split_axis=0, concat_axis=1, tiled=True
        )
        d_dt_tok = lax.all_to_all(
            grads[2].astype(jnp.bfloat16), "seq", split_axis=0, concat_axis=1, tiled=True
        )
        d_bc_tok = lax.psum_scatter(
            grads[1].astype(jnp.bfloat16), "seq", scatter_dimension=0, tiled=True
        ).astype(jnp.float32)
        d_proj = jnp.concatenate(
            [d_gate, d_x_tok.astype(jnp.float32), d_bc_tok, d_dt_tok.astype(jnp.float32)], axis=1
        ).astype(jnp.bfloat16)
        d_in = lax.dot_general(
            d_proj, in_weight_b, (((1,), (1,)), ((), ())), preferred_element_type=jnp.float32
        )
        inv_rms = lax.rsqrt(
            jnp.mean(backward_h_in * backward_h_in, axis=-1, keepdims=True) + EPSILON
        )
        normed_h = backward_h_in * inv_rms
        g_norm = jnp.sum(d_in * normed_h, axis=0)
        d_scaled_in = d_in * gain_in[None, :]
        d_h = out_grad + inv_rms * (
            d_scaled_in - normed_h * jnp.mean(d_scaled_in * normed_h, axis=-1, keepdims=True)
        )
        row_pieces = (normed_in, d_proj, normed_out, out_grad_b)
        d_h, row_pieces, grads = (
            d_h,
            row_pieces,
            (g_norm, g_gate, grads[3], grads[4], grads[5], grads[6], grads[7], grads[8], grads[9]),
        )
        d_list.append(d_h)
        if step_index < micro_count:
            received = passed_along(d_h.astype(jnp.bfloat16), "section", -1).astype(d_h.dtype)
        piece_list.append(row_pieces)
        acc_norm = acc_norm + grads[0]
        acc_gate = acc_gate + grads[1]
        conv_step = jnp.concatenate(
            [
                lax.dynamic_update_slice_in_dim(
                    jnp.zeros((KERNEL, INNER), jnp.float32), grads[2], chan_start, 1
                ),
                grads[4],
            ],
            axis=1,
        )
        bias_step = jnp.concatenate(
            [
                lax.dynamic_update_slice_in_dim(
                    jnp.zeros((INNER,), jnp.float32), grads[3], chan_start, 0
                ),
                grads[5],
            ],
            axis=0,
        )
        acc_conv_w = acc_conv_w + conv_step
        acc_conv_b = acc_conv_b + bias_step
        acc_dt_bias = acc_dt_bias + lax.dynamic_update_slice_in_dim(
            jnp.zeros((HEADS,), jnp.float32), grads[6], head_start, 0
        )
        acc_a_log = acc_a_log + lax.dynamic_update_slice_in_dim(
            jnp.zeros((HEADS,), jnp.float32), grads[7], head_start, 0
        )
        acc_skip = acc_skip + lax.dynamic_update_slice_in_dim(
            jnp.zeros((HEADS,), jnp.float32), grads[8], head_start, 0
        )
    all_normed_in = jnp.concatenate([p[0] for p in piece_list], axis=0)
    all_d_proj = jnp.concatenate([p[1] for p in piece_list], axis=0)
    all_normed_out = jnp.concatenate([p[2] for p in piece_list], axis=0)
    all_out_grad = jnp.concatenate([p[3] for p in piece_list], axis=0)
    whole_in = outer_rows(all_normed_in, all_d_proj)
    whole_out = outer_rows(all_normed_out, all_out_grad)
    acc_in, acc_out = (
        lax.psum_scatter(
            whole_in.astype(jnp.bfloat16), "wt", scatter_dimension=0, tiled=True
        ).astype(jnp.float32),
        lax.psum_scatter(
            whole_out.astype(jnp.bfloat16), "wt", scatter_dimension=0, tiled=True
        ).astype(jnp.float32),
    )
    acc_in, acc_out = (
        lax.psum(acc_in.astype(jnp.bfloat16), "seq").astype(jnp.float32),
        lax.psum(acc_out.astype(jnp.bfloat16), "seq").astype(jnp.float32),
    )
    summed = lax.psum(
        (acc_norm, acc_conv_w, acc_conv_b, acc_dt_bias, acc_a_log, acc_skip, acc_gate),
        ("seq", "wt"),
    )
    section_out = jnp.stack(
        [jnp.where(first_section, outs_list[m], outs_list[m + 1]) for m in range(micro_count)]
    )[None, :, None]
    input_grad = jnp.stack(
        [jnp.where(first_section, d_list[m + 1], d_list[m]) for m in range(micro_count)]
    )[None, :, None]
    return (
        section_out,
        input_grad,
        summed[0][None],
        acc_in[None],
        summed[1][None],
        summed[2][None],
        summed[3][None],
        summed[4][None],
        summed[5][None],
        summed[6][None],
        acc_out[None],
    )


def solution(mesh):
    placed = (
        P(None, "wt", "seq", None),
        P(None, "wt", "seq", None),
        P("section", None),
        P("section", "wt", None),
        P("section", None, None),
        P("section", None),
        P("section", None),
        P("section", None),
        P("section", None),
        P("section", None),
        P("section", "wt", None),
    )
    return jax.shard_map(
        local,
        mesh=mesh,
        in_specs=placed,
        out_specs=(
            P("section", None, "wt", "seq", None),
            P("section", None, "wt", "seq", None),
            P("section", None),
            P("section", "wt", None),
            P("section", None, None),
            P("section", None),
            P("section", None),
            P("section", None),
            P("section", None),
            P("section", None),
            P("section", "wt", None),
        ),
        check_vma=False,
    )
```

profile of v0, /device:TPU:8, one launch (start us, length us, event | category | flops | bytes accessed | tf_op | source)
XLA Modules:
  0.0 2117.3 jit_solution(2018476657929949981)
XLA Ops:
  13.6 332.6 %all-gather.3.cloned.1.call-done = bf16[1,1536,6448]{1,2,0:T(8,128)(2,1)} async-done(((bf16[1,384,6448]{1,2,0:T(8,128)(2,1)}), bf16[1,1536,6448]{1,2,0:T(8,128)(2,1)}) %all-gather.3.cloned.1.call-update) | async-done | bytes 19808272 | tf_op jit(solution)/shard_map/all_gather | solution.py:113
  346.2 9.7 fusion.42
  425.1 12.1 all_to_all.243
  439.5 73.3 %all-gather.5.cloned.1.call-done = bf16[1,3072,1536]{2,1,0:T(8,128)(2,1)} async-done(((bf16[1,768,1536]{2,1,0:T(8,128)(2,1)}), bf16[1,3072,1536]{2,1,0:T(8,128)(2,1)}) %all-gather.5.cloned.1.call-update) | async-done | bytes 9437200 | tf_op jit(solution)/shard_map/all_gather | solution.py:114
  609.7 13.4 all_to_all.244
  645.2 9.7 fusion.48
  799.1 11.2 while.151
  883.7 23.7 %reduce-scatter.16.cloned.1.call-done = bf16[128,256]{1,0:T(8,128)(2,1)} async-done(((bf16[512,256]{1,0:T(8,128)(2,1)}), bf16[128,256]{1,0:T(8,128)(2,1)}) %reduce-scatter.16.cloned.1.call-update) | async-done | bytes 65552
  908.8 10.6 multiply_reduce_fusion.32
  926.2 10.4 multiply_reduce_fusion.4
  946.2 10.7 all-to-all-done.12
  984.8 12.6 while.153
  1070.8 24.0 %reduce-scatter.18.cloned.1.call-done = bf16[128,256]{1,0:T(8,128)(2,1)} async-done(((bf16[512,256]{1,0:T(8,128)(2,1)}), bf16[128,256]{1,0:T(8,128)(2,1)}) %reduce-scatter.18.cloned.1.call-update) | async-done | bytes 65552
  1096.2 10.6 multiply_reduce_fusion.31
  1131.9 10.6 all-to-all-done.15
  1170.5 13.2 while.155
  1256.0 24.9 %reduce-scatter.20.cloned.1.call-done = bf16[128,256]{1,0:T(8,128)(2,1)} async-done(((bf16[512,256]{1,0:T(8,128)(2,1)}), bf16[128,256]{1,0:T(8,128)(2,1)}) %reduce-scatter.20.cloned.1.call-update) | async-done | bytes 65552
  1282.9 20.3 convolution_convert_fusion
  1303.2 24.5 %copy.1225 = bf16[1536,6448]{1,0:T(8,128)(2,1)} copy(bf16[1536,6448]{0,1:T(8,128)(2,1)} %convolution_convert_fusion) | data formatting | bytes 39616512
  1341.0 318.7 %reduce-scatter.22.cloned.1.call-done = bf16[384,6448]{1,0:T(8,128)(2,1)} async-done(((bf16[1536,6448]{1,0:T(8,128)(2,1)}), bf16[384,6448]{1,0:T(8,128)(2,1)}) %reduce-scatter.22.cloned.1.call-update) | async-done | bytes 4952080
  1667.2 158.7 %reduce-scatter.14.cloned.1.call-done = bf16[768,1536]{1,0:T(8,128)(2,1)} async-done(((bf16[3072,1536]{1,0:T(8,128)(2,1)}), bf16[768,1536]{1,0:T(8,128)(2,1)}) %reduce-scatter.14.cloned.1.call-update) | async-done | bytes 2359312 | tf_op jit(solution)/shard_map/reduce_scatter | solution.py:301
  1839.7 10.5 multiply_reduce_fusion.30
  1853.5 133.0 %all-reduce.76.cloned.1.call-done = (bf16[1,384,6448]{1,2,0:T(8,128)(2,1)}, bf16[1,768,1536]{2,1,0:T(8,128)(2,1)}) async-done(((bf16[1,384,6448]{1,2,0:T(8,128)(2,1)}, bf16[1,768,1536]{2,1,0:T(8,128)(2,1)}), (bf16[1,384,6448]{1,2,0:T(8,128)(2,1)}, bf16[1,768,1536]{2,1,0:T(8,128)(2,1)})) %all-reduce.76.cloned.1.call-update) | async-done | bytes 7311376 | tf_op jit(solution)/shard_map/psum | solution.py:306
  1996.5 105.3 %all-reduce.74.cloned.1.call-done = (f32[1,1536]{1,0:T(1,128)}, f32[1,4,3328]{2,1,0:T(4,128)}, f32[1,3328]{1,0:T(1,128)}, f32[1,48]{1,0:T(1,128)}, f32[1,48]{1,0...) async-done(((f32[1,1536]{1,0:T(1,128)}, f32[1,4,3328]{2,1,0:T(4,128)}, f32[1,3328]{1,0:T(1,128)}, f32[1,48]{1,0:T(1,128)}, f32[1,48]{1,0:T(1,128)}, ...) | async-done | bytes 85584 | tf_op jit(solution)/shard_map/psum | solution.py:309
  (1522 shorter events, 796.6 us)
Async XLA Ops:
  7.2 339.0 %all-gather.3.cloned.1.call-start = ((), (), s32[]{:S(2)}) async-start(), calls=%async_computation.23 | async-start | bytes 24760320 | tf_op jit(solution)/shard_map/all_gather | solution.py:113
  8.0 504.8 %all-gather.5.cloned.1.call-start = ((), (), s32[]{:S(2)}) async-start(), calls=%async_computation.24 | async-start | bytes 11796480 | tf_op jit(solution)/shard_map/all_gather | solution.py:114
  369.2 10.7 all-to-all-start.1
  379.9 13.3 all-to-all-start
  549.8 10.7 all-to-all-start.4
  560.5 15.0 all-to-all-start.3
  677.2 21.9 %all-to-all-start.6 = ((bf16[128,4,768]{2,0,1:T(8,128)(2,1)}), bf16[128,4,768]{2,0,1:T(8,128)(2,1)}, u32[]{:S(2)}, u32[]{:S(2)}) async-start(bf16[128,4,768]{2,0,1:T(8,128)(2,1)} %copy.982), calls=%async_computation.6 | async-start | bytes 1572864 | tf_op jit(solution)/shard_map/all_to_all | solution.py:130
  733.7 12.9 all-to-all-start.8
  760.9 11.8 all-to-all-start.9
  848.1 25.6 %all-to-all-start.11 = ((bf16[4,128,12]{1,2,0:T(8,128)(2,1)}), bf16[4,128,12]{1,2,0:T(8,128)(2,1)S(1)}, u32[]{:S(2)}, u32[]{:S(2)}) async-start(bf16[4,128,12]{1,2,0:T(8,128)(2,1)} %copy.1048), calls=%async_computation.11 | async-start | bytes 32768 | tf_op jit(solution)/shard_map/all_to_all | solution.py:229
  873.8 34.6 %all-to-all-start.10 = ((bf16[4,128,768]{2,1,0:T(8,128)(2,1)}), bf16[4,128,768]{2,1,0:T(8,128)(2,1)S(1)}, u32[]{:S(2)}, u32[]{:S(2)}) async-start(bf16[4,128,768]{2,1,0:T(8,128)(2,1)} %bitcast.87), calls=%async_computation.10 | async-start | bytes 1572864 | tf_op jit(solution)/shard_map/all_to_all | solution.py:226
  878.0 29.3 %reduce-scatter.16.cloned.1.call-start = ((), (), s32[]{:S(2)}) async-start(), calls=%async_computation.26 | async-start | bytes 327680
  941.7 15.2 all-to-all-start.12
  1035.4 25.5 %all-to-all-start.14 = ((bf16[4,128,12]{1,2,0:T(8,128)(2,1)}), bf16[4,128,12]{1,2,0:T(8,128)(2,1)S(1)}, u32[]{:S(2)}, u32[]{:S(2)}) async-start(bf16[4,128,12]{1,2,0:T(8,128)(2,1)} %copy.1093), calls=%async_computation.14 | async-start | bytes 32768 | tf_op jit(solution)/shard_map/all_to_all | solution.py:229
  1060.9 34.9 %all-to-all-start.13 = ((bf16[4,128,768]{2,1,0:T(8,128)(2,1)}), bf16[4,128,768]{2,1,0:T(8,128)(2,1)S(1)}, u32[]{:S(2)}, u32[]{:S(2)}) async-start(bf16[4,128,768]{2,1,0:T(8,128)(2,1)} %bitcast.123), calls=%async_computation.13 | async-start | bytes 1572864 | tf_op jit(solution)/shard_map/all_to_all | solution.py:226
  1065.2 29.6 %reduce-scatter.18.cloned.1.call-start = ((), (), s32[]{:S(2)}) async-start(), calls=%async_computation.27 | async-start | bytes 327680
  1127.5 15.0 all-to-all-start.15
  1221.7 25.5 %all-to-all-start.17 = ((bf16[4,128,12]{1,2,0:T(8,128)(2,1)}), bf16[4,128,12]{1,2,0:T(8,128)(2,1)S(1)}, u32[]{:S(2)}, u32[]{:S(2)}) async-start(bf16[4,128,12]{1,2,0:T(8,128)(2,1)} %copy.1138), calls=%async_computation.17 | async-start | bytes 32768 | tf_op jit(solution)/shard_map/all_to_all | solution.py:229
  1247.2 35.2 %all-to-all-start.16 = ((bf16[4,128,768]{2,1,0:T(8,128)(2,1)}), bf16[4,128,768]{2,1,0:T(8,128)(2,1)S(1)}, u32[]{:S(2)}, u32[]{:S(2)}) async-start(bf16[4,128,768]{2,1,0:T(8,128)(2,1)} %bitcast.159), calls=%async_computation.16 | async-start | bytes 1572864 | tf_op jit(solution)/shard_map/all_to_all | solution.py:226
  1251.5 29.4 %reduce-scatter.20.cloned.1.call-start = ((), (), s32[]{:S(2)}) async-start(), calls=%async_computation.28 | async-start | bytes 327680
  1254.5 405.2 %reduce-scatter.22.cloned.1.call-start = ((), (), s32[]{:S(2)}) async-start(), calls=%async_computation.29 | async-start | bytes 25067520
  1327.7 498.2 %reduce-scatter.14.cloned.1.call-start = ((), (), s32[]{:S(2)}) async-start(), calls=%async_computation.25 | async-start | bytes 11796480 | tf_op jit(solution)/shard_map/reduce_scatter | solution.py:301
  1340.9 645.7 %all-reduce.76.cloned.1.call-start = ((), (), s32[]{:S(2)}) async-start(), calls=%async_computation.31 | async-start | bytes 14622720 | tf_op jit(solution)/shard_map/psum | solution.py:306
  1826.0 275.7 %all-reduce.74.cloned.1.call-start = ((), (), s32[]{:S(2)}) async-start(), calls=%async_computation.30 | async-start | bytes 173056 | tf_op jit(solution)/shard_map/psum | solution.py:309
  (417 other events, 10630.9 us)
Sparse Core Ops, SparseCore 0:
  9.6 336.5 all-gather.2
  347.8 164.9 all-gather.4
  881.6 25.7 reduce-scatter.15
  1069.2 25.5 reduce-scatter.17
  1255.4 25.4 reduce-scatter.19
  1327.8 331.7 reduce-scatter.21
  1662.7 163.1 reduce-scatter.13
  1829.8 156.6 all-reduce.75
  1995.3 106.4 all-reduce.73
where the time goes:
time: 2130 us; the launch traced here: 2120 us
  waiting for transfers between devices  1240 us (58%)
  matrix products  303 us (14%)
  local copies, waits for them, and re-layouts  256 us (12%)
  other arithmetic  174 us (8%)
  starting transfers between devices  70.7 us (3%)
  blocking collectives  52.6 us (2%)
    unnamed x13, waiting for transfers between devices  393 us
    all_gather x1, waiting for transfers between devices, local(): lax.all_gather(w_in, 'wt', axis=1, tiled=True)  333 us
    reduce_scatter x1, waiting for transfers between devices, local(): lax.psum_scatter(whole_out.astype(jnp.bfloat16), 'wt', scatter_dimension=...  159 us
    psum x1, waiting for transfers between devices, local(): lax.psum(acc_in.astype(jnp.bfloat16), 'seq').astype(jnp.float32)  133 us
    psum x1, waiting for transfers between devices, local(): lax.psum((acc_norm, acc_conv_w, acc_conv_b, acc_dt_bias, acc_a_log, acc_s...  105 us
    all_gather x1, waiting for transfers between devices, local(): lax.all_gather(w_out, 'wt', axis=1, tiled=True)  73.3 us
    unnamed x772, local copies, waits for them, and re-layouts  62.4 us
    dot_general x9, matrix products, mixer(): jnp.einsum('ctsh,cshp->cthp', mix_weight, x_blocks, precision=EXACT_DOT)  60.4 us
  transfers between devices with their start and end apart: 29, of which 18 were waited for; matrix products, arithmetic and copies ran while one was open for 12% of the time, Pallas kernels for 0%

commit v1 on v0

v1 whole, which is shorter than its diff:
```python
import functools

import jax
import jax.numpy as jnp
from jax import lax
from jax.experimental import pallas as pl
from jax.experimental.pallas import tpu as pltpu
from jax.sharding import PartitionSpec as P

D = 1536
HEADS = 48
HEAD_DIM = 64
STATE = 128
KERNEL = 4
INNER = 3072
CONV = 3328
EPSILON = 1e-05

Q = 128
F32 = jnp.float32
BF = jnp.bfloat16
VMEM_LIMIT = 48 * 2**20


def dot(a, b, ca, cb, precision=None):
    return lax.dot_general(a, b, (((ca,), (cb,)), ((), ())), precision=precision, preferred_element_type=F32)

def sigmoid(x):
    return 1.0 / (1.0 + jnp.exp(-x))

def softplus(x):
    return jnp.maximum(x, 0.0) + jnp.log1p(jnp.exp(-jnp.abs(x)))

def lane_mask(rows):
    return lax.broadcasted_iota(jnp.int32, (rows, 128), 1) < HEAD_DIM

def spread(cols, pair, mask):
    a = jnp.broadcast_to(cols[:, 2 * pair : 2 * pair + 1], mask.shape)
    b = jnp.broadcast_to(cols[:, 2 * pair + 1 : 2 * pair + 2], mask.shape)
    return jnp.where(mask, a, b)

def split_pair(u, mask):
    zero = jnp.zeros_like(u)
    return jnp.concatenate([jnp.where(mask, u, zero), jnp.where(mask, zero, u)], axis=0)

def conv_tile(proj_ref, cw_ref, pad, proj_at, conv_at, rows):
    pad[0:8, :] = jnp.zeros((8, 128), F32)
    pad[8 : 8 + rows, :] = proj_ref[:, pl.ds(proj_at, 128)].astype(F32)
    pre = jnp.broadcast_to(cw_ref[4:5, pl.ds(conv_at, 128)], (rows, 128))
    for k in range(KERNEL):
        pre = pre + cw_ref[k : k + 1, pl.ds(conv_at, 128)] * pad[5 + k : 5 + k + rows, :]
    return pre

def steps(proj_ref, hp_ref, dt_at):
    raw = proj_ref[:, dt_at : dt_at + 128].astype(F32) + hp_ref[0:1, :]
    return raw, softplus(raw)

def chunk_factors(dt, hp_ref):
    rate = dt * hp_ref[1:2, :]
    rows = lax.broadcasted_iota(jnp.int32, (Q, Q), 0)
    cols = lax.broadcasted_iota(jnp.int32, (Q, Q), 1)
    tri = (rows >= cols).astype(F32)
    cum = dot(tri, rate, 1, 0, lax.Precision.HIGHEST)
    return rate, cum, rows >= cols

def decay_pair(cum, cum_t, causal, pair):
    parts = []
    for h in (2 * pair, 2 * pair + 1):
        diff = jnp.broadcast_to(cum[:, h : h + 1], (Q, Q)) - jnp.broadcast_to(cum_t[h : h + 1, :], (Q, Q))
        parts.append(jnp.exp(jnp.where(causal, diff, -1e30)))
    return jnp.concatenate(parts, axis=1)

def scan_forward(G, proj_ref, cw_ref, hp_ref, gw_ref, vg_ref, ssq_ref, mixed_ref, yp_ref, st_ref, pad, xc, dts, state):
    L = proj_ref.shape[0]
    for tile in range((G + 2 * STATE) // 128):
        pre = conv_tile(proj_ref, cw_ref, pad, G + tile * 128, tile * 128, L)
        xc[:, tile * 128 : tile * 128 + 128] = pre * sigmoid(pre)
    _, dts[...] = steps(proj_ref, hp_ref, 2 * G + 2 * STATE)
    state[...] = jnp.zeros_like(state)
    mask = lane_mask(Q)

    def chunk(c, _):
        at = pl.ds(pl.multiple_of(c * Q, Q), Q)
        dt = dts[at, :]
        rate, cum, causal = chunk_factors(dt, hp_ref)
        cum_t = cum.T
        last = cum[Q - 1 : Q, :]
        e_cum = jnp.exp(cum)
        tail = jnp.exp(last - cum) * dt
        e_last = jnp.broadcast_to(jnp.exp(last), (8, 128))
        b = xc[at, G : G + STATE].astype(BF)
        cc = xc[at, G + STATE : G + 2 * STATE].astype(BF)
        scores = dot(cc, b, 1, 1)
        scores2 = jnp.concatenate([scores, scores], axis=1)
        ssq = jnp.zeros((Q, 1), F32)
        for p in range(G // 128):
            lanes = slice(p * 128, p * 128 + 128)
            x = xc[at, lanes]
            u = (x * spread(dt, p, mask)).astype(BF)
            m = (scores2 * decay_pair(cum, cum_t, causal, p)).astype(BF)
            before = state[:, lanes]
            st_ref[c, :, lanes] = before
            y = dot(m, split_pair(u, mask), 1, 0)
            y = y + dot(cc, before.astype(BF), 1, 0) * spread(e_cum, p, mask)
            yp_ref[at, lanes] = y
            after = dot(b, (x * spread(tail, p, mask)).astype(BF), 0, 0)
            state[:, lanes] = before * spread(e_last, p, mask[0:8])[0:1, :] + after
            mixed = (y + gw_ref[1:2, lanes] * x).astype(BF)
            mixed_ref[at, lanes] = mixed
            gate = proj_ref[at, lanes].astype(F32)
            v = mixed.astype(F32) * (gate * sigmoid(gate))
            vg_ref[at, lanes] = (v * gw_ref[0:1, lanes]).astype(BF)
            ssq = ssq + jnp.sum(v * v, axis=1, keepdims=True)
        ssq_ref[c] = jnp.broadcast_to(ssq, (Q, 128)).T[0:8, :]
        return 0

    lax.fori_loop(0, L // Q, chunk, 0)

def scan_fwd_call(proj, cw, hp, gw):
    L, _ = proj.shape
    G = gw.shape[1]
    nb = L // Q
    vm = pl.BlockSpec(memory_space=pltpu.VMEM)
    return pl.pallas_call(
        functools.partial(scan_forward, G),
        out_shape=(
            jax.ShapeDtypeStruct((L, G), BF),
            jax.ShapeDtypeStruct((nb, 8, 128), F32),
            jax.ShapeDtypeStruct((L, G), BF),
            jax.ShapeDtypeStruct((L, G), F32),
            jax.ShapeDtypeStruct((nb, STATE, G), F32),
        ),
        in_specs=[vm] * 4,
        out_specs=[vm] * 5,
        scratch_shapes=[
            pltpu.VMEM((8 + L, 128), F32),
            pltpu.VMEM((L, G + 2 * STATE), F32),
            pltpu.VMEM((L, 128), F32),
            pltpu.VMEM((STATE, G), F32),
        ],
        compiler_params=pltpu.CompilerParams(vmem_limit_bytes=VMEM_LIMIT),
        cost_estimate=pl.CostEstimate(flops=L * G * 1500, bytes_accessed=L * G * 20, transcendentals=L * G * 4),
        name="scan_forward",
    )(proj, cw, hp, gw)

def scan_backward(G, proj_ref, mixed_ref, yp_ref, st_ref, dn_ref, sc_ref, cw_ref, hp_ref, gw_ref,
                  dproj_ref, no_ref, gg_ref, gc_ref, gh_ref,
                  pad, xc, dts, dy, dxc, dstate, ddt):
    L = proj_ref.shape[0]
    nb = L // Q
    mask = lane_mask(Q)
    for tile in range((G + 2 * STATE) // 128):
        pre = conv_tile(proj_ref, cw_ref, pad, G + tile * 128, tile * 128, L)
        xc[:, tile * 128 : tile * 128 + 128] = pre * sigmoid(pre)
    raw, dts[...] = steps(proj_ref, hp_ref, 2 * G + 2 * STATE)
    dstate[...] = jnp.zeros_like(dstate)
    gg_ref[...] = jnp.zeros_like(gg_ref)
    gh_ref[...] = jnp.zeros_like(gh_ref)

    def chunk(step, _):
        c = nb - 1 - step
        at = pl.ds(pl.multiple_of(c * Q, Q), Q)
        sc = jnp.concatenate([sc_ref[c], jnp.zeros((Q - 8, 128), F32)], axis=0).T
        inv2 = jnp.broadcast_to(sc[:, 0:1], (Q, 128))
        mdot = jnp.broadcast_to(sc[:, 1:2], (Q, 128))
        dt = dts[at, :]
        rate, cum, causal = chunk_factors(dt, hp_ref)
        cum_t = cum.T
        last = cum[Q - 1 : Q, :]
        e_cum = jnp.exp(cum)
        tail = jnp.exp(last - cum)
        e_last = jnp.broadcast_to(jnp.exp(last), (8, 128))
        b = xc[at, G : G + STATE].astype(BF)
        cc = xc[at, G + STATE : G + 2 * STATE].astype(BF)
        scores = dot(cc, b, 1, 1)
        scores2 = jnp.concatenate([scores, scores], axis=1)
        d_scores = jnp.zeros((Q, Q), F32)
        d_b = jnp.zeros((Q, STATE), F32)
        d_c = jnp.zeros((Q, STATE), F32)
        d_cum = jnp.zeros((Q, 128), F32)
        d_dt = jnp.zeros((Q, 128), F32)
        d_last = jnp.zeros((8, 128), F32)
        lane_ids = lax.broadcasted_iota(jnp.int32, (Q, 128), 1)
        for p in range(G // 128):
            lanes = slice(p * 128, p * 128 + 128)
            gate = proj_ref[at, lanes].astype(F32)
            sig = sigmoid(gate)
            act = gate * sig
            mixed = mixed_ref[at, lanes].astype(F32)
            n2 = mixed * act * inv2
            no_ref[at, lanes] = (n2 * gw_ref[0:1, lanes]).astype(BF)
            dn = dn_ref[at, lanes]
            gg_ref[0:1, lanes] += jnp.sum(dn * n2, axis=0, keepdims=True)
            d_v = inv2 * (dn * gw_ref[0:1, lanes] - n2 * mdot)
            dyb = (d_v * act).astype(BF)
            dproj_ref[at, lanes] = (d_v * mixed * (sig * (1.0 + gate * (1.0 - sig)))).astype(BF)
            d_y = dyb.astype(F32)
            x = xc[at, lanes]
            dt_x = spread(dt, p, mask)
            u = (x * dt_x).astype(BF)
            u2 = split_pair(u, mask)
            uf = u.astype(F32)
            dec = decay_pair(cum, cum_t, causal, p)
            m = (scores2 * dec).astype(BF)
            dm = dot(dyb, u2, 1, 1) * dec
            d_scores = d_scores + dm[:, :Q] + dm[:, Q:]
            both = dot(m, dyb, 0, 0)
            du = jnp.where(mask, both[:Q], both[Q:])
            tail_x = spread(tail, p, mask)
            before = st_ref[c, :, lanes]
            after = dstate[:, lanes]
            afterb = after.astype(BF)
            du_out = tail_x * dot(b, afterb, 1, 0)
            du = du + du_out
            dye = (d_y * spread(e_cum, p, mask)).astype(BF)
            d_c = d_c + dot(dye, before.astype(BF), 1, 1)
            d_b = d_b + dot((uf * tail_x).astype(BF), afterb, 1, 1)
            e_last_x = spread(e_last, p, mask[0:8])
            dstate[:, lanes] = after * e_last_x[0:1, :] + dot(cc, dye, 0, 0)
            z3 = jnp.sum(uf * du_out, axis=0, keepdims=True) + e_last_x[0:1, :] * jnp.sum(before * after, axis=0, keepdims=True)
            z1 = d_y * yp_ref[at, lanes] - uf * du
            z2 = x * du
            zero = jnp.zeros_like(z1)
            for half, h in ((True, 2 * p), (False, 2 * p + 1)):
                keep = mask if half else jnp.logical_not(mask)
                here = lane_ids == h
                d_cum = jnp.where(here, jnp.sum(jnp.where(keep, z1, zero), axis=1, keepdims=True), d_cum)
                d_dt = jnp.where(here, jnp.sum(jnp.where(keep, z2, zero), axis=1, keepdims=True), d_dt)
                s3 = jnp.sum(jnp.where(keep[0:8], jnp.broadcast_to(z3, (8, 128)), 0.0), axis=1, keepdims=True)
                d_last = jnp.where(here[0:8], s3, d_last)
            dxc[at, lanes] = dt_x * du + gw_ref[1:2, lanes] * d_y
            gg_ref[1:2, lanes] += jnp.sum(d_y * x, axis=0, keepdims=True)
        dsb = d_scores.astype(BF)
        dxc[at, G : G + STATE] = d_b + dot(dsb, cc, 0, 0)
        dxc[at, G + STATE : G + 2 * STATE] = d_c + dot(dsb, b, 1, 0)
        rows = lax.broadcasted_iota(jnp.int32, (Q, Q), 0)
        cols = lax.broadcasted_iota(jnp.int32, (Q, Q), 1)
        upper = (rows <= cols).astype(F32)
        d_rate = dot(upper, d_cum, 1, 0, lax.Precision.HIGHEST) + d_last[0:1, :]
        d_step = d_dt + d_rate * hp_ref[1:2, :]
        raw_c = proj_ref[at, 2 * G + 2 * STATE : 2 * G + 2 * STATE + 128].astype(F32) + hp_ref[0:1, :]
        d_raw = d_step * sigmoid(raw_c)
        dproj_ref[at, 2 * G + 2 * STATE : 2 * G + 2 * STATE + 128] = d_raw.astype(BF)
        gh_ref[0:1, :] += jnp.sum(d_raw, axis=0, keepdims=True)
        gh_ref[1:2, :] += jnp.sum(d_rate * rate, axis=0, keepdims=True)
        return 0

    lax.fori_loop(0, nb, chunk, 0)

    gc_ref[...] = jnp.zeros_like(gc_ref)
    for tile in range((G + 2 * STATE) // 128):
        lanes = slice(tile * 128, tile * 128 + 128)
        pre = conv_tile(proj_ref, cw_ref, pad, G + tile * 128, tile * 128, L)
        sig = sigmoid(pre)
        d_pre = dxc[:, lanes] * (sig * (1.0 + pre * (1.0 - sig)))
        for k in range(KERNEL):
            gc_ref[k : k + 1, lanes] = jnp.sum(d_pre * pad[5 + k : 5 + k + L, :], axis=0, keepdims=True)
        gc_ref[4:5, lanes] = jnp.sum(d_pre, axis=0, keepdims=True)
        pad[0:L, :] = d_pre
        pad[L : L + 8, :] = jnp.zeros((8, 128), F32)
        d_in = cw_ref[3:4, lanes] * d_pre
        for k in range(KERNEL - 1):
            d_in = d_in + cw_ref[k : k + 1, lanes] * pad[3 - k : 3 - k + L, :]
        dproj_ref[:, G + tile * 128 : G + tile * 128 + 128] = d_in.astype(BF)

def scan_bwd_call(proj, mixed, yp, st, dn, sc, cw, hp, gw):
    L, NC = proj.shape
    G = gw.shape[1]
    vm = pl.BlockSpec(memory_space=pltpu.VMEM)
    CX = G + 2 * STATE
    return pl.pallas_call(
        functools.partial(scan_backward, G),
        out_shape=(
            jax.ShapeDtypeStruct((L, NC), BF),
            jax.ShapeDtypeStruct((L, G), BF),
            jax.ShapeDtypeStruct((8, G), F32),
            jax.ShapeDtypeStruct((8, CX), F32),
            jax.ShapeDtypeStruct((8, 128), F32),
        ),
        in_specs=[vm] * 9,
        out_specs=[vm] * 5,
        scratch_shapes=[
            pltpu.VMEM((8 + L, 128), F32),
            pltpu.VMEM((L, CX), F32),
            pltpu.VMEM((L, 128), F32),
            pltpu.VMEM((8, 128), F32),
            pltpu.VMEM((L, CX), F32),
            pltpu.VMEM((STATE, G), F32),
            pltpu.VMEM((8, 128), F32),
        ],
        compiler_params=pltpu.CompilerParams(vmem_limit_bytes=VMEM_LIMIT),
        cost_estimate=pl.CostEstimate(flops=L * G * 4000, bytes_accessed=L * G * 30, transcendentals=L * G * 6),
        name="scan_backward",
    )(proj, mixed, yp, st, dn, sc, cw, hp, gw)


MESH = pl.DeviceIdType.MESH
VM = pl.BlockSpec(memory_space=pltpu.VMEM)
ANY = pl.BlockSpec(memory_space=pl.ANY)
TILE = 16


def meet(axis, n):
    me = lax.axis_index(axis)
    barrier = pltpu.get_barrier_semaphore()
    for k in range(1, n):
        pl.semaphore_signal(
            barrier, inc=1, device_id={axis: lax.rem(me + k, n)}, device_id_type=MESH
        )
    pl.semaphore_wait(barrier, n - 1)


def send(src, dst, sems, at, axis, peer):
    copy = pltpu.make_async_remote_copy(
        src, dst, sems[0].at[at], sems[1].at[at], device_id={axis: peer}, device_id_type=MESH
    )
    copy.start()
    return copy


def column(row):
    return jnp.broadcast_to(row, (128, 128)).T


def sum_parts(n, part_ref, stat_ref, got, got_stat, sems, stat_sems):
    me = lax.axis_index("seq")
    copies = []
    for k in range(1, n):
        peer = lax.rem(me + k, n)
        copies.append(send(part_ref.at[peer], got.at[k - 1], sems, k - 1, "seq", peer))
        if stat_ref is not None:
            copies.append(
                send(stat_ref.at[peer], got_stat.at[k - 1], stat_sems, k - 1, "seq", peer)
            )
    return copies


def gather_rows(n, own, all_ref, own_stat, stat_ref, sems, stat_sems):
    me = lax.axis_index("seq")
    copies = []
    for k in range(1, n):
        peer = lax.rem(me + k, n)
        copies.append(send(own, all_ref.at[me], sems, k - 1, "seq", peer))
        if stat_ref is not None:
            copies.append(send(own_stat, stat_ref.at[me], stat_sems, k - 1, "seq", peer))
    return copies


def rows_loop(rows, body):
    def step(r, carry):
        body(pl.ds(pl.multiple_of(r * TILE, TILE), TILE))
        return carry

    lax.fori_loop(0, rows // TILE, step, 0)


def total_of(n, part_ref, got, at):
    total = part_ref[lax.axis_index("seq"), at, :].astype(F32)
    for k in range(n - 1):
        total = total + got[k, at, :].astype(F32)
    return total


def start_kernel(n, h_ref, gain_ref, all_ref, own, s0, r0):
    rows = h_ref.shape[0]

    def norm(at):
        h = h_ref[at, :]
        inv = lax.rsqrt(jnp.mean(h * h, axis=1, keepdims=True) + EPSILON)
        own[at, :] = (h * inv * gain_ref[0:1, :]).astype(BF)

    rows_loop(rows, norm)
    meet("seq", n)
    copies = gather_rows(n, own, all_ref, None, None, (s0, r0), None)
    all_ref[lax.axis_index("seq")] = own[...]
    for copy in copies:
        copy.wait()


def start_call(h, gain, n):
    rows = h.shape[0]
    return pl.pallas_call(
        functools.partial(start_kernel, n),
        out_shape=jax.ShapeDtypeStruct((n, rows, D), BF),
        in_specs=[VM, VM],
        out_specs=VM,
        scratch_shapes=[
            pltpu.VMEM((rows, D), BF),
            pltpu.SemaphoreType.DMA((n - 1,)),
            pltpu.SemaphoreType.DMA((n - 1,)),
        ],
        compiler_params=pltpu.CompilerParams(
            collective_id=0, has_side_effects=True, vmem_limit_bytes=VMEM_LIMIT
        ),
        name="start",
    )(h, gain)


def forward_turn_kernel(
    n, last, part_ref, ssq_ref, h_ref, next_ref, hout_ref, pout_ref, all_ref, stat_ref,
    got, got_stat, own, own_stat, cols, mdots, s0, r0, s1, r1, s2, r2, s3, r3
):
    me = lax.axis_index("seq")
    rows = h_ref.shape[0]
    meet("seq", n)
    copies = sum_parts(n, part_ref, ssq_ref, got, got_stat, (s0, r0), (s1, r1))
    for copy in copies:
        copy.wait()
    ssq = ssq_ref[me]
    for k in range(n - 1):
        ssq = ssq + got_stat[k]
    inv2 = lax.rsqrt(ssq * (1.0 / INNER) + EPSILON)
    own_stat[...] = inv2
    cols[...] = column(inv2[0:1, :])

    def finish(at):
        pout = total_of(n, part_ref, got, at) * cols[at, 0:1]
        h = h_ref[at, :] + pout
        hout_ref[at, :] = h
        pout_ref[at, :] = pout
        if last:
            out = next_ref[at, :].astype(BF)
            dots = jnp.sum(out.astype(F32) * pout, axis=1, keepdims=True)
            mdots[at, :] = jnp.broadcast_to(dots * (1.0 / INNER), (TILE, 128))
            own[at, :] = out
        else:
            inv = lax.rsqrt(jnp.mean(h * h, axis=1, keepdims=True) + EPSILON)
            own[at, :] = (h * inv * next_ref[0:1, :]).astype(BF)

    rows_loop(rows, finish)
    if last:
        own_stat[1:2, :] = mdots[...].T[0:1, :]
    copies = gather_rows(n, own, all_ref, own_stat, stat_ref, (s2, r2), (s3, r3))
    all_ref[me] = own[...]
    stat_ref[me] = own_stat[...]
    for copy in copies:
        copy.wait()


def forward_turn(part, ssq, h, following, n, last):
    rows = h.shape[0]
    sems = [pltpu.SemaphoreType.DMA((n - 1,))] * 8
    return pl.pallas_call(
        functools.partial(forward_turn_kernel, n, last),
        out_shape=(
            jax.ShapeDtypeStruct((rows, D), F32),
            jax.ShapeDtypeStruct((rows, D), F32),
            jax.ShapeDtypeStruct((n, rows, D), BF),
            jax.ShapeDtypeStruct((n, 8, 128), F32),
        ),
        in_specs=[VM] * 4,
        out_specs=[VM] * 4,
        scratch_shapes=[
            pltpu.VMEM((n - 1, rows, D), BF),
            pltpu.VMEM((n - 1, 8, 128), F32),
            pltpu.VMEM((rows, D), BF),
            pltpu.VMEM((8, 128), F32),
            pltpu.VMEM((rows, 128), F32),
            pltpu.VMEM((rows, 128), F32),
        ]
        + sems,
        compiler_params=pltpu.CompilerParams(
            collective_id=2 if last else 1, has_side_effects=True, vmem_limit_bytes=VMEM_LIMIT
        ),
        name="forward_end" if last else "forward_turn",
    )(part, ssq, h, following)


def backward_turn_kernel(n, last, *refs):
    if last:
        part_ref, h_ref, og_ref, gain_ref, dh_ref, gn_ref, got, s0, r0 = refs
    else:
        (part_ref, h_ref, og_ref, gain_ref, pout_ref, low_ref, dh_ref, gn_ref, all_ref, stat_ref,
         got, own, own_stat, mdots, s0, r0, s2, r2, s3, r3) = refs
    me = lax.axis_index("seq")
    rows = h_ref.shape[0]
    meet("seq", n)
    for copy in sum_parts(n, part_ref, None, got, None, (s0, r0), None):
        copy.wait()
    gn_ref[...] = jnp.zeros_like(gn_ref)

    def finish(at):
        d_in = total_of(n, part_ref, got, at)
        h = h_ref[at, :]
        inv = lax.rsqrt(jnp.mean(h * h, axis=1, keepdims=True) + EPSILON)
        normed = h * inv
        gn_ref[0:1, :] += jnp.sum(d_in * normed, axis=0, keepdims=True)
        d_s = d_in * gain_ref[0:1, :]
        d_h = og_ref[at, :] + inv * (d_s - normed * jnp.mean(d_s * normed, axis=1, keepdims=True))
        dh_ref[at, :] = d_h
        if not last:
            out = d_h.astype(BF)
            own[at, :] = out
            dots = jnp.sum(out.astype(F32) * pout_ref[at, :], axis=1, keepdims=True)
            mdots[at, :] = jnp.broadcast_to(dots * (1.0 / INNER), (TILE, 128))

    rows_loop(rows, finish)
    if last:
        return
    own_stat[...] = low_ref[...]
    own_stat[1:2, :] = mdots[...].T[0:1, :]
    copies = gather_rows(n, own, all_ref, own_stat, stat_ref, (s2, r2), (s3, r3))
    all_ref[me] = own[...]
    stat_ref[me] = own_stat[...]
    for copy in copies:
        copy.wait()


def backward_turn(part, h, out_grad, gain, below, n):
    rows = h.shape[0]
    last = below is None
    sem = pltpu.SemaphoreType.DMA((n - 1,))
    outs = [jax.ShapeDtypeStruct((rows, D), F32), jax.ShapeDtypeStruct((8, D), F32)]
    scratch = [pltpu.VMEM((n - 1, rows, D), BF)]
    if not last:
        outs += [
            jax.ShapeDtypeStruct((n, rows, D), BF),
            jax.ShapeDtypeStruct((n, 8, 128), F32),
        ]
        scratch += [
            pltpu.VMEM((rows, D), BF),
            pltpu.VMEM((8, 128), F32),
            pltpu.VMEM((rows, 128), F32),
        ]
    args = (part, h, out_grad, gain) + (() if last else below)
    return pl.pallas_call(
        functools.partial(backward_turn_kernel, n, last),
        out_shape=outs,
        in_specs=[VM] * len(args),
        out_specs=[VM] * len(outs),
        scratch_shapes=scratch + [sem] * (2 if last else 6),
        compiler_params=pltpu.CompilerParams(
            collective_id=4 if last else 3, has_side_effects=True, vmem_limit_bytes=VMEM_LIMIT
        ),
        name="backward_end" if last else "backward_turn",
    )(*args)


def swap_kernel(axis, n, scatter, *refs):
    count = (len(refs) - 3) // 2
    sources, targets, (s0, r0, l0) = refs[:count], refs[count : 2 * count], refs[2 * count :]
    me = lax.axis_index(axis)
    meet(axis, n)
    copies = []
    for a in range(count):
        for k in range(1, n):
            peer = lax.rem(me + k, n)
            source = sources[a].at[peer] if scatter else sources[a]
            copies.append(
                send(source, targets[a].at[me], (s0, r0), a * (n - 1) + k - 1, axis, peer)
            )
        mine = sources[a].at[me] if scatter else sources[a]
        local_copy = pltpu.make_async_copy(mine, targets[a].at[me], l0.at[a])
        local_copy.start()
        copies.append(local_copy)
    for copy in copies:
        copy.wait()


def swap(arrays, axis, n, scatter, cid):
    count = len(arrays)
    return pl.pallas_call(
        functools.partial(swap_kernel, axis, n, scatter),
        out_shape=[
            jax.ShapeDtypeStruct(a.shape if scatter else (n,) + a.shape, a.dtype) for a in arrays
        ],
        in_specs=[ANY] * count,
        out_specs=[ANY] * count,
        scratch_shapes=[
            pltpu.SemaphoreType.DMA((count * (n - 1),)),
            pltpu.SemaphoreType.DMA((count * (n - 1),)),
            pltpu.SemaphoreType.DMA((count,)),
        ],
        compiler_params=pltpu.CompilerParams(
            collective_id=cid, has_side_effects=True, vmem_limit_bytes=VMEM_LIMIT
        ),
        name=f"swap_{axis}_{cid}",
    )(*arrays)


def padded(array, size):
    return jnp.pad(array, ((0, 0), (0, size - array.shape[1])))


class Group:
    def __init__(self, n_seq, n_wt):
        self.n_seq, self.n_wt = n_seq, n_wt
        self.heads = HEADS // n_seq
        self.runs = n_wt if HEADS % (n_seq * n_wt) == 0 else 1
        self.run_heads = self.heads // self.runs
        self.chans = self.heads * HEAD_DIM
        self.G = -(-self.chans // 128) * 128
        self.CX = self.G + 2 * STATE
        self.NC = 2 * self.G + 2 * STATE + 128

    def take(self, array, first, width):
        at = lax.axis_index("seq") * self.run_heads * width
        stride = HEADS // self.runs * width
        return [
            lax.dynamic_slice_in_dim(array, first + r * stride + at, self.run_heads * width, 1)
            for r in range(self.runs)
        ]

    def place(self, arrays, width):
        run = self.run_heads * width
        return [
            arrays[g][..., r * run : (r + 1) * run]
            for r in range(self.runs)
            for g in range(self.n_seq)
        ]

    def weight(self, w):
        gate = padded(jnp.concatenate(self.take(w, 0, HEAD_DIM), 1), self.G)
        x = padded(jnp.concatenate(self.take(w, INNER, HEAD_DIM), 1), self.G)
        bc = w[:, 2 * INNER : 2 * INNER + 2 * STATE]
        dt = padded(jnp.concatenate(self.take(w, 2 * INNER + 2 * STATE, 1), 1), 128)
        return jnp.concatenate([gate, x, bc, dt], 1)

    def small(self, norm_gain, conv_w, conv_b, dt_bias, a_log, skip_d, gate_gain):
        conv = jnp.concatenate([conv_w, conv_b[None], jnp.zeros((3, CONV), F32)], 0)
        conv_x = padded(jnp.concatenate(self.take(conv, 0, HEAD_DIM), 1), self.G)
        zero = jnp.zeros((6, HEADS), F32)
        head = jnp.concatenate([dt_bias[None], -jnp.exp(a_log)[None], zero], 0)
        head = padded(jnp.concatenate(self.take(head, 0, 1), 1), 128)
        wide = jnp.concatenate(
            [gate_gain[None], jnp.repeat(skip_d, HEAD_DIM)[None], jnp.zeros((6, INNER), F32)], 0
        )
        wide = padded(jnp.concatenate(self.take(wide, 0, HEAD_DIM), 1), self.G)
        gain = jnp.broadcast_to(norm_gain[None], (8, D))
        return jnp.concatenate([conv_x, conv[:, INNER:], head, wide, gain], 1)

    def parts(self, packed):
        cuts = [0, self.CX, self.CX + 128, self.CX + 128 + self.G, self.CX + 128 + self.G + D]
        return [packed[..., a:b] for a, b in zip(cuts, cuts[1:])]


def local(
    tokens, cotangent, norm_gain, w_in, conv_w, conv_b, dt_bias, a_log, skip_d, gate_gain, w_out
):
    n_seq, n_wt = lax.axis_size("seq"), lax.axis_size("wt")
    core = lax.axis_index("section")
    here = lax.axis_index("seq")
    group = Group(n_seq, n_wt)
    G, rows = group.G, tokens.shape[2]
    length = rows * n_seq

    both = ("section", "wt")
    win = lax.all_gather(group.weight(w_in[0]), both, axis=0, tiled=False)
    win = win.reshape(2, D, group.NC)
    if group.runs == n_wt:
        part = group.chans // n_wt
        piece = lax.dynamic_slice_in_dim(w_out[0], here * part, part, 0)
        wout = lax.all_gather(piece, both, axis=0, tiled=False).reshape(2, group.chans, D)
    else:
        wout = lax.all_gather(w_out[0], both, axis=0, tiled=False).reshape(2, INNER, D)
        wout = lax.dynamic_slice_in_dim(wout, here * group.chans, group.chans, 1)
    wout = jnp.pad(wout, ((0, 0), (0, G - group.chans), (0, 0)))
    packed = group.small(
        norm_gain[0], conv_w[0], conv_b[0], dt_bias[0], a_log[0], skip_d[0], gate_gain[0]
    )
    packed = lax.all_gather(packed, "section", axis=0, tiled=False)
    params = [group.parts(packed[s]) for s in range(2)]

    h0 = lax.dynamic_index_in_dim(tokens, core, 0, keepdims=False)[0]
    last_grad = lax.dynamic_index_in_dim(cotangent, core, 0, keepdims=False)[0]

    def forward(s, normed):
        conv, head, wide, _ = params[s]
        proj = jnp.dot(normed, win[s], preferred_element_type=F32).astype(BF)
        vg, ssq, mixed, yp, states = scan_fwd_call(proj, conv, head, wide)
        part = jnp.dot(vg, wout[s], preferred_element_type=F32).astype(BF)
        return part.reshape(n_seq, rows, D), ssq, (proj, mixed, yp, states)

    def backward(s, normed, kept, grad_b, stats):
        conv, head, wide, _ = params[s]
        proj, mixed, yp, states = kept
        d_normed = dot(grad_b, wout[s], 1, 1)
        d_proj, normed_out, g_wide, g_conv, g_head = scan_bwd_call(
            proj, mixed, yp, states, d_normed, stats, conv, head, wide
        )
        part = dot(d_proj, win[s], 1, 1).astype(BF).reshape(n_seq, rows, D)
        g_out = dot(normed_out, grad_b, 0, 0).astype(BF)
        g_in = dot(normed, d_proj, 0, 0).astype(BF)
        return part, g_in, g_out, (g_conv, g_head, g_wide)

    n0 = start_call(h0, params[0][3], n_seq)
    n0 = n0.reshape(length, D)
    part, ssq, kept0 = forward(0, n0)
    h1, pout0, n1, stat0 = forward_turn(part, ssq, h0, params[1][3], n_seq, False)
    n1 = n1.reshape(length, D)
    part, ssq, kept1 = forward(1, n1)
    h2, pout1, grad_b, stats = forward_turn(part, ssq, h1, last_grad, n_seq, True)
    part, gin1, gout1, small1 = backward(1, n1, kept1, grad_b.reshape(length, D), stats)
    low = lax.dynamic_index_in_dim(stat0, here, 0, keepdims=False)
    d1, gnorm1, grad_b, stats = backward_turn(
        part, h1, last_grad, params[1][3], (pout0, low), n_seq
    )
    part, gin0, gout0, small0 = backward(0, n0, kept0, grad_b.reshape(length, D), stats)
    d0, gnorm0 = backward_turn(part, h0, d1, params[0][3], None, n_seq)

    def to_layer(low_val, top_val):
        own = jnp.where(core == 0, low_val, top_val)
        other = jnp.where(core == 0, top_val, low_val)
        return own, lax.ppermute(other, "section", [(0, 1), (1, 0)])

    own, other = to_layer(gin0, gin1)
    gin = (own.astype(F32) + other.astype(F32)).astype(BF).reshape(n_wt, D // n_wt, group.NC)
    own, other = to_layer(gout0, gout1)
    gout = (own.astype(F32) + other.astype(F32)).astype(BF)
    if group.runs == n_wt:
        gout = gout.reshape(n_wt, G // n_wt, D)
        gin, gout = swap([gin, gout], "wt", n_wt, True, 5)
        gin = jnp.sum(gin.astype(F32), 0).astype(BF)
        gout = jnp.sum(gout.astype(F32), 0).astype(BF)
        gin, gout = swap([gin, gout], "seq", n_seq, False, 6)
        g_out = gout.reshape(INNER // n_wt, D).astype(F32)
    else:
        [gin] = swap([gin], "wt", n_wt, True, 5)
        gin = jnp.sum(gin.astype(F32), 0).astype(BF)
        gout = lax.psum(gout[: group.chans], "wt")
        gin, gout = swap([gin, gout], "seq", n_seq, False, 6)
        mine = INNER // n_wt
        gout = gout.reshape(INNER, D)
        g_out = lax.dynamic_slice_in_dim(gout, lax.axis_index("wt") * mine, mine, 0).astype(F32)
    shards = [gin[g] for g in range(n_seq)]
    shared = jnp.sum(gin[:, :, 2 * G : 2 * G + 2 * STATE].astype(F32), 0)
    g_in = jnp.concatenate(
        [a.astype(F32) for a in group.place([s[:, :G] for s in shards], HEAD_DIM)]
        + [a.astype(F32) for a in group.place([s[:, G : 2 * G] for s in shards], HEAD_DIM)]
        + [shared]
        + [a.astype(F32) for a in group.place([s[:, 2 * G + 2 * STATE :] for s in shards], 1)],
        axis=1,
    )

    packs = jnp.stack(
        [
            jnp.concatenate([*small0, gnorm0], 1),
            jnp.concatenate([*small1, gnorm1], 1),
        ]
    )
    packs = lax.psum(packs, ("section", "wt"))
    packs = lax.dynamic_index_in_dim(packs, core, 0, keepdims=False)
    packs = lax.all_gather(packs, "seq", axis=0, tiled=False)
    conv, head, wide, norm = group.parts(packs)
    conv_all = jnp.concatenate(
        group.place([conv[g, :, : group.chans] for g in range(n_seq)], HEAD_DIM)
        + [jnp.sum(conv[:, :, G:], 0)],
        axis=1,
    )
    head_all = jnp.concatenate(group.place([head[g] for g in range(n_seq)], 1), 1)
    wide_all = jnp.concatenate(
        group.place([wide[g, :, : group.chans] for g in range(n_seq)], HEAD_DIM), 1
    )
    g_skip = jnp.sum(wide_all[1].reshape(HEADS, HEAD_DIM), 1)

    own, other = to_layer(h1, h2)
    section_out = jnp.where(core == 0, jnp.stack([own, other]), jnp.stack([other, own]))
    own, other = to_layer(d0, d1)
    input_grad = jnp.where(core == 0, jnp.stack([own, other]), jnp.stack([other, own]))
    return (
        section_out[None, :, None],
        input_grad[None, :, None],
        jnp.sum(norm[:, 0], 0)[None],
        g_in[None],
        conv_all[None, :KERNEL],
        conv_all[None, KERNEL],
        head_all[None, 0],
        head_all[None, 1],
        g_skip[None],
        wide_all[None, 0],
        g_out[None],
    )


def solution(mesh):
    placed = (
        P(None, "wt", "seq", None),
        P(None, "wt", "seq", None),
        P("section", None),
        P("section", "wt", None),
        P("section", None, None),
        P("section", None),
        P("section", None),
        P("section", None),
        P("section", None),
        P("section", None),
        P("section", "wt", None),
    )
    return jax.shard_map(
        local,
        mesh=mesh,
        in_specs=placed,
        out_specs=(
            P("section", None, "wt", "seq", None),
            P("section", None, "wt", "seq", None),
            P("section", None),
            P("section", "wt", None),
            P("section", None, None),
            P("section", None),
            P("section", None),
            P("section", None),
            P("section", None),
            P("section", None),
            P("section", "wt", None),
        ),
        check_vma=False,
    )
```

time: 2130 us -> 879 us (0.41)
  waiting for transfers between devices: 1240 us -> 164 us
  Pallas kernels: 0 us -> 512 us
  matrix products: 303 us -> 61.7 us
  local copies, waits for them, and re-layouts: 256 us -> 56.3 us
  other arithmetic: 174 us -> 46.9 us
  starting transfers between devices: 70.7 us -> 0.46 us
  blocking collectives: 52.6 us -> 12 us
    pallas_call x0 -> x11, Pallas kernels: none -> 512 us  [the longest x2 268 us: swap(): pl.pallas_call(functools.partial(swap_kernel, axis, n, scatter), out_shap...]
    unnamed x13 -> x3, waiting for transfers between devices: 393 us -> 0.05 us
    all_gather x2, waiting for transfers between devices: 406 us -> 119 us  [the longest x1 105 us: local(): win = lax.all_gather(group.weight(w_in[0]), both, axis=0, tiled=False)]
    dot_general x53 -> x12, matrix products: 286 us -> 61.7 us  [the longest x8 41.9 us: dot(): lax.dot_general(a, b, (((ca,), (cb,)), ((), ())), precision=precision, pr...]
    psum x2 -> x1, waiting for transfers between devices: 238 us -> 44.6 us  [local(): packs = lax.psum(packs, ('section', 'wt'))]
    reduce_scatter x1 -> x0, waiting for transfers between devices: 159 us -> none  [local(): lax.psum_scatter(whole_out.astype(jnp.bfloat16), 'wt', scatter_dimension=...]
    all_to_all x16 -> x0, starting transfers between devices: 61.9 us -> none  [the longest x3 13.3 us: local(): lax.all_to_all(projected[:, INNER:2 * INNER], 'seq', split_axis=1, concat...]
    another operation x44 -> x5, other arithmetic: 47.7 us -> 3.31 us  [the longest x2 2.58 us: local(): jnp.stack([own, other])]
  transfers between devices with their start and end apart: 29 -> 7, of which waited for: 18 -> 3; matrix products, arithmetic and copies ran while one was open for 12% -> 8% of each run, Pallas kernels for 0% -> 15%
where the time goes in v1:
time: 879 us; the launch traced here: 868 us
  Pallas kernels  512 us (58%)
  waiting for transfers between devices  164 us (19%)
  matrix products  61.7 us (7%)
  local copies, waits for them, and re-layouts  56.3 us (6%)
  other arithmetic  46.9 us (5%)
  between operations  14.8 us (2%)
  blocking collectives  12 us (1%)
    pallas_call x2, Pallas kernels, swap(): pl.pallas_call(functools.partial(swap_kernel, axis, n, scatter), out_shap...  268 us
    all_gather x1, waiting for transfers between devices, local(): win = lax.all_gather(group.weight(w_in[0]), both, axis=0, tiled=False)  105 us
    pallas_call x2, Pallas kernels, forward_turn(): pl.pallas_call(functools.partial(forward_turn_kernel, n, last), out_shape...  84.2 us
    pallas_call x2, Pallas kernels, backward_turn(): pl.pallas_call(functools.partial(backward_turn_kernel, n, last), out_shap...  66.2 us
    pallas_call x2, Pallas kernels, scan_bwd_call(): pl.pallas_call(functools.partial(scan_backward, G), out_shape=(jax.ShapeD...  46.7 us
    psum x1, waiting for transfers between devices, local(): packs = lax.psum(packs, ('section', 'wt'))  44.6 us
    dot_general x8, matrix products, dot(): lax.dot_general(a, b, (((ca,), (cb,)), ((), ())), precision=precision, pr...  41.9 us
    unnamed x84, local copies, waits for them, and re-layouts  25.5 us
  transfers between devices with their start and end apart: 7, of which 3 were waited for; matrix products, arithmetic and copies ran while one was open for 8% of the time, Pallas kernels for 15%

profile of v1, /device:TPU:8, one launch (start us, length us, event | category | flops | bytes accessed | tf_op | source)
XLA Modules:
  0.0 867.8 jit_solution(11038279058804914533)
XLA Ops:
  24.8 21.6 %start.1 = bf16[4,128,1536]{2,1,0:T(8,128)(2,1)S(1)} custom-call(f32[128,1536]{1,0:T(8,128)S(1)} %dynamic-slice_bitcast_fusion.1.h_ref.refs_1_, f32[8,1536]{1,0:T(8,128)S(1)} %get-tuple-element.177.gain_ref.refs_3_), custom_call_target="tpu_custom_call" | custom-call | tf_op jit(solution)/shard_map/start/pallas_call | solution.py:382
  47.6 14.0 %all-gather.5.cloned.1.call-done = bf16[8,192,1536]{2,1,0:T(8,128)(2,1)} async-done(((bf16[1,192,1536]{2,1,0:T(8,128)(2,1)}), bf16[8,192,1536]{2,1,0:T(8,128)(2,1)}) %all-gather.5.cloned.1.call-update) | async-done | bytes 4718608 | tf_op jit(solution)/shard_map/all_gather | solution.py:653
  66.4 104.9 %all-gather.7.cloned.1.call-done = bf16[3072,1920]{0,1:T(8,128)(2,1)} async-done(((bf16[384,1920]{0,1:T(8,128)(2,1)}), bf16[3072,1920]{0,1:T(8,128)(2,1)}) %all-gather.7.cloned.1.call-update) | async-done | bytes 11796496 | tf_op jit(solution)/shard_map/all_gather | solution.py:648
  171.4 7.9 fusion.11.proj_ref
  179.3 12.5 %scan_forward.2 = (bf16[512,768]{1,0:T(8,128)(2,1)S(1)}, f32[4,8,128]{2,1,0:T(8,128)S(1)}, bf16[512,768]{1,0:T(8,128)(2,1)S(1)}, f32[512,768]{1,0:T(8,128)S(1)}, f32[4,128,768]{2,1,0:T(8,128)S(1)}) custom-call(bf16[512,1920]{1,0:T(8,128)(2,1)} %fusion.11.proj_ref, f32[8,1024]{1,0:T(8,128)S(1)} %get-tuple-element.175.cw_ref, ...), custom_call_target="tpu_custom_call" | custom-call | flops 589824000 | bytes 7864320 | tf_op jit(solution)/shard_map/scan_forward/pallas_call | solution.py:124
  193.2 42.2 %forward_turn.1 = (f32[128,1536]{1,0:T(8,128)S(1)}, f32[128,1536]{1,0:T(8,128)S(1)}, bf16[4,128,1536]{2,1,0:T(8,128)(2,1)S(1)}, f32[4,8,128]{2,1,0:T(8,128)S(1)}) custom-call(bf16[4,128,1536]{2,1,0:T(8,128)(2,1)S(1)} %bitcast.119, f32[4,8,128]{2,1,0:T(8,128)S(1)} %get-tuple-element.49.ssq_ref, f32[128,1536]{1,0:T(8,128)S(1)} %dynamic-slice_bitcast_fusion.1.h_ref.refs_1_, ...), custom_call_target="tpu_custom_call" | custom-call | tf_op jit(solution)/shard_map/forward_turn/pallas_call | solution.py:443
  235.4 7.9 fusion.17.proj_ref
  243.3 12.8 %scan_forward.3 = (bf16[512,768]{1,0:T(8,128)(2,1)S(1)}, f32[4,8,128]{2,1,0:T(8,128)S(1)}, bf16[512,768]{1,0:T(8,128)(2,1)S(1)}, f32[512,768]{1,0:T(8,128)S(1)}, f32[4,128,768]{2,1,0:T(8,128)S(1)}) custom-call(bf16[512,1920]{1,0:T(8,128)(2,1)} %fusion.17.proj_ref, f32[8,1024]{1,0:T(8,128)S(1)} %get-tuple-element.174.cw_ref, ...), custom_call_target="tpu_custom_call" | custom-call | flops 589824000 | bytes 7864320 | tf_op jit(solution)/shard_map/scan_forward/pallas_call | solution.py:124
  258.6 42.0 %forward_end.1 = (f32[128,1536]{1,0:T(8,128)S(1)}, f32[128,1536]{1,0:T(8,128)}, bf16[4,128,1536]{2,1,0:T(8,128)(2,1)S(1)}, f32[4,8,128]{2,1,0:T(8,128)S(1)}) custom-call(bf16[4,128,1536]{2,1,0:T(8,128)(2,1)} %bitcast.136, f32[4,8,128]{2,1,0:T(8,128)S(1)} %get-tuple-element.53.ssq_ref, f32[128,1536]{1,0:T(8,128)S(1)} %get-tuple-element.50.h_ref.refs_1_, ...), custom_call_target="tpu_custom_call" | custom-call | tf_op jit(solution)/shard_map/forward_end/pallas_call | solution.py:443
  306.7 23.2 %scan_backward.2 = (bf16[512,1920]{1,0:T(8,128)(2,1)}, bf16[512,768]{1,0:T(8,128)(2,1)S(1)}, f32[8,768]{1,0:T(8,128)S(1)}, f32[8,1024]{1,0:T(8,128)S(1)}, f32[8,128]{1,0:T(8,128)S(1)}) custom-call(bf16[512,1920]{1,0:T(8,128)(2,1)} %fusion.17.proj_ref, bf16[512,768]{1,0:T(8,128)(2,1)S(1)} %get-tuple-element.58.mixed_ref, ...), custom_call_target="tpu_custom_call" | custom-call | flops 1572864000 | bytes 11796480 | tf_op jit(solution)/shard_map/scan_backward/pallas_call | solution.py:271
  329.9 8.1 fusion.14
  338.0 44.6 %backward_turn.1 = (f32[128,1536]{1,0:T(8,128)S(1)}, f32[8,1536]{1,0:T(8,128)S(1)}, bf16[4,128,1536]{2,1,0:T(8,128)(2,1)S(1)}, f32[4,8,128]{2,1,0:T(8,128)S(1)}) custom-call(bf16[4,128,1536]{2,1,0:T(8,128)(2,1)} %bitcast.135, f32[128,1536]{1,0:T(8,128)S(1)} %get-tuple-element.50.h_ref.refs_1_, f32[128,1536]{1,0:T(8,128)S(1)} %dynamic-slice_bitcast_fusion.next_ref.refs_2_, ...), custom_call_target="tpu_custom_call" | custom-call | tf_op jit(solution)/shard_map/backward_turn/pallas_call | solution.py:526
  385.2 23.5 %scan_backward.3 = (bf16[512,1920]{1,0:T(8,128)(2,1)}, bf16[512,768]{1,0:T(8,128)(2,1)S(1)}, f32[8,768]{1,0:T(8,128)S(1)}, f32[8,1024]{1,0:T(8,128)S(1)}, f32[8,128]{1,0:T(8,128)S(1)}) custom-call(bf16[512,1920]{1,0:T(8,128)(2,1)} %fusion.11.proj_ref, bf16[512,768]{1,0:T(8,128)(2,1)S(1)} %get-tuple-element.55.mixed_ref, ...), custom_call_target="tpu_custom_call" | custom-call | flops 1572864000 | bytes 11796480 | tf_op jit(solution)/shard_map/scan_backward/pallas_call | solution.py:271
  408.7 7.2 convolution_convert_fusion.1
  415.9 6.1 fusion.8
  422.0 21.6 %backward_end.1 = (f32[128,1536]{1,0:T(8,128)S(1)}, f32[8,1536]{1,0:T(8,128)S(1)}) custom-call(bf16[4,128,1536]{2,1,0:T(8,128)(2,1)S(1)} %bitcast.120, f32[128,1536]{1,0:T(8,128)S(1)} %dynamic-slice_bitcast_fusion.1.h_ref.refs_1_, f32[128,1536]{1,0:T(8,128)S(1)} %get-tuple-element.69.refs_2_, f32[8,1536]{1,0:T(8,128)S(1)} %get-tuple-element.177.gain_ref.refs_3_), custom_call_target="tpu_custom_call" | custom-call | tf_op jit(solution)/shard_map/backward_end/pallas_call | solution.py:526
  453.6 6.6 broadcast_select_fusion
  460.3 44.6 %all-reduce.4.cloned.1.call-done = f32[2,8,3456]{2,1,0:T(8,128)} async-done(((f32[2,8,3456]{2,1,0:T(8,128)}), f32[2,8,3456]{2,1,0:T(8,128)}) %all-reduce.4.cloned.1.call-update) | async-done | bytes 221200 | tf_op jit(solution)/shard_map/psum | solution.py:741
  505.7 10.0 %all_gather.25 = f32[4,8,3456]{2,1,0:T(8,128)S(1)} all-gather(f32[1,8,3456]{2,1,0:T(8,128)S(1)} %constant_dynamic-slice_fusion), channel_id=1, replica_groups=mesh['section'=2,'seq'=4,'wt'=4] {'seq'}, dimensions={0}, use_global_device_ids=true | all-gather | bytes 552960 | tf_op jit(solution)/shard_map/all_gather | solution.py:743
  528.9 9.1 %add_convert_fusion = bf16[1536,1920]{1,0:T(8,128)(2,1)} fusion(bf16[1536,1920]{1,0:T(8,128)(2,1)} %collective-permute-done.2, bf16[1536,1920]{1,0:T(8,128)(2,1)} %convolution_convert_fusion.1, bf16[1536,1920]{1,0:T(8,128)(2,1)} %get-tuple-element.243, pred[]{:T(512)S(6)} %eq.2), kind=kLoop, calls=%fused_computation | loop fusion | flops 14745600 | bytes 23592960 | tf_op jit(solution)/shard_map/convert_element_type | solution.py:707
  538.0 177.2 %swap_wt_5.1 = (bf16[4,384,1920]{2,1,0:T(8,128)(2,1)}, bf16[4,192,1536]{2,1,0:T(8,128)(2,1)S(1)}) custom-call(bf16[4,384,1920]{2,1,0:T(8,128)(2,1)} %bitcast.128, bf16[4,192,1536]{2,1,0:T(8,128)(2,1)S(1)} %bitcast.115), custom_call_target="tpu_custom_call" | custom-call | tf_op jit(solution)/shard_map/swap_wt_5/pallas_call | solution.py:562
  723.4 90.9 %swap_seq_6.1 = (bf16[4,384,1920]{2,1,0:T(8,128)(2,1)}, bf16[4,192,1536]{2,1,0:T(8,128)(2,1)S(1)}) custom-call(bf16[384,1920]{1,0:T(8,128)(2,1)S(1)} %reduce_sum.61.refs_0_, bf16[192,1536]{1,0:T(8,128)(2,1)S(1)} %reduce_sum.62.refs_1_), custom_call_target="tpu_custom_call" | custom-call | tf_op jit(solution)/shard_map/swap_seq_6/pallas_call | solution.py:562
  831.5 14.0 %concatenate.82 = f32[384,6448]{1,0:T(8,128)} concatenate(f32[384,192]{1,0:T(8,128)} %get-tuple-element.157, f32[384,192]{1,0:T(8,128)} %get-tuple-element.149, f32[384,192]{1,0:T(8,128)} %get-tuple-element.141, f32[384,192]{1,0:T(8,128)} %get-tuple-element.133, f32[384,192]{1,0:T(8,128)} %get-tuple-element.156, f32[384,192]{1,0:T(8,128)} %get-tuple-element.148, ...), dimensions={1} | concatenate | bytes 19808256 | tf_op jit(solution)/shard_map/concatenate | solution.py:727
  845.5 10.7 %copy.70 = f32[1,384,6448]{1,2,0:T(8,128)} copy(f32[1,384,6448]{2,1,0:T(8,128)} %bitcast.127) | data formatting | bytes 19808256
  (181 shorter events, 89.7 us)
Async XLA Ops:
  7.2 54.4 %all-gather.5.cloned.1.call-start = ((), (), s32[]{:S(2)}) async-start(), calls=%async_computation | async-start | bytes 5308416 | tf_op jit(solution)/shard_map/all_gather | solution.py:653
  9.7 161.6 %all-gather.7.cloned.1.call-start = ((), (), s32[]{:S(2)}) async-start(), calls=%async_computation.2 | async-start | bytes 13271040 | tf_op jit(solution)/shard_map/all_gather | solution.py:648
  12.5 8.2 copy-start.30
  12.5 8.3 copy-start.26
  12.5 8.3 copy-start.27
  13.5 7.4 copy-start.29
  13.5 7.5 copy-start.34
  13.5 7.5 copy-start.31
  13.5 7.7 copy-start.28
  20.4 484.4 %all-reduce.4.cloned.1.call-start = ((), (), s32[]{:S(2)}) async-start(), calls=%async_computation.1 | async-start | bytes 442368 | tf_op jit(solution)/shard_map/psum | solution.py:741
  23.5 24.1 %copy-start.25 = (f32[2,1,128,1536]{3,2,1,0:T(8,128)S(1)}, f32[2,1,128,1536]{3,2,1,0:T(8,128)}, u32[]{:S(2)}) copy-start(f32[2,1,128,1536]{3,2,1,0:T(8,128)} %param.12) | copy-start | bytes 4718596
  179.3 12.5 %copy-start.20 = (bf16[4,192,1536]{2,1,0:T(8,128)(2,1)S(1)}, bf16[4,192,1536]{2,1,0:T(8,128)(2,1)}, u32[]{:S(2)}) copy-start(bf16[4,192,1536]{2,1,0:T(8,128)(2,1)} %get-tuple-element.105) | copy-start | bytes 7077892
  235.4 7.9 copy-start.6
  243.3 12.8 %copy-start.22 = (bf16[4,192,1536]{2,1,0:T(8,128)(2,1)S(1)}, bf16[4,192,1536]{2,1,0:T(8,128)(2,1)}, u32[]{:S(2)}) copy-start(bf16[4,192,1536]{2,1,0:T(8,128)(2,1)} %get-tuple-element.104) | copy-start | bytes 7077892
  306.7 214.0 %collective-permute-start = (f32[128,1536]{1,0:T(8,128)}, f32[128,1536]{1,0:T(8,128)}, u32[]{:S(2)}, u32[]{:S(2)}) collective-permute-start(f32[128,1536]{1,0:T(8,128)} %get-tuple-element.109), channel_id=1, source_target_pairs={{0,16},{16,0},{1,17},{17,1},{2,18},{18,2},{3,19},{19,3},{4,20},{20... | collective-permute-start | bytes 2359304 | tf_op jit(solution)/shard_map/ppermute | solution.py:704
  329.9 8.1 copy-start.12
  338.0 44.6 %copy-start.21 = (bf16[4,192,1536]{2,1,0:T(8,128)(2,1)S(1)}, bf16[4,192,1536]{2,1,0:T(8,128)(2,1)}, u32[]{:S(2)}) copy-start(bf16[4,192,1536]{2,1,0:T(8,128)(2,1)} %get-tuple-element.105) | copy-start | bytes 7077892
  385.2 23.5 %copy-start.5 = (bf16[4,128,1536]{2,1,0:T(8,128)(2,1)S(1)}, bf16[4,128,1536]{2,1,0:T(8,128)(2,1)}, u32[]{:S(2)}) copy-start(bf16[4,128,1536]{2,1,0:T(8,128)(2,1)} %copy-done.4) | copy-start | bytes 4718596
  408.7 7.2 copy-start.14
  408.7 7.2 copy-start.33
  448.4 75.1 %collective-permute-start.1 = (f32[128,1536]{1,0:T(8,128)S(1)}, f32[128,1536]{1,0:T(8,128)}, u32[]{:S(2)}, u32[]{:S(2)}) collective-permute-start(f32[128,1536]{1,0:T(8,128)S(1)} %copy-done.24), channel_id=1, source_target_pairs={{0,16},{16,0},{1,17},{17,1},{2,18},{18,2},{3,19},{19,3},{4,20},{20... | collective-permute-start | bytes 2359304 | tf_op jit(solution)/shard_map/ppermute | solution.py:704
  452.5 73.9 %collective-permute-start.3 = (bf16[768,1536]{1,0:T(8,128)(2,1)}, bf16[768,1536]{1,0:T(8,128)(2,1)}, u32[]{:S(2)}, u32[]{:S(2)}) collective-permute-start(bf16[768,1536]{1,0:T(8,128)(2,1)} %get-tuple-element.244), channel_id=1, source_target_pairs={{0,16},{16,0},{1,17},{17,1},{2,18},{18,2},{3,19},{19,3},{4,20},{20... | collective-permute-start | bytes 7077896 | tf_op jit(solution)/shard_map/ppermute | solution.py:704
  460.3 60.4 %copy-start.15 = (f32[1,1,1,128,1536]{4,3,2,1,0:T(8,128)S(1)}, f32[1,1,1,128,1536]{4,3,2,1,0:T(8,128)}, u32[]{:S(2)}) copy-start(f32[1,1,1,128,1536]{4,3,2,1,0:T(8,128)} %get-tuple-element.108) | copy-start | bytes 2359300
  460.3 68.7 %collective-permute-start.2 = (bf16[1536,1920]{1,0:T(8,128)(2,1)}, bf16[1536,1920]{1,0:T(8,128)(2,1)}, u32[]{:S(2)}, u32[]{:S(2)}) collective-permute-start(bf16[1536,1920]{1,0:T(8,128)(2,1)} %get-tuple-element.242), channel_id=1, source_target_pairs={{0,16},{16,0},{1,17},{17,1},{2,18},{18,2},{3,19},{19,3},{4,20},{20... | collective-permute-start | bytes 17694728 | tf_op jit(solution)/shard_map/ppermute | solution.py:704
  (20 other events, 73.4 us)
Sparse Core Ops, SparseCore 0:
  10.2 51.3 all-gather.4
  63.8 107.5 all-gather.6
  445.8 59.0 all-reduce.3

commit v2 on v1

--- a/solution.py
+++ b/solution.py
@@ -536,6 +536,92 @@
     )(*args)
 
 
+def backward_tail_kernel(n, G, *refs):
+    ins, outs, scratch = refs[:13], refs[13:20], refs[20:]
+    proj, mixed, yp, st, dn, sc, cw, hp, gw, win_ref, h_ref, og_ref, gain_ref = ins
+    dproj_ref, no_ref, gg_ref, gc_ref, gh_ref, dh_ref, gn_ref = outs
+    part_ref, got, s0, r0 = scratch[7:]
+    meet("seq", n)
+    scan_backward(
+        G, proj, mixed, yp, st, dn, sc, cw, hp, gw, dproj_ref, no_ref, gg_ref, gc_ref, gh_ref,
+        *scratch[:7]
+    )
+    me = lax.axis_index("seq")
+    rows = h_ref.shape[0]
+
+    def product(block):
+        at = pl.ds(pl.multiple_of(block * rows, rows), rows)
+
+        def tile(t, carry):
+            lanes = pl.ds(pl.multiple_of(t * 256, 256), 256)
+            part_ref[block, :, lanes] = dot(dproj_ref[at, :], win_ref[lanes, :], 1, 1).astype(BF)
+            return carry
+
+        lax.fori_loop(0, D // 256, tile, 0)
+
+    copies = []
+    for k in range(1, n):
+        peer = lax.rem(me + k, n)
+        product(peer)
+        copies.append(send(part_ref.at[peer], got.at[k - 1], (s0, r0), k - 1, "seq", peer))
+    product(me)
+    for copy in copies:
+        copy.wait()
+    gn_ref[...] = jnp.zeros_like(gn_ref)
+
+    def finish(at):
+        d_in = total_of(n, part_ref, got, at)
+        h = h_ref[at, :]
+        inv = lax.rsqrt(jnp.mean(h * h, axis=1, keepdims=True) + EPSILON)
+        normed = h * inv
+        gn_ref[0:1, :] += jnp.sum(d_in * normed, axis=0, keepdims=True)
+        d_s = d_in * gain_ref[0:1, :]
+        dh_ref[at, :] = og_ref[at, :] + inv * (
+            d_s - normed * jnp.mean(d_s * normed, axis=1, keepdims=True)
+        )
+
+    rows_loop(rows, finish)
+
+
+def backward_tail(proj, mixed, yp, st, dn, sc, cw, hp, gw, win, h, out_grad, gain, n):
+    L, NC = proj.shape
+    G = gw.shape[1]
+    CX = G + 2 * STATE
+    rows = h.shape[0]
+    args = (proj, mixed, yp, st, dn, sc, cw, hp, gw, win, h, out_grad, gain)
+    return pl.pallas_call(
+        functools.partial(backward_tail_kernel, n, G),
+        out_shape=(
+            jax.ShapeDtypeStruct((L, NC), BF),
+            jax.ShapeDtypeStruct((L, G), BF),
+            jax.ShapeDtypeStruct((8, G), F32),
+            jax.ShapeDtypeStruct((8, CX), F32),
+            jax.ShapeDtypeStruct((8, 128), F32),
+            jax.ShapeDtypeStruct((rows, D), F32),
+            jax.ShapeDtypeStruct((8, D), F32),
+        ),
+        in_specs=[VM] * len(args),
+        out_specs=[VM] * 7,
+        scratch_shapes=[
+            pltpu.VMEM((8 + L, 128), F32),
+            pltpu.VMEM((L, CX), F32),
+            pltpu.VMEM((L, 128), F32),
+            pltpu.VMEM((8, 128), F32),
+            pltpu.VMEM((L, CX), F32),
+            pltpu.VMEM((STATE, G), F32),
+            pltpu.VMEM((8, 128), F32),
+            pltpu.VMEM((n, rows, D), BF),
+            pltpu.VMEM((n - 1, rows, D), BF),
+            pltpu.SemaphoreType.DMA((n - 1,)),
+            pltpu.SemaphoreType.DMA((n - 1,)),
+        ],
+        compiler_params=pltpu.CompilerParams(
+            collective_id=4, has_side_effects=True, vmem_limit_bytes=VMEM_LIMIT
+        ),
+        name="backward_tail",
+    )(*args)
+
+
 def swap_kernel(axis, n, scatter, *refs):
     count = (len(refs) - 3) // 2
     sources, targets, (s0, r0, l0) = refs[:count], refs[count : 2 * count], refs[2 * count :]
@@ -695,8 +781,15 @@
     d1, gnorm1, grad_b, stats = backward_turn(
         part, h1, last_grad, params[1][3], (pout0, low), n_seq
     )
-    part, gin0, gout0, small0 = backward(0, n0, kept0, grad_b.reshape(length, D), stats)
-    d0, gnorm0 = backward_turn(part, h0, d1, params[0][3], None, n_seq)
+    grad_b = grad_b.reshape(length, D)
+    conv, head, wide, _ = params[0]
+    d_proj, normed_out, g_wide, g_conv, g_head, d0, gnorm0 = backward_tail(
+        *kept0, dot(grad_b, wout[0], 1, 1), stats, conv, head, wide, win[0], h0, d1,
+        params[0][3], n_seq
+    )
+    gout0 = dot(normed_out, grad_b, 0, 0).astype(BF)
+    gin0 = dot(n0, d_proj, 0, 0).astype(BF)
+    small0 = (g_conv, g_head, g_wide)
 
     def to_layer(low_val, top_val):
         own = jnp.where(core == 0, low_val, top_val)

time: 879 us -> 866 us (0.985)
  local copies, waits for them, and re-layouts: 56.3 us -> 67.8 us
  matrix products: 61.7 us -> 52.7 us
  waiting for transfers between devices: 164 us -> 155 us
    pallas_call x0 -> x1, Pallas kernels: none -> 50.2 us  [backward_tail(): pl.pallas_call(functools.partial(backward_tail_kernel, n, G), out_shape=(...]
    pallas_call x2 -> x1, Pallas kernels: 66.2 us -> 42.2 us  [backward_turn(): pl.pallas_call(functools.partial(backward_turn_kernel, n, last), out_shap...]
    pallas_call x2 -> x1, Pallas kernels: 46.7 us -> 23.2 us  [scan_bwd_call(): pl.pallas_call(functools.partial(scan_backward, G), out_shape=(jax.ShapeD...]
    dot_general x8 -> x7, matrix products: 41.9 us -> 33.1 us  [dot(): lax.dot_general(a, b, (((ca,), (cb,)), ((), ())), precision=precision, pr...]
    unnamed x84 -> x74, local copies, waits for them, and re-layouts: 25.5 us -> 23.5 us
  transfers between devices with their start and end apart: 7 -> 7, of which waited for: 3 -> 3; matrix products, arithmetic and copies ran while one was open for 8% -> 6% of each run, Pallas kernels for 15% -> 3%
where the time goes in v2:
time: 866 us; the launch traced here: 862 us
  Pallas kernels  515 us (59%)
  waiting for transfers between devices  155 us (18%)
  local copies, waits for them, and re-layouts  67.8 us (8%)
  matrix products  52.7 us (6%)
  other arithmetic  43.9 us (5%)
  between operations  14.7 us (2%)
  blocking collectives  12.2 us (1%)
    pallas_call x2, Pallas kernels, swap(): pl.pallas_call(functools.partial(swap_kernel, axis, n, scatter), out_shap...  268 us
    all_gather x1, waiting for transfers between devices, local(): win = lax.all_gather(group.weight(w_in[0]), both, axis=0, tiled=False)  105 us
    pallas_call x2, Pallas kernels, forward_turn(): pl.pallas_call(functools.partial(forward_turn_kernel, n, last), out_shape...  84.2 us
    pallas_call x1, Pallas kernels, backward_tail(): pl.pallas_call(functools.partial(backward_tail_kernel, n, G), out_shape=(...  50.2 us
    pallas_call x1, Pallas kernels, backward_turn(): pl.pallas_call(functools.partial(backward_turn_kernel, n, last), out_shap...  42.2 us
    psum x1, waiting for transfers between devices, local(): packs = lax.psum(packs, ('section', 'wt'))  40.5 us
    dot_general x7, matrix products, dot(): lax.dot_general(a, b, (((ca,), (cb,)), ((), ())), precision=precision, pr...  33.1 us
    pallas_call x2, Pallas kernels, scan_fwd_call(): pl.pallas_call(functools.partial(scan_forward, G), out_shape=(jax.ShapeDt...  25.3 us
  transfers between devices with their start and end apart: 7, of which 3 were waited for; matrix products, arithmetic and copies ran while one was open for 6% of the time, Pallas kernels for 3%

profile of v2, /device:TPU:8, one launch (start us, length us, event | category | flops | bytes accessed | tf_op | source)
XLA Modules:
  0.0 861.7 jit_solution(12809610212769871532)
XLA Ops:
  9.8 7.5 copy.91
  28.7 21.6 %start.1 = bf16[4,128,1536]{2,1,0:T(8,128)(2,1)S(1)} custom-call(f32[128,1536]{1,0:T(8,128)S(1)} %dynamic-slice_bitcast_fusion.1.h_ref.refs_10_, f32[8,1536]{1,0:T(8,128)S(1)} %get-tuple-element.185.gain_ref.refs_12_), custom_call_target="tpu_custom_call" | custom-call | tf_op jit(solution)/shard_map/start/pallas_call | solution.py:382
  52.6 9.0 %all-gather.5.cloned.1.call-done = bf16[8,192,1536]{2,1,0:T(8,128)(2,1)} async-done(((bf16[1,192,1536]{2,1,0:T(8,128)(2,1)}), bf16[8,192,1536]{2,1,0:T(8,128)(2,1)}) %all-gather.5.cloned.1.call-update) | async-done | bytes 4718608 | tf_op jit(solution)/shard_map/all_gather | solution.py:739
  66.4 105.0 %all-gather.7.cloned.1.call-done = bf16[3072,1920]{1,0:T(8,128)(2,1)} async-done(((bf16[384,1920]{1,0:T(8,128)(2,1)}), bf16[3072,1920]{1,0:T(8,128)(2,1)}) %all-gather.7.cloned.1.call-update) | async-done | bytes 11796496 | tf_op jit(solution)/shard_map/all_gather | solution.py:734
  171.4 7.9 convolution_convert_fusion.6.proj_ref.refs_0_
  179.3 12.5 %scan_forward.2 = (bf16[512,768]{1,0:T(8,128)(2,1)S(1)}, f32[4,8,128]{2,1,0:T(8,128)S(1)}, bf16[512,768]{1,0:T(8,128)(2,1)S(1)}, f32[512,768]{1,0:T(8,128)S(1)}, f32[4,128,768]{2,1,0:T(8,128)S(1)}) custom-call(bf16[512,1920]{1,0:T(8,128)(2,1)} %convolution_convert_fusion.6.proj_ref.refs_0_, f32[8,1024]{1,0:T(8,128)S(1)} %get-tuple-element.183.cw_ref.refs_6_, ...), custom_call_target="tpu_custom_call" | custom-call | flops 589824000 | bytes 7864320 | tf_op jit(solution)/shard_map/scan_forward/pallas_call | solution.py:124
  193.1 42.2 %forward_turn.1 = (f32[128,1536]{1,0:T(8,128)S(1)}, f32[128,1536]{1,0:T(8,128)S(1)}, bf16[4,128,1536]{2,1,0:T(8,128)(2,1)S(1)}, f32[4,8,128]{2,1,0:T(8,128)S(1)}) custom-call(bf16[4,128,1536]{2,1,0:T(8,128)(2,1)S(1)} %bitcast.109, f32[4,8,128]{2,1,0:T(8,128)S(1)} %get-tuple-element.49.ssq_ref, f32[128,1536]{1,0:T(8,128)S(1)} %dynamic-slice_bitcast_fusion.1.h_ref.refs_10_, ...), custom_call_target="tpu_custom_call" | custom-call | tf_op jit(solution)/shard_map/forward_turn/pallas_call | solution.py:443
  235.4 7.9 fusion.7.proj_ref
  243.2 12.8 %scan_forward.3 = (bf16[512,768]{1,0:T(8,128)(2,1)S(1)}, f32[4,8,128]{2,1,0:T(8,128)S(1)}, bf16[512,768]{1,0:T(8,128)(2,1)S(1)}, f32[512,768]{1,0:T(8,128)S(1)}, f32[4,128,768]{2,1,0:T(8,128)S(1)}) custom-call(bf16[512,1920]{1,0:T(8,128)(2,1)} %fusion.7.proj_ref, f32[8,1024]{1,0:T(8,128)S(1)} %get-tuple-element.182.cw_ref, ...), custom_call_target="tpu_custom_call" | custom-call | flops 589824000 | bytes 7864320 | tf_op jit(solution)/shard_map/scan_forward/pallas_call | solution.py:124
  258.6 42.0 %forward_end.1 = (f32[128,1536]{1,0:T(8,128)S(1)}, f32[128,1536]{1,0:T(8,128)}, bf16[4,128,1536]{2,1,0:T(8,128)(2,1)S(1)}, f32[4,8,128]{2,1,0:T(8,128)S(1)}) custom-call(bf16[4,128,1536]{2,1,0:T(8,128)(2,1)} %bitcast.124, f32[4,8,128]{2,1,0:T(8,128)S(1)} %get-tuple-element.53.ssq_ref, f32[128,1536]{1,0:T(8,128)S(1)} %get-tuple-element.50.h_ref.refs_1_, ...), custom_call_target="tpu_custom_call" | custom-call | tf_op jit(solution)/shard_map/forward_end/pallas_call | solution.py:443
  300.6 5.1 fusion.35.dn_ref
  305.7 23.2 %scan_backward.1 = (bf16[512,1920]{1,0:T(8,128)(2,1)}, bf16[512,768]{1,0:T(8,128)(2,1)S(1)}, f32[8,768]{1,0:T(8,128)S(1)}, f32[8,1024]{1,0:T(8,128)S(1)}, f32[8,128]{1,0:T(8,128)S(1)}) custom-call(bf16[512,1920]{1,0:T(8,128)(2,1)} %fusion.7.proj_ref, bf16[512,768]{1,0:T(8,128)(2,1)S(1)} %get-tuple-element.58.mixed_ref, ...), custom_call_target="tpu_custom_call" | custom-call | flops 1572864000 | bytes 11796480 | tf_op jit(solution)/shard_map/scan_backward/pallas_call | solution.py:271
  328.9 8.1 fusion.4
  337.0 42.2 %backward_turn.1 = (f32[128,1536]{1,0:T(8,128)S(1)}, f32[8,1536]{1,0:T(8,128)S(1)}, bf16[4,128,1536]{2,1,0:T(8,128)(2,1)S(1)}, f32[4,8,128]{2,1,0:T(8,128)S(1)}) custom-call(bf16[4,128,1536]{2,1,0:T(8,128)(2,1)} %bitcast.123, f32[128,1536]{1,0:T(8,128)S(1)} %get-tuple-element.50.h_ref.refs_1_, f32[128,1536]{1,0:T(8,128)S(1)} %dynamic-slice_bitcast_fusion.next_ref.refs_2_, ...), custom_call_target="tpu_custom_call" | custom-call | tf_op jit(solution)/shard_map/backward_turn/pallas_call | solution.py:526
  381.8 5.7 slice.649.refs_9_
  387.5 50.2 %backward_tail.1 = (bf16[512,1920]{1,0:T(8,128)(2,1)}, bf16[512,768]{1,0:T(8,128)(2,1)S(1)}, f32[8,768]{1,0:T(8,128)S(1)}, f32[8,1024]{1,0:T(8,128)S(1)}, f32[8,...) custom-call(bf16[512,1920]{1,0:T(8,128)(2,1)} %convolution_convert_fusion.6.proj_ref.refs_0_, ...), custom_call_target="tpu_custom_call" | custom-call | tf_op jit(solution)/shard_map/backward_tail/pallas_call | solution.py:592
  450.5 6.6 broadcast_select_fusion
  460.2 40.5 %all-reduce.4.cloned.1.call-done = f32[2,8,3456]{2,1,0:T(8,128)} async-done(((f32[2,8,3456]{2,1,0:T(8,128)}), f32[2,8,3456]{2,1,0:T(8,128)}) %all-reduce.4.cloned.1.call-update) | async-done | bytes 221200 | tf_op jit(solution)/shard_map/psum | solution.py:834
  501.7 10.0 %all_gather.25 = f32[4,8,3456]{2,1,0:T(8,128)S(1)} all-gather(f32[1,8,3456]{2,1,0:T(8,128)S(1)} %constant_dynamic-slice_fusion), channel_id=1, replica_groups=mesh['section'=2,'seq'=4,'wt'=4] {'seq'}, dimensions={0}, use_global_device_ids=true | all-gather | bytes 552960 | tf_op jit(solution)/shard_map/all_gather | solution.py:836
  523.3 9.1 %add_convert_fusion = bf16[1536,1920]{1,0:T(8,128)(2,1)} fusion(bf16[1536,1920]{1,0:T(8,128)(2,1)} %collective-permute-done.2, bf16[1536,1920]{1,0:T(8,128)(2,1)} %copy-done.19, bf16[1536,1920]{1,0:T(8,128)(2,1)} %get-tuple-element.251, pred[]{:T(512)S(6)} %eq.2), kind=kLoop, calls=%fused_computation | loop fusion | flops 14745600 | bytes 23592960 | tf_op jit(solution)/shard_map/convert_element_type | solution.py:800
  532.4 177.2 %swap_wt_5.1 = (bf16[4,384,1920]{2,1,0:T(8,128)(2,1)}, bf16[4,192,1536]{2,1,0:T(8,128)(2,1)S(1)}) custom-call(bf16[4,384,1920]{2,1,0:T(8,128)(2,1)} %bitcast.117, bf16[4,192,1536]{2,1,0:T(8,128)(2,1)S(1)} %bitcast.105), custom_call_target="tpu_custom_call" | custom-call | tf_op jit(solution)/shard_map/swap_wt_5/pallas_call | solution.py:648
  717.8 90.9 %swap_seq_6.1 = (bf16[4,384,1920]{2,1,0:T(8,128)(2,1)}, bf16[4,192,1536]{2,1,0:T(8,128)(2,1)S(1)}) custom-call(bf16[384,1920]{1,0:T(8,128)(2,1)S(1)} %reduce_sum.61.refs_0_, bf16[192,1536]{1,0:T(8,128)(2,1)S(1)} %reduce_sum.62.refs_1_), custom_call_target="tpu_custom_call" | custom-call | tf_op jit(solution)/shard_map/swap_seq_6/pallas_call | solution.py:648
  825.4 14.1 %concatenate.82 = f32[384,6448]{1,0:T(8,128)} concatenate(f32[384,192]{1,0:T(8,128)} %get-tuple-element.165, f32[384,192]{1,0:T(8,128)} %get-tuple-element.157, f32[384,192]{1,0:T(8,128)} %get-tuple-element.149, f32[384,192]{1,0:T(8,128)} %get-tuple-element.141, f32[384,192]{1,0:T(8,128)} %get-tuple-element.164, f32[384,192]{1,0:T(8,128)} %get-tuple-element.156, ...), dimensions={1} | concatenate | bytes 19808256 | tf_op jit(solution)/shard_map/concatenate | solution.py:820
  839.5 10.7 %copy.93 = f32[1,384,6448]{1,2,0:T(8,128)} copy(f32[1,384,6448]{2,1,0:T(8,128)} %bitcast.116) | data formatting | bytes 19808256
  (182 shorter events, 85.1 us)
Async XLA Ops:
  7.2 54.4 %all-gather.5.cloned.1.call-start = ((), (), s32[]{:S(2)}) async-start(), calls=%async_computation | async-start | bytes 5308416 | tf_op jit(solution)/shard_map/all_gather | solution.py:739
  9.7 161.7 %all-gather.7.cloned.1.call-start = ((), (), s32[]{:S(2)}) async-start(), calls=%async_computation.2 | async-start | bytes 13271040 | tf_op jit(solution)/shard_map/all_gather | solution.py:734
  24.2 476.5 %all-reduce.4.cloned.1.call-start = ((), (), s32[]{:S(2)}) async-start(), calls=%async_computation.1 | async-start | bytes 442368 | tf_op jit(solution)/shard_map/psum | solution.py:834
  179.3 12.5 %copy-start.24 = (bf16[4,192,1536]{2,1,0:T(8,128)(2,1)S(1)}, bf16[4,192,1536]{2,1,0:T(8,128)(2,1)}, u32[]{:S(2)}) copy-start(bf16[4,192,1536]{2,1,0:T(8,128)(2,1)} %get-tuple-element.113) | copy-start | bytes 7077892
  235.3 7.9 copy-start.11
  243.2 12.9 %copy-start.26 = (bf16[4,192,1536]{2,1,0:T(8,128)(2,1)S(1)}, bf16[4,192,1536]{2,1,0:T(8,128)(2,1)}, u32[]{:S(2)}) copy-start(bf16[4,192,1536]{2,1,0:T(8,128)(2,1)} %get-tuple-element.112) | copy-start | bytes 7077892
  300.6 5.1 copy-start.7
  300.6 5.1 copy-start.13
  328.9 8.1 copy-start.16
  337.0 42.2 %copy-start.25 = (bf16[4,192,1536]{2,1,0:T(8,128)(2,1)S(1)}, bf16[4,192,1536]{2,1,0:T(8,128)(2,1)}, u32[]{:S(2)}) copy-start(bf16[4,192,1536]{2,1,0:T(8,128)(2,1)} %get-tuple-element.113) | copy-start | bytes 7077892
  379.2 8.3 copy-start.15
  438.6 4.1 copy-start.9
  446.3 74.4 %collective-permute-start.3 = (bf16[768,1536]{1,0:T(8,128)(2,1)}, bf16[768,1536]{1,0:T(8,128)(2,1)}, u32[]{:S(2)}, u32[]{:S(2)}) collective-permute-start(bf16[768,1536]{1,0:T(8,128)(2,1)} %get-tuple-element.252), channel_id=1, source_target_pairs={{0,16},{16,0},{1,17},{17,1},{2,18},{18,2},{3,19},{19,3},{4,20},{20... | collective-permute-start | bytes 7077896 | tf_op jit(solution)/shard_map/ppermute | solution.py:797
  446.5 3.9 copy-start.12
  446.5 3.9 copy-start.33
  450.4 6.6 copy-start.19
  450.4 7.0 copy-start.10
  457.0 66.3 %collective-permute-start.2 = (bf16[1536,1920]{1,0:T(8,128)(2,1)}, bf16[1536,1920]{1,0:T(8,128)(2,1)}, u32[]{:S(2)}, u32[]{:S(2)}) collective-permute-start(bf16[1536,1920]{1,0:T(8,128)(2,1)} %get-tuple-element.250), channel_id=1, source_target_pairs={{0,16},{16,0},{1,17},{17,1},{2,18},{18,2},{3,19},{19,3},{4,20},{20... | collective-permute-start | bytes 17694728 | tf_op jit(solution)/shard_map/ppermute | solution.py:797
  458.7 57.9 %collective-permute-start.1 = (f32[128,1536]{1,0:T(8,128)}, f32[128,1536]{1,0:T(8,128)S(1)}, u32[]{:S(2)}, u32[]{:S(2)}) collective-permute-start(f32[128,1536]{1,0:T(8,128)} %get-tuple-element.115), channel_id=1, source_target_pairs={{0,16},{16,0},{1,17},{17,1},{2,18},{18,2},{3,19},{19,3},{4,20},{20... | collective-permute-start | bytes 2359304 | tf_op jit(solution)/shard_map/ppermute | solution.py:797
  459.8 56.8 %copy-start.20 = (f32[1,1,1,128,1536]{4,3,2,1,0:T(8,128)S(1)}, f32[1,1,1,128,1536]{4,3,2,1,0:T(8,128)}, u32[]{:S(2)}) copy-start(f32[1,1,1,128,1536]{4,3,2,1,0:T(8,128)} %get-tuple-element.114) | copy-start | bytes 2359300
  459.8 58.1 %collective-permute-start = (f32[128,1536]{1,0:T(8,128)}, f32[128,1536]{1,0:T(8,128)}, u32[]{:S(2)}, u32[]{:S(2)}) collective-permute-start(f32[128,1536]{1,0:T(8,128)} %get-tuple-element.117), channel_id=1, source_target_pairs={{0,16},{16,0},{1,17},{17,1},{2,18},{18,2},{3,19},{19,3},{4,20},{20... | collective-permute-start | bytes 2359304 | tf_op jit(solution)/shard_map/ppermute | solution.py:797
  516.6 4.1 copy-start.23
  808.7 4.0 copy-start.2
  850.2 4.7 copy-start.1
  (19 other events, 47.3 us)
Sparse Core Ops, SparseCore 0:
  10.2 51.3 all-gather.4
  63.8 107.6 all-gather.6
  439.5 61.2 all-reduce.3

commit v3 on v0

v3 whole, which is shorter than its diff:
```python
import functools
from typing import Any, NamedTuple

import jax
import jax.numpy as jnp
from jax import lax
from jax.experimental import pallas as pl
from jax.experimental.pallas import tpu as pltpu
from jax.sharding import PartitionSpec as P

D = 1536
HEADS = 48
HEAD_DIM = 64
STATE = 128
KERNEL = 4
INNER = 3072
CONV = 3328
EPSILON = 1e-05

Q = 128
F32 = jnp.float32
BF = jnp.bfloat16
SEQ, WT, SECTION = "seq", "wt", "section"
FORWARD_VMEM = 56 * 2**20
BACKWARD_VMEM = 60 * 2**20
SMALL_VMEM = 40 * 2**20
MESH = pl.DeviceIdType.MESH
VM = pl.BlockSpec(memory_space=pltpu.VMEM)
ANY = pl.BlockSpec(memory_space=pl.ANY)
TILE = 16


def dot(a, b, ca, cb, precision=None):
    return lax.dot_general(a, b, (((ca,), (cb,)), ((), ())), precision=precision, preferred_element_type=F32)

def sigmoid(x):
    return 1.0 / (1.0 + jnp.exp(-x))

def softplus(x):
    return jnp.maximum(x, 0.0) + jnp.log1p(jnp.exp(-jnp.abs(x)))

def lane_mask(rows):
    return lax.broadcasted_iota(jnp.int32, (rows, 128), 1) < HEAD_DIM

def spread(cols, pair, mask):
    a = jnp.broadcast_to(cols[:, 2 * pair : 2 * pair + 1], mask.shape)
    b = jnp.broadcast_to(cols[:, 2 * pair + 1 : 2 * pair + 2], mask.shape)
    return jnp.where(mask, a, b)

def split_pair(u, mask):
    zero = jnp.zeros_like(u)
    return jnp.concatenate([jnp.where(mask, u, zero), jnp.where(mask, zero, u)], axis=0)

def conv_tile(proj_ref, cw_ref, pad, proj_at, conv_at, rows):
    pad[0:8, :] = jnp.zeros((8, 128), F32)
    pad[8 : 8 + rows, :] = proj_ref[:, pl.ds(proj_at, 128)].astype(F32)
    pre = jnp.broadcast_to(cw_ref[4:5, pl.ds(conv_at, 128)], (rows, 128))
    for k in range(KERNEL):
        pre = pre + cw_ref[k : k + 1, pl.ds(conv_at, 128)] * pad[5 + k : 5 + k + rows, :]
    return pre

def step_inputs(proj_ref, at, hp_ref, sel_ref, dt_at):
    return dot(proj_ref[at, dt_at : dt_at + 128], sel_ref[...], 1, 0) + hp_ref[0:1, :]

def chunk_factors(dt, hp_ref):
    rate = dt * hp_ref[1:2, :]
    rows = lax.broadcasted_iota(jnp.int32, (Q, Q), 0)
    cols = lax.broadcasted_iota(jnp.int32, (Q, Q), 1)
    tri = (rows >= cols).astype(F32)
    cum = dot(tri, rate, 1, 0, lax.Precision.HIGHEST)
    return rate, cum, rows >= cols

def decay_pair(cum, cum_t, causal, pair):
    parts = []
    for h in (2 * pair, 2 * pair + 1):
        diff = jnp.broadcast_to(cum[:, h : h + 1], (Q, Q)) - jnp.broadcast_to(cum_t[h : h + 1, :], (Q, Q))
        parts.append(jnp.exp(jnp.where(causal, diff, -1e30)))
    return jnp.concatenate(parts, axis=1)

def scan_forward(G, proj_ref, cw_ref, hp_ref, gw_ref, sel_ref, mixed_ref, yp_ref, st_ref, pad, xc, dts, state):
    L = proj_ref.shape[0]

    def conv(tile, carry):
        lanes = pl.ds(pl.multiple_of(tile * 128, 128), 128)
        pre = conv_tile(proj_ref, cw_ref, pad, pl.multiple_of(G + tile * 128, 128), lanes.start, L)
        xc[:, lanes] = pre * sigmoid(pre)
        return carry

    lax.fori_loop(0, (G + 2 * STATE) // 128, conv, 0)
    dt_at = 2 * G + 2 * STATE
    dts[...] = softplus(step_inputs(proj_ref, slice(0, L), hp_ref, sel_ref, dt_at))
    state[...] = jnp.zeros_like(state)
    mask = lane_mask(Q)

    def chunk(c, _):
        at = pl.ds(pl.multiple_of(c * Q, Q), Q)
        dt = dts[at, :]
        rate, cum, causal = chunk_factors(dt, hp_ref)
        cum_t = cum.T
        last = cum[Q - 1 : Q, :]
        e_cum = jnp.exp(cum)
        tail = jnp.exp(last - cum) * dt
        e_last = jnp.broadcast_to(jnp.exp(last), (8, 128))
        b = xc[at, G : G + STATE].astype(BF)
        cc = xc[at, G + STATE : G + 2 * STATE].astype(BF)
        scores = dot(cc, b, 1, 1)
        scores2 = jnp.concatenate([scores, scores], axis=1)
        for p in range(G // 128):
            lanes = slice(p * 128, p * 128 + 128)
            x = xc[at, lanes]
            u = (x * spread(dt, p, mask)).astype(BF)
            m = (scores2 * decay_pair(cum, cum_t, causal, p)).astype(BF)
            before = state[:, lanes]
            st_ref[c, :, lanes] = before
            y = dot(m, split_pair(u, mask), 1, 0)
            y = y + dot(cc, before.astype(BF), 1, 0) * spread(e_cum, p, mask)
            yp_ref[at, lanes] = y
            after = dot(b, (x * spread(tail, p, mask)).astype(BF), 0, 0)
            state[:, lanes] = before * spread(e_last, p, mask[0:8])[0:1, :] + after
            mixed_ref[at, lanes] = (y + gw_ref[1:2, lanes] * x).astype(BF)
        return 0

    lax.fori_loop(0, L // Q, chunk, 0)


def gate_forward(G, proj_ref, gw_ref, mixed_ref, vg_ref, ssq_ref):
    def chunk(c, _):
        at = pl.ds(pl.multiple_of(c * Q, Q), Q)
        ssq = jnp.zeros((Q, 1), F32)
        for p in range(G // 128):
            lanes = slice(p * 128, p * 128 + 128)
            gate = proj_ref[at, lanes].astype(F32)
            v = mixed_ref[at, lanes].astype(F32) * (gate * sigmoid(gate))
            vg_ref[at, lanes] = (v * gw_ref[0:1, lanes]).astype(BF)
            ssq = ssq + jnp.sum(v * v, axis=1, keepdims=True)
        ssq_ref[c] = jnp.broadcast_to(ssq, (Q, 128)).T[0:8, :]
        return 0

    lax.fori_loop(0, proj_ref.shape[0] // Q, chunk, 0)


def gate_backward(G, proj_ref, mixed_ref, dn_ref, sc_ref, gw_ref, dy_ref, gg_ref):
    gg_ref[...] = jnp.zeros_like(gg_ref)

    def chunk(c, _):
        at = pl.ds(pl.multiple_of(c * Q, Q), Q)
        sc = jnp.concatenate([sc_ref[c], jnp.zeros((Q - 8, 128), F32)], axis=0).T
        inv2 = jnp.broadcast_to(sc[:, 0:1], (Q, 128))
        mdot = jnp.broadcast_to(sc[:, 1:2], (Q, 128))
        for p in range(G // 128):
            lanes = slice(p * 128, p * 128 + 128)
            gate = proj_ref[at, lanes].astype(F32)
            sig = sigmoid(gate)
            act = gate * sig
            mixed = mixed_ref[at, lanes].astype(F32)
            n2 = mixed * act * inv2
            mixed_ref[at, lanes] = (n2 * gw_ref[0:1, lanes]).astype(BF)
            dn = dn_ref[at, lanes]
            gg_ref[0:1, lanes] += jnp.sum(dn * n2, axis=0, keepdims=True)
            d_v = inv2 * (dn * gw_ref[0:1, lanes] - n2 * mdot)
            dy_ref[at, lanes] = (d_v * act).astype(BF)
            proj_ref[at, lanes] = (d_v * mixed * (sig * (1.0 + gate * (1.0 - sig)))).astype(BF)
        return 0

    lax.fori_loop(0, proj_ref.shape[0] // Q, chunk, 0)


def scan_backward(G, proj_ref, dy_ref, yp_ref, st_ref, cw_ref, hp_ref, gw_ref, sel_ref, gg_ref, gc_ref, gh_ref,
                  pad, xc, dts, dstate):
    L = proj_ref.shape[0]
    nb = L // Q
    mask = lane_mask(Q)

    def conv(tile, carry):
        lanes = pl.ds(pl.multiple_of(tile * 128, 128), 128)
        pre = conv_tile(proj_ref, cw_ref, pad, pl.multiple_of(G + tile * 128, 128), lanes.start, L)
        xc[:, lanes] = pre * sigmoid(pre)
        return carry

    lax.fori_loop(0, (G + 2 * STATE) // 128, conv, 0)
    dt_at = 2 * G + 2 * STATE
    dts[...] = softplus(step_inputs(proj_ref, slice(0, L), hp_ref, sel_ref, dt_at))
    dstate[...] = jnp.zeros_like(dstate)
    gh_ref[...] = jnp.zeros_like(gh_ref)

    def chunk(step, _):
        c = nb - 1 - step
        at = pl.ds(pl.multiple_of(c * Q, Q), Q)
        dt = dts[at, :]
        rate, cum, causal = chunk_factors(dt, hp_ref)
        cum_t = cum.T
        last = cum[Q - 1 : Q, :]
        e_cum = jnp.exp(cum)
        tail = jnp.exp(last - cum)
        e_last = jnp.broadcast_to(jnp.exp(last), (8, 128))
        b = xc[at, G : G + STATE].astype(BF)
        cc = xc[at, G + STATE : G + 2 * STATE].astype(BF)
        scores = dot(cc, b, 1, 1)
        scores2 = jnp.concatenate([scores, scores], axis=1)
        d_scores = jnp.zeros((Q, Q), F32)
        d_b = jnp.zeros((Q, STATE), F32)
        d_c = jnp.zeros((Q, STATE), F32)
        d_cum = jnp.zeros((Q, 128), F32)
        d_dt = jnp.zeros((Q, 128), F32)
        d_last = jnp.zeros((8, 128), F32)
        lane_ids = lax.broadcasted_iota(jnp.int32, (Q, 128), 1)
        for p in range(G // 128):
            lanes = slice(p * 128, p * 128 + 128)
            dyb = dy_ref[at, lanes]
            d_y = dyb.astype(F32)
            x = xc[at, lanes]
            dt_x = spread(dt, p, mask)
            u = (x * dt_x).astype(BF)
            u2 = split_pair(u, mask)
            uf = u.astype(F32)
            dec = decay_pair(cum, cum_t, causal, p)
            m = (scores2 * dec).astype(BF)
            dm = dot(dyb, u2, 1, 1) * dec
            d_scores = d_scores + dm[:, :Q] + dm[:, Q:]
            both = dot(m, dyb, 0, 0)
            du = jnp.where(mask, both[:Q], both[Q:])
            tail_x = spread(tail, p, mask)
            before = st_ref[c, :, lanes]
            after = dstate[:, lanes]
            afterb = after.astype(BF)
            du_out = tail_x * dot(b, afterb, 1, 0)
            du = du + du_out
            dye = (d_y * spread(e_cum, p, mask)).astype(BF)
            d_c = d_c + dot(dye, before.astype(BF), 1, 1)
            d_b = d_b + dot((uf * tail_x).astype(BF), afterb, 1, 1)
            e_last_x = spread(e_last, p, mask[0:8])
            dstate[:, lanes] = after * e_last_x[0:1, :] + dot(cc, dye, 0, 0)
            z3 = jnp.sum(uf * du_out, axis=0, keepdims=True) + e_last_x[0:1, :] * jnp.sum(before * after, axis=0, keepdims=True)
            z1 = d_y * yp_ref[at, lanes] - uf * du
            z2 = x * du
            zero = jnp.zeros_like(z1)
            for half, h in ((True, 2 * p), (False, 2 * p + 1)):
                keep = mask if half else jnp.logical_not(mask)
                here = lane_ids == h
                d_cum = jnp.where(here, jnp.sum(jnp.where(keep, z1, zero), axis=1, keepdims=True), d_cum)
                d_dt = jnp.where(here, jnp.sum(jnp.where(keep, z2, zero), axis=1, keepdims=True), d_dt)
                s3 = jnp.sum(jnp.where(keep[0:8], jnp.broadcast_to(z3, (8, 128)), 0.0), axis=1, keepdims=True)
                d_last = jnp.where(here[0:8], s3, d_last)
            xc[at, lanes] = dt_x * du + gw_ref[1:2, lanes] * d_y
            gg_ref[1:2, lanes] += jnp.sum(d_y * x, axis=0, keepdims=True)
        dsb = d_scores.astype(BF)
        xc[at, G : G + STATE] = d_b + dot(dsb, cc, 0, 0)
        xc[at, G + STATE : G + 2 * STATE] = d_c + dot(dsb, b, 1, 0)
        rows = lax.broadcasted_iota(jnp.int32, (Q, Q), 0)
        cols = lax.broadcasted_iota(jnp.int32, (Q, Q), 1)
        upper = (rows <= cols).astype(F32)
        d_rate = dot(upper, d_cum, 1, 0, lax.Precision.HIGHEST) + d_last[0:1, :]
        d_step = d_dt + d_rate * hp_ref[1:2, :]
        d_raw = d_step * sigmoid(step_inputs(proj_ref, at, hp_ref, sel_ref, dt_at))
        proj_ref[at, dt_at : dt_at + 128] = dot(d_raw.astype(BF), sel_ref[...], 1, 1).astype(BF)
        gh_ref[0:1, :] += jnp.sum(d_raw, axis=0, keepdims=True)
        gh_ref[1:2, :] += jnp.sum(d_rate * rate, axis=0, keepdims=True)
        return 0

    lax.fori_loop(0, nb, chunk, 0)

    gc_ref[...] = jnp.zeros_like(gc_ref)

    def conv_back(tile, carry):
        lanes = pl.ds(pl.multiple_of(tile * 128, 128), 128)
        proj_at = pl.multiple_of(G + tile * 128, 128)
        pre = conv_tile(proj_ref, cw_ref, pad, proj_at, lanes.start, L)
        sig = sigmoid(pre)
        d_pre = xc[:, lanes] * (sig * (1.0 + pre * (1.0 - sig)))
        for k in range(KERNEL):
            gc_ref[k : k + 1, lanes] = jnp.sum(d_pre * pad[5 + k : 5 + k + L, :], axis=0, keepdims=True)
        gc_ref[4:5, lanes] = jnp.sum(d_pre, axis=0, keepdims=True)
        pad[0:L, :] = d_pre
        pad[L : L + 8, :] = jnp.zeros((8, 128), F32)
        d_in = cw_ref[3:4, lanes] * d_pre
        for k in range(KERNEL - 1):
            d_in = d_in + cw_ref[k : k + 1, lanes] * pad[3 - k : 3 - k + L, :]
        proj_ref[:, pl.ds(proj_at, 128)] = d_in.astype(BF)
        return carry

    lax.fori_loop(0, (G + 2 * STATE) // 128, conv_back, 0)


def column(row):
    return jnp.broadcast_to(row, (128, 128)).T


def rows_loop(rows, body):
    def step(r, carry):
        body(pl.ds(pl.multiple_of(r * TILE, TILE), TILE))
        return carry

    lax.fori_loop(0, rows // TILE, step, 0)


def total_of(n, part_ref, got, at):
    total = part_ref[lax.axis_index(SEQ), at, :].astype(F32)
    for k in range(n - 1):
        total = total + got[k, at, :].astype(F32)
    return total


class Group:
    def __init__(self, n_seq, n_wt):
        self.n_seq = n_seq
        self.heads = HEADS // n_seq
        self.runs = n_wt if HEADS % (n_seq * n_wt) == 0 else 1
        self.run_heads = self.heads // self.runs
        self.chans = self.heads * HEAD_DIM
        self.G = -(-self.chans // 128) * 128
        self.CX = self.G + 2 * STATE
        self.NC = 2 * self.G + 2 * STATE + 128
        self.rest = self.G + 2 * STATE + 64
        self.half = (self.G + self.rest) // 2


def head_of(g, here, local_head):
    stride = HEADS // g.runs
    run = local_head // g.run_heads
    return run * stride + here * g.run_heads + (local_head - run * g.run_heads)


def one_hot(found):
    return jnp.where(found, 1.0, 0.0)


def step_select(g, here):
    from_ids = lax.broadcasted_iota(jnp.int32, (128, 128), 0)
    to_ids = lax.broadcasted_iota(jnp.int32, (128, 128), 1)
    return one_hot((from_ids == head_of(g, here, to_ids)) & (to_ids < g.heads))


OUT, GATE, REST = KINDS = range(3)


class Wire:
    def __init__(self, send_sems, recv_sems):
        self.send_sems, self.recv_sems, self.used = send_sems, recv_sems, 0

    def put(self, src, dst, axis, peer):
        copy = pltpu.make_async_remote_copy(
            src, dst, self.send_sems.at[self.used], self.recv_sems.at[self.used],
            device_id={axis: peer}, device_id_type=MESH,
        )
        copy.start()
        self.used += 1
        return copy


class Mover:
    def __init__(self, sems):
        self.sems, self.used = sems, 0

    def put(self, src, dst):
        copy = pltpu.make_async_copy(src, dst, self.sems.at[self.used])
        copy.start()
        self.used += 1
        return copy


def meet_all(axes):
    barrier = pltpu.get_barrier_semaphore()
    count = 0
    for axis, n in axes:
        me = lax.axis_index(axis)
        for k in range(1, n):
            pl.semaphore_signal(
                barrier, inc=1, device_id={axis: lax.rem(me + k, n)}, device_id_type=MESH
            )
        count += n - 1
    pl.semaphore_wait(barrier, count)


def column_tiles(first, last, body):
    whole = (last - first) // 256

    def step(t, carry):
        body(pl.ds(pl.multiple_of(first + t * 256, 128), 256))
        return carry

    lax.fori_loop(0, whole, step, 0)
    if first + whole * 256 < last:
        body(slice(first + whole * 256, last))


class ForwardOuts(NamedTuple):
    sec: Any
    pout: Any
    stat0: Any
    h1: Any
    gb_o: Any
    stats: Any
    packs_o: Any
    wf_o: Any
    of_o: Any
    n_o: Any
    proj_o: Any
    mixed_o: Any
    yp_o: Any
    st_o: Any


class ForwardRefs(NamedTuple):
    tokens: Any
    cotangent: Any
    pack: Any
    w_src: Any
    o_src: Any
    sec: Any
    pout: Any
    stat0: Any
    h1: Any
    gb_o: Any
    stats: Any
    packs_o: Any
    wf_o: Any
    of_o: Any
    n_o: Any
    proj_o: Any
    mixed_o: Any
    yp_o: Any
    st_o: Any
    h0: Any
    cot: Any
    packs: Any
    wf: Any
    of: Any
    normed: Any
    proj: Any
    mixed: Any
    yp: Any
    st: Any
    pad: Any
    xc: Any
    dts: Any
    state: Any
    vg: Any
    ssq: Any
    part: Any
    got: Any
    got_stat: Any
    hbuf: Any
    own_stat: Any
    cols: Any
    mdots: Any
    sel: Any
    ss: Any
    rs: Any
    ls: Any


def forward_kernel(g, n, w, rows, *refs):
    r = ForwardRefs(*refs)
    G, NC = g.G, g.NC
    core, here, shard = lax.axis_index(SECTION), lax.axis_index(SEQ), lax.axis_index(WT)
    sibling = 1 - core
    wire, mover = Wire(r.ss, r.rs), Mover(r.ls)
    wf, of, packs = r.wf, r.of, r.packs
    sends, saves = [], []

    def aligned(at, size):
        return pl.ds(pl.multiple_of(at, 16), size)

    def put(src, dst, axis, peer):
        copy = wire.put(src, dst, axis, peer)
        sends.append(copy)
        return copy

    for layer in range(2):
        for first, last in ((g.chans, G), (G + g.chans, 2 * G), (2 * G + 2 * STATE + HEADS, NC)):
            if first < last:
                wf[layer, first:last, :] = jnp.zeros((last - first, D), BF)
    r.sel[...] = step_select(g, here).astype(BF)
    meet_all(((SEQ, n), (WT, w), (SECTION, 2)))
    o_rows = G // w
    lanes_of = D // w
    mine_o = aligned(shard * o_rows, o_rows)
    piece = here if g.runs == w else shard
    o_own = r.o_src.at[aligned(piece * o_rows, o_rows)]
    mine_lanes = pl.ds(pl.multiple_of(shard * lanes_of, 128), lanes_of)
    width = g.run_heads * HEAD_DIM
    runs = []
    for kind_at, source_at in ((0, 0), (G, INNER)):
        for run in range(g.runs):
            source = source_at + run * (INNER // g.runs) + here * width
            runs.append((source, kind_at + run * width, width))
    runs.append((2 * INNER, 2 * G, 2 * STATE))
    runs.append((2 * INNER + 2 * STATE, 2 * G + 2 * STATE, HEADS))
    siblings = [put(r.pack, packs.at[core], SECTION, sibling)]
    locals_ = [
        mover.put(r.pack, packs.at[core]),
        mover.put(o_own, of.at[core, mine_o]),
        mover.put(r.tokens.at[core, 0], r.h0),
        mover.put(r.cotangent.at[core, 0], r.cot),
    ]
    for source, target, size in runs:
        taken = r.w_src.at[aligned(source, size)]
        siblings.append(put(taken, wf.at[core, target : target + size, mine_lanes], SECTION, sibling))
        locals_.append(mover.put(taken, wf.at[core, target : target + size, mine_lanes]))
    siblings.append(put(o_own, of.at[core, mine_o], SECTION, sibling))

    def part_of(layer, kind, at_shard, at_core):
        if kind == OUT:
            return of.at[layer, aligned(at_shard * o_rows + at_core * (o_rows // 2), o_rows // 2)]
        size = (G if kind == GATE else g.rest) // 2
        first = (0 if kind == GATE else G) + at_core * size
        lanes = pl.ds(pl.multiple_of(at_shard * lanes_of, 128), lanes_of)
        return wf.at[layer, aligned(first, size), lanes]

    def fetch(layer, kind):
        mine = part_of(layer, kind, shard, core)
        return [put(mine, mine, WT, lax.rem(shard + k, w)) for k in range(1, w)]

    def hand_on(copies, layer, kind):
        found = []
        for k, copy in enumerate(copies, 1):
            copy.wait_recv()
            block = part_of(layer, kind, lax.rem(shard + w - k, w), core)
            found.append(put(block, block, SECTION, sibling))
        return found

    def received(copies):
        for copy in copies:
            copy.wait_recv()

    own_rows = aligned(here * rows, rows)

    def gather(layer_ref):
        return [
            wire.put(layer_ref.at[own_rows], layer_ref.at[own_rows], SEQ, lax.rem(here + k, n))
            for k in range(1, n)
        ]

    def save(source, target):
        saves.append(mover.put(source, target))

    def saved():
        while saves:
            saves.pop().wait()

    for copy in locals_:
        copy.wait()
    received(siblings)
    pending = fetch(0, REST)
    gain_at = g.CX + 128 + G

    def norm(at):
        h = r.h0[at, :]
        inv = lax.rsqrt(jnp.mean(h * h, axis=1, keepdims=True) + EPSILON)
        r.normed[pl.ds(pl.multiple_of(here * rows + at.start, TILE), TILE), :] = (
            h * inv * packs[0, 0:1, gain_at:]
        ).astype(BF)

    rows_loop(rows, norm)
    arriving = gather(r.normed)

    for layer in range(2):
        proj, mixed, normed = r.proj, r.mixed, r.normed
        conv = packs.at[layer, :, 0 : g.CX]
        head = packs.at[layer, :, g.CX : g.CX + 128]
        wide = packs.at[layer, :, g.CX + 128 : gain_at]

        def project(lanes):
            proj[:, lanes] = dot(normed[...], wf[layer, lanes, :], 1, 1).astype(BF)

        handed = hand_on(pending, layer, REST)
        pending_gate, pending_o = fetch(layer, GATE), fetch(layer, OUT)
        received(arriving)
        received(handed)
        gathered = arriving
        column_tiles(G, NC, project)
        scan_forward(
            G, proj, conv, head, wide, r.sel, mixed, r.yp, r.st,
            r.pad, r.xc, r.dts, r.state,
        )
        save(mixed, r.mixed_o.at[layer])
        save(r.yp, r.yp_o.at[layer])
        save(r.st, r.st_o.at[layer])
        save(normed, r.n_o.at[layer])
        handed = hand_on(pending_gate, layer, GATE) + hand_on(pending_o, layer, OUT)
        if layer == 0:
            pending = fetch(1, REST)
        received(handed)
        column_tiles(0, G, project)
        save(proj, r.proj_o.at[layer])
        gate_forward(G, proj, wide, mixed, r.vg, r.ssq)

        def out_product(block):
            at = aligned(block * rows, rows)

            def tile(lanes):
                r.part[block, :, lanes] = dot(r.vg[at, :], of[layer, :, lanes], 1, 0).astype(BF)

            column_tiles(0, D, tile)

        saved()
        summing = []
        for k in range(1, n):
            peer = lax.rem(here + k, n)
            out_product(peer)
            summing.append(wire.put(r.part.at[peer], r.got.at[k - 1], SEQ, peer))
            summing.append(wire.put(r.ssq.at[peer], r.got_stat.at[k - 1], SEQ, peer))
        out_product(here)
        for copy in summing:
            copy.wait()
        ssq = r.ssq[here]
        for k in range(n - 1):
            ssq = ssq + r.got_stat[k]
        inv2 = lax.rsqrt(ssq * (1.0 / INNER) + EPSILON)
        r.own_stat[...] = inv2
        r.cols[...] = column(inv2[0:1, :])
        if layer == 0:
            r.stat0[...] = inv2

        def finish(at):
            pout = total_of(n, r.part, r.got, at) * r.cols[at, 0:1]
            whole = pl.ds(pl.multiple_of(here * rows + at.start, TILE), TILE)
            h_in = r.h0[at, :] if layer == 0 else r.hbuf[0, at, :]
            h = h_in + pout
            r.hbuf[layer, at, :] = h
            if layer == 0:
                r.pout[at, :] = pout
                r.h1[at, :] = h
                inv = lax.rsqrt(jnp.mean(h * h, axis=1, keepdims=True) + EPSILON)
                r.normed[whole, :] = (h * inv * packs[1, 0:1, gain_at:]).astype(BF)
            else:
                out = r.cot[at, :].astype(BF)
                dots = jnp.sum(out.astype(F32) * pout, axis=1, keepdims=True)
                r.mdots[at, :] = jnp.broadcast_to(dots * (1.0 / INNER), (TILE, 128))
                r.normed[whole, :] = out

        for copy in gathered:
            copy.wait_send()
        rows_loop(rows, finish)
        if layer == 0:
            arriving = gather(r.normed)
    r.stats[here] = r.own_stat[...]
    r.stats[here, 1:2, :] = r.mdots[...].T[0:1, :]
    arriving = gather(r.normed)
    sends.extend(arriving)
    for k in range(1, n):
        block = r.stats.at[here]
        arriving.append(put(block, block, SEQ, lax.rem(here + k, n)))
    arriving.append(put(r.hbuf.at[1 - core], r.sec.at[core], SECTION, sibling))
    save(r.hbuf.at[core], r.sec.at[core])
    save(packs, r.packs_o)
    save(wf, r.wf_o)
    save(of, r.of_o)
    received(arriving)
    save(r.normed, r.gb_o)
    for copy in sends:
        copy.wait_send()
    saved()


def forward_call(g, n, w, tokens, cotangent, pack, w_src, o_src):
    rows = tokens.shape[2]
    L, G, NC, CX, PK = rows * n, g.G, g.NC, g.CX, pack.shape[1]
    S = jax.ShapeDtypeStruct
    shapes = ForwardOuts(
        sec=S((2, rows, D), F32),
        pout=S((rows, D), F32),
        stat0=S((8, 128), F32),
        h1=S((rows, D), F32),
        gb_o=S((L, D), BF),
        stats=S((n, 8, 128), F32),
        packs_o=S((2, 8, PK), F32),
        wf_o=S((2, NC, D), BF),
        of_o=S((2, G, D), BF),
        n_o=S((2, L, D), BF),
        proj_o=S((2, L, NC), BF),
        mixed_o=S((2, L, G), BF),
        yp_o=S((2, L, G), F32),
        st_o=S((2, L // Q, STATE, G), F32),
    )
    scratch = [
        S((rows, D), F32), S((rows, D), F32), shapes.packs_o, shapes.wf_o, shapes.of_o, S((L, D), BF), S((L, NC), BF), S((L, G), BF),
        S((L, G), F32), S((L // Q, STATE, G), F32), S((8 + L, 128), F32), S((L, CX), F32), S((L, 128), F32), S((STATE, G), F32),
        S((L, G), BF), S((n, 8, 128), F32), S((n, rows, D), BF), S((n - 1, rows, D), BF), S((n - 1, 8, 128), F32),
        S((2, rows, D), F32), S((8, 128), F32), S((rows, 128), F32), S((rows, 128), F32),
        S((128, 128), BF),
    ]
    remote = 4 + 2 * g.runs + 12 * (w - 1) + 8 * (n - 1) + 2
    outs = pl.pallas_call(
        functools.partial(forward_kernel, g, n, w, rows),
        out_shape=list(shapes),
        in_specs=[ANY, ANY, VM, ANY, ANY],
        out_specs=[VM] * 4 + [ANY, VM] + [ANY] * 8,
        scratch_shapes=[pltpu.VMEM(s.shape, s.dtype) for s in scratch]
        + [
            pltpu.SemaphoreType.DMA((remote,)),
            pltpu.SemaphoreType.DMA((remote,)),
            pltpu.SemaphoreType.DMA((22 + 2 * g.runs,)),
        ],
        compiler_params=pltpu.CompilerParams(
            collective_id=0, has_side_effects=True, vmem_limit_bytes=FORWARD_VMEM
        ),
        name="forward",
    )(tokens, cotangent, pack, w_src, o_src)
    return ForwardOuts(*outs)


class BackwardOuts(NamedTuple):
    ig: Any
    gi: Any
    go: Any
    gi_sib: Any
    go_sib: Any
    small: Any
    far: Any


class BackwardRefs(NamedTuple):
    packs_i: Any
    wf_i: Any
    of_i: Any
    n_i: Any
    proj_i: Any
    mixed_i: Any
    yp_i: Any
    st_i: Any
    gb_i: Any
    stats1_i: Any
    stat0_i: Any
    pout_i: Any
    h1_i: Any
    tokens_i: Any
    cotangent_i: Any
    ig: Any
    gi: Any
    go: Any
    gi_sib: Any
    go_sib: Any
    small: Any
    far: Any
    packs: Any
    wf: Any
    of: Any
    n: Any
    proj: Any
    mixed: Any
    yp: Any
    st: Any
    gb: Any
    stats: Any
    pout: Any
    h1: Any
    h0: Any
    cot: Any
    dy: Any
    pad: Any
    xc: Any
    dts: Any
    dstate: Any
    part: Any
    got: Any
    own_stat: Any
    mdots: Any
    grads: Any
    gw: Any
    gout: Any
    sib_w: Any
    sib_o: Any
    z_w: Any
    z_o: Any
    sm: Any
    sm_sib: Any
    sm_z: Any
    sm_own: Any
    sel: Any
    ss: Any
    rs: Any
    ls: Any
    free: Any


def backward_kernel(g, n, w, rows, *refs):
    r = BackwardRefs(*refs)
    G, NC, CX = g.G, g.NC, g.CX
    core, here, shard = lax.axis_index(SECTION), lax.axis_index(SEQ), lax.axis_index(WT)
    sibling = 1 - core
    wire, mover = Wire(r.ss, r.rs), Mover(r.ls)
    o_half, lanes_of = G // (2 * w), D // w
    gain_at = CX + 128 + G

    def aligned(at, size):
        return pl.ds(pl.multiple_of(at, 16), size)

    def load(layer, *pairs):
        return [mover.put(source.at[layer], target) for source, target in pairs]

    first = load(1, (r.of_i, r.of), (r.proj_i, r.proj), (r.mixed_i, r.mixed))
    first += [mover.put(r.packs_i, r.packs), mover.put(r.gb_i, r.gb), mover.put(r.stats1_i, r.stats)]
    later = load(1, (r.n_i, r.n), (r.yp_i, r.yp), (r.st_i, r.st), (r.wf_i, r.wf))
    later += [mover.put(r.pout_i, r.pout), mover.put(r.h1_i, r.h1), mover.put(r.stat0_i, r.own_stat)]
    later += [mover.put(r.tokens_i.at[core, 0], r.h0), mover.put(r.cotangent_i.at[core, 0], r.cot)]
    meet_all(((SEQ, n), (WT, w), (SECTION, 2)))
    r.sm[...] = jnp.zeros_like(r.sm)
    r.sel[...] = step_select(g, here).astype(BF)
    open_sends, record = [], {}
    arrivals = r.got if r.got.shape[0] == n - 1 else r.far

    def put(src, dst, axis, peer):
        copy = wire.put(src, dst, axis, peer)
        open_sends.append(copy)
        return copy

    def rows_of(kind):
        return ((0, G), (0, G), (G, g.rest))[kind]

    def kept(kind):
        return (slice(0, G // (2 * w)), slice(0, G // 2), slice(G // 2, g.half))[kind]

    def buffers(kind):
        if kind == OUT:
            return r.gout, r.sib_o, r.z_o, r.go, r.go_sib
        return r.gw, r.sib_w, r.z_w, r.gi, r.gi_sib

    def block_of(kind, at_shard, at_core):
        if kind == OUT:
            return aligned((2 * at_shard + at_core) * o_half, o_half), slice(0, D)
        first, size = rows_of(kind)
        return (
            aligned(first + at_core * (size // 2), size // 2),
            pl.ds(pl.multiple_of(at_shard * lanes_of, 128), lanes_of),
        )

    def ready(kind):
        for copy in record.pop(kind, ()):
            copy.wait_send()

    def to_sibling(layer, kind):
        grad, sib, _, _, _ = buffers(kind)
        if layer == 0:
            pl.semaphore_wait(r.free.at[kind], 1)
        if kind == OUT:
            pairs = [
                (grad.at[block_of(kind, q, sibling)], sib.at[aligned(q * o_half, o_half)])
                for q in range(w)
            ]
        else:
            first, size = rows_of(kind)
            rows_there = aligned(first + sibling * (size // 2), size // 2)
            pairs = [(grad.at[rows_there], sib.at[kept(kind)])]
        copies = [wire.put(source, target, SECTION, sibling) for source, target in pairs]
        record[kind] = list(copies)
        return copies

    def to_shards(layer, kind, copies):
        grad, sib, z, _, _ = buffers(kind)
        for copy in copies:
            copy.wait_recv()
        if kind == OUT:
            per = o_half // TILE

            def places(t):
                q = t // per
                return (2 * q + core) * o_half + (t - q * per) * TILE, t * TILE

            steps = w * per
        else:
            first, size = rows_of(kind)
            steps = size // 2 // TILE

            def places(t):
                return first + core * (size // 2) + t * TILE, kept(kind).start + t * TILE

        def add(t, carry):
            mine, theirs = (pl.ds(pl.multiple_of(at, TILE), TILE) for at in places(t))
            grad[mine, :] = (grad[mine, :].astype(F32) + sib[theirs, :].astype(F32)).astype(BF)
            return carry

        lax.fori_loop(0, steps, add, 0)
        if layer == 1:
            pl.semaphore_signal(
                r.free.at[kind], inc=1, device_id={SECTION: sibling}, device_id_type=MESH
            )
        found = []
        for k in range(1, w):
            peer = lax.rem(shard + k, w)
            source = grad.at[block_of(kind, peer, core)]
            found.append(wire.put(source, z.at[layer, k - 1, kept(kind)], WT, peer))
        record[kind] += found
        return found

    def to_plane(layer, kind, copies):
        grad, _, z, result, _ = buffers(kind)
        for copy in copies:
            copy.wait_recv()
        at_rows, at_lanes = block_of(kind, shard, core)
        here_rows = kept(kind)

        def add(at):
            mine = pl.ds(pl.multiple_of(at_rows.start + at.start, TILE), TILE)
            there = pl.ds(pl.multiple_of(here_rows.start + at.start, TILE), TILE)
            total = grad[mine, at_lanes].astype(F32)
            for k in range(w - 1):
                total = total + z[layer, k, there, :].astype(F32)
            z[layer, 0, there, :] = total.astype(BF)

        rows_loop(here_rows.stop - here_rows.start, add)
        block, target = z.at[layer, 0, here_rows], result.at[layer, here, here_rows]
        found = [put(block, target, SEQ, lax.rem(here + k, n)) for k in range(1, n)]
        return found, mover.put(block, target)

    def landed(kind, *arrivals):
        _, _, _, result, target = buffers(kind)
        for found, own in arrivals:
            for copy in found:
                copy.wait_recv()
            own.wait()
        return put(result.at[sibling, :, kept(kind)], target.at[:, kept(kind)], SECTION, sibling)

    def done(copies):
        for copy in copies:
            copy.wait()

    arrived = {}
    for layer in (1, 0):
        conv = r.packs.at[layer, :, 0:CX]
        head = r.packs.at[layer, :, CX : CX + 128]
        wide = r.packs.at[layer, :, CX + 128 : gain_at]
        g_conv = r.sm.at[layer, :, 0:CX]
        g_head = r.sm.at[layer, :, CX : CX + 128]
        g_wide = r.sm.at[layer, :, CX + 128 : gain_at]
        g_gain = r.sm.at[layer, :, gain_at : gain_at + D]
        done(first)

        def d_normed(lanes):
            r.xc[:, lanes] = dot(r.gb[...], r.of[lanes, :], 1, 1)

        column_tiles(0, G, d_normed)
        gate_backward(
            G, r.proj, r.mixed, r.xc, r.stats, wide, r.dy, g_wide
        )

        def out_rows(t, carry):
            at = pl.ds(pl.multiple_of(t * 128, 128), 128)
            r.gout[at, :] = dot(r.mixed[:, at], r.gb[...], 0, 0).astype(BF)
            return carry

        def in_rows(first, last):
            def step(t, carry):
                at = pl.ds(pl.multiple_of(t * 128, 128), 128)
                r.gw[at, :] = dot(r.proj[:, at], r.n[...], 0, 0).astype(BF)
                return carry

            lax.fori_loop(first // 128, last // 128, step, 0)

        ready(OUT)
        lax.fori_loop(0, G // 128, out_rows, 0)
        out_sib = to_sibling(layer, OUT)
        done(later)
        ready(GATE)
        in_rows(0, G)
        gate_sib = to_sibling(layer, GATE)
        out_z = to_shards(layer, OUT, out_sib)
        gate_z = to_shards(layer, GATE, gate_sib)
        if layer == 0:
            arrived[1, REST] = to_plane(1, REST, rest_z)
        scan_backward(
            G, r.proj, r.dy, r.yp, r.st, conv, head, wide, r.sel, g_wide, g_conv, g_head,
            r.pad, r.xc, r.dts, r.dstate,
        )
        if layer == 1:
            first = load(0, (r.of_i, r.of), (r.mixed_i, r.mixed))
            later = load(0, (r.yp_i, r.yp), (r.st_i, r.st))

        def in_product(block):
            at = aligned(block * rows, rows)

            def tile(lanes):
                r.part[block, :, lanes] = dot(r.proj[at, :], r.wf[:, lanes], 1, 0).astype(BF)

            column_tiles(0, D, tile)

        summing = []
        for k in range(1, n):
            peer = lax.rem(here + k, n)
            in_product(peer)
            summing.append(wire.put(r.part.at[peer], arrivals.at[k - 1], SEQ, peer))
        in_product(here)
        if layer == 1:
            later += load(0, (r.wf_i, r.wf))
        ready(REST)
        in_rows(G, NC)
        if layer == 1:
            first += load(0, (r.proj_i, r.proj))
            later += load(0, (r.n_i, r.n))
        rest_sib = to_sibling(layer, REST)
        rest_z = to_shards(layer, REST, rest_sib)
        done(summing)
        if arrivals is not r.got:
            done(
                [
                    mover.put(arrivals.at[k - 1], r.part.at[lax.rem(here + k, n)])
                    for k in range(1, n)
                ]
            )

        def finish(at):
            if arrivals is r.got:
                d_in = total_of(n, r.part, r.got, at)
            else:
                d_in = r.part[0, at, :].astype(F32)
                for k in range(1, n):
                    d_in = d_in + r.part[k, at, :].astype(F32)
            h = r.h1[at, :] if layer == 1 else r.h0[at, :]
            above = r.cot[at, :] if layer == 1 else r.grads[1, at, :]
            inv = lax.rsqrt(jnp.mean(h * h, axis=1, keepdims=True) + EPSILON)
            normed = h * inv
            g_gain[0:1, :] += jnp.sum(d_in * normed, axis=0, keepdims=True)
            d_s = d_in * r.packs[layer, 0:1, gain_at:]
            d_h = above + inv * (d_s - normed * jnp.mean(d_s * normed, axis=1, keepdims=True))
            r.grads[layer, at, :] = d_h
            if layer == 1:
                out = d_h.astype(BF)
                whole = pl.ds(pl.multiple_of(here * rows + at.start, TILE), TILE)
                r.gb[whole, :] = out
                dots = jnp.sum(out.astype(F32) * r.pout[at, :], axis=1, keepdims=True)
                r.mdots[at, :] = jnp.broadcast_to(dots * (1.0 / INNER), (TILE, 128))

        rows_loop(rows, finish)
        if layer == 1:
            r.stats[here] = r.own_stat[...]
            r.stats[here, 1:2, :] = r.mdots[...].T[0:1, :]
            own = aligned(here * rows, rows)
            gathering = []
            for k in range(1, n):
                peer = lax.rem(here + k, n)
                gathering.append(put(r.gb.at[own], r.gb.at[own], SEQ, peer))
                gathering.append(put(r.stats.at[here], r.stats.at[here], SEQ, peer))
            arrived[1, OUT] = to_plane(1, OUT, out_z)
            arrived[1, GATE] = to_plane(1, GATE, gate_z)
            for copy in gathering:
                copy.wait_recv()
    ends = [put(r.grads.at[sibling], r.ig.at[core], SECTION, sibling)]
    ends.append(put(r.sm.at[sibling], r.sm_sib, SECTION, sibling))
    local_grad = mover.put(r.grads.at[core], r.ig.at[core])
    arrived[0, OUT] = to_plane(0, OUT, out_z)
    arrived[0, GATE] = to_plane(0, GATE, gate_z)
    ends[1].wait_recv()
    r.sm_own[...] = r.sm[core] + r.sm_sib[...]
    sums = [
        put(r.sm_own, r.sm_z.at[k - 1], WT, lax.rem(shard + k, w)) for k in range(1, w)
    ]
    for copy in sums:
        copy.wait_recv()
    total = r.sm_own[...]
    for k in range(w - 1):
        total = total + r.sm_z[k]
    r.small[here] = total
    sums = [
        put(r.small.at[here], r.small.at[here], SEQ, lax.rem(here + k, n))
        for k in range(1, n)
    ]
    ends.append(landed(OUT, arrived[1, OUT], arrived[0, OUT]))
    ends.append(landed(GATE, arrived[1, GATE], arrived[0, GATE]))
    arrived[0, REST] = to_plane(0, REST, rest_z)
    ends.append(landed(REST, arrived[1, REST], arrived[0, REST]))
    ends[0].wait_recv()
    for copy in ends[2:] + sums:
        copy.wait_recv()
    local_grad.wait()
    for kind in KINDS:
        ready(kind)
    for copy in open_sends:
        copy.wait_send()


def backward_call(g, n, w, fwd, tokens, cotangent):
    rows = tokens.shape[2]
    L, G, NC, CX = rows * n, g.G, g.NC, g.CX
    PK = CX + 128 + G + D
    S = jax.ShapeDtypeStruct
    o_half, lanes_of = G // (2 * w), D // w
    spill = n > 8
    outs = BackwardOuts(
        ig=S((2, rows, D), F32),
        gi=S((2, n, g.half, lanes_of), BF),
        go=S((2, n, o_half, D), BF),
        gi_sib=S((n, g.half, lanes_of), BF),
        go_sib=S((n, o_half, D), BF),
        small=S((n, 8, PK), F32),
        far=S((n - 1, rows, D) if spill else (8, 128), BF),
    )
    scratch = [
        S((2, 8, PK), F32), S((NC, D), BF), S((G, D), BF), S((L, D), BF), S((L, NC), BF), S((L, G), BF),
        S((L, G), F32), S((L // Q, STATE, G), F32), S((L, D), BF), S((n, 8, 128), F32), S((rows, D), F32),
        S((rows, D), F32), S((rows, D), F32), S((rows, D), F32),
        S((L, G), BF), S((8 + L, 128), F32), S((L, CX), F32), S((L, 128), F32), S((STATE, G), F32),
        S((n, rows, D), BF), S((1 if spill else n - 1, rows, D), BF), S((8, 128), F32), S((rows, 128), F32), S((2, rows, D), F32),
        S((NC, D), BF), S((G, D), BF), S((g.half, D), BF), S((G // 2, D), BF),
        S((2, w - 1, g.half, lanes_of), BF),
        S((2, w - 1, o_half, D), BF), S((2, 8, PK), F32), S((8, PK), F32), S((w - 1, 8, PK), F32), S((8, PK), F32),
        S((128, 128), BF),
    ]
    remote = 2 * (3 * (w + w - 1 + n - 1) + n - 1) + 2 * (n - 1) + 5 + (w - 1) + (n - 1)
    args = [
        fwd.packs_o, fwd.wf_o, fwd.of_o, fwd.n_o, fwd.proj_o, fwd.mixed_o, fwd.yp_o, fwd.st_o,
        fwd.gb_o, fwd.stats, fwd.stat0, fwd.pout, fwd.h1, tokens, cotangent,
    ]
    results = pl.pallas_call(
        functools.partial(backward_kernel, g, n, w, rows),
        out_shape=list(outs),
        in_specs=[ANY] * len(args),
        out_specs=[VM, ANY, ANY, ANY, ANY, VM, ANY],
        scratch_shapes=[pltpu.VMEM(s.shape, s.dtype) for s in scratch]
        + [
            pltpu.SemaphoreType.DMA((remote,)),
            pltpu.SemaphoreType.DMA((remote,)),
            pltpu.SemaphoreType.DMA((36 + 2 * n,)),
            pltpu.SemaphoreType.REGULAR((3,)),
        ],
        compiler_params=pltpu.CompilerParams(
            collective_id=1, has_side_effects=True, vmem_limit_bytes=BACKWARD_VMEM
        ),
        name="backward",
    )(*args)
    return BackwardOuts(*results)


def pack_kernel(g, win, conv_ref, bias_ref, dtb_ref, a_ref, skip_ref, gate_ref, norm_ref, pack_ref):
    here = lax.axis_index(SEQ)
    G, width = g.G, g.run_heads * HEAD_DIM
    start = here * width
    base = pl.multiple_of(start // 128 * 128, 128)
    from_ids = lax.broadcasted_iota(jnp.int32, (win, G), 0)
    to_ids = lax.broadcasted_iota(jnp.int32, (win, G), 1)
    exact = lax.Precision.HIGHEST

    def take(ref, rows):
        total = jnp.zeros((rows, G), F32)
        for run in range(g.runs):
            window = ref[0:rows, pl.ds(pl.multiple_of(base + run * (INNER // g.runs), 128), win)]
            inside = (to_ids >= run * width) & (to_ids < (run + 1) * width)
            pick = one_hot(inside & (from_ids == to_ids - run * width + (start - base)))
            total = total + dot(window, pick, 1, 0, exact)
        return total

    head_from = lax.broadcasted_iota(jnp.int32, (HEADS, 128), 0)
    head_to = lax.broadcasted_iota(jnp.int32, (HEADS, 128), 1)
    head_pick = one_hot((head_from == head_of(g, here, head_to)) & (head_to < g.heads))
    wide_from = lax.broadcasted_iota(jnp.int32, (HEADS, G), 0)
    wide_to = lax.broadcasted_iota(jnp.int32, (HEADS, G), 1)
    wide_pick = (wide_from == head_of(g, here, wide_to // HEAD_DIM)) & (wide_to < g.chans)
    head_at, wide_at, gain_at = g.CX, g.CX + 128, g.CX + 128 + G
    pack_ref[...] = jnp.zeros_like(pack_ref)
    pack_ref[0:KERNEL, 0:G] = take(conv_ref, KERNEL)
    pack_ref[4:5, 0:G] = take(bias_ref, 1)
    pack_ref[0:KERNEL, G:head_at] = conv_ref[:, INNER:]
    pack_ref[4:5, G:head_at] = bias_ref[:, INNER:]
    pack_ref[0:1, head_at:wide_at] = dot(dtb_ref[...], head_pick, 1, 0, exact)
    pack_ref[1:2, head_at:wide_at] = dot(-jnp.exp(a_ref[...]), head_pick, 1, 0, exact)
    pack_ref[0:1, wide_at:gain_at] = take(gate_ref, 1)
    pack_ref[1:2, wide_at:gain_at] = dot(skip_ref[...], one_hot(wide_pick), 1, 0, exact)
    pack_ref[0:1, gain_at:] = norm_ref[...]


def pack_call(g, *small):
    win = -(-(g.run_heads * HEAD_DIM + 64) // 128) * 128
    return pl.pallas_call(
        functools.partial(pack_kernel, g, win),
        out_shape=jax.ShapeDtypeStruct((8, g.CX + 128 + g.G + D), F32),
        in_specs=[VM] * len(small),
        out_specs=VM,
        compiler_params=pltpu.CompilerParams(vmem_limit_bytes=SMALL_VMEM),
        name="pack",
    )(*small)


def halves_of_heads(g, ref_of, column_at, head):
    parts = []
    for h in (head, head + 1):
        stride = HEADS // g.runs
        group = h % stride // g.run_heads
        local_head = h // stride * g.run_heads + h % g.run_heads
        value = ref_of(group, slice(column_at + local_head // 2 * 128, column_at + local_head // 2 * 128 + 128))
        parts.append(value if local_head % 2 == h % 2 else pltpu.roll(value, HEAD_DIM, 1))
    lanes = lax.broadcasted_iota(jnp.int32, parts[0].shape, 1)
    return jnp.where(lanes < HEAD_DIM, parts[0], parts[1])


def layout_kernel(g, own_ref, sib_ref, small_ref, g_in_ref, norm_ref, conv_ref, bias_ref, dtb_ref, a_ref, skip_ref, gate_ref):
    n, G = g.n_seq, g.G
    first_core = lax.axis_index(SECTION) == 0

    def copy(groups, kind_at, half_at, half_rows, source, target, size):
        done = 0
        while done < size:
            half, offset = divmod(source + done, half_rows)
            count = min(size - done, half_rows - offset)
            at = slice(half_at + offset, half_at + offset + count)
            total = None
            for group in groups:
                own, sib = own_ref[0, group, at, :], sib_ref[group, at, :]
                value = (jnp.where(first_core, own, sib) if half == 0 else jnp.where(first_core, sib, own)).astype(F32)
                total = value if total is None else total + value
            g_in_ref[target + done : target + done + count, :] = total
            done += count

    width = g.run_heads * HEAD_DIM
    rest = (G, G // 2, g.rest // 2)
    everyone = range(n)
    for run in range(g.runs):
        for group in range(n):
            target = run * (INNER // g.runs) + group * width
            copy([group], 0, 0, G // 2, run * width, target, width)
            copy([group], *rest, run * width, INNER + target, width)
    copy(everyone, *rest, G, 2 * INNER, 2 * STATE)
    copy(everyone, *rest, G + 2 * STATE, 2 * INNER + 2 * STATE, HEADS)

    @pl.when(pl.program_id(0) == 0)
    def _():
        from_ids = lax.broadcasted_iota(jnp.int32, (128, HEADS), 0)
        to_ids = lax.broadcasted_iota(jnp.int32, (128, HEADS), 1)
        picks = [one_hot((to_ids == head_of(g, group, from_ids)) & (from_ids < g.heads)) for group in range(n)]
        exact = lax.Precision.HIGHEST
        head_at, wide_at, gain_at = g.CX, g.CX + 128, g.CX + 128 + G

        def small(group, columns):
            return small_ref[group, :, columns]

        for head in range(0, HEADS, 2):
            at = slice(head * HEAD_DIM, head * HEAD_DIM + 128)
            conv = halves_of_heads(g, small, 0, head)
            conv_ref[:, at] = conv[0:KERNEL]
            bias_ref[:, at] = conv[KERNEL : KERNEL + 1]
            gate_ref[:, at] = halves_of_heads(g, small, wide_at, head)[0:1]
        conv = small(0, slice(G, head_at))
        norm = small(0, slice(gain_at, gain_at + D))
        for group in range(1, n):
            conv = conv + small(group, slice(G, head_at))
            norm = norm + small(group, slice(gain_at, gain_at + D))
        conv_ref[:, INNER:] = conv[0:KERNEL]
        bias_ref[:, INNER:] = conv[KERNEL : KERNEL + 1]
        norm_ref[...] = norm[0:1]
        heads = jnp.zeros((8, HEADS), F32)
        skips = jnp.zeros((8, HEADS), F32)
        wide_from = lax.broadcasted_iota(jnp.int32, (G, HEADS), 0)
        wide_to = lax.broadcasted_iota(jnp.int32, (G, HEADS), 1)
        for group in range(n):
            heads = heads + dot(small(group, slice(head_at, wide_at)), picks[group], 1, 0, exact)
            pick = (wide_to == head_of(g, group, wide_from // HEAD_DIM)) & (wide_from < g.chans)
            skips = skips + dot(small(group, slice(wide_at, gain_at)), one_hot(pick), 1, 0, exact)
        dtb_ref[...] = heads[0:1]
        a_ref[...] = heads[1:2]
        skip_ref[...] = skips[1:2]


def layout_call(g, core, gi, gi_sib, small):
    _, n, half, lanes = gi.shape
    PK = small.shape[2]
    columns = 2 * INNER + 2 * STATE + HEADS
    S = jax.ShapeDtypeStruct
    shapes = (
        S((columns, lanes), F32), S((1, D), F32), S((KERNEL, CONV), F32), S((1, CONV), F32), S((1, HEADS), F32),
        S((1, HEADS), F32), S((1, HEADS), F32), S((1, INNER), F32),
    )
    return pl.pallas_call(
        lambda core_ref, *refs: layout_kernel(g, *refs),
        grid_spec=pltpu.PrefetchScalarGridSpec(
            num_scalar_prefetch=1,
            grid=(lanes // 128,),
            in_specs=[
                pl.BlockSpec((1, n, half, 128), lambda t, c: (c[0], 0, 0, t)),
                pl.BlockSpec((n, half, 128), lambda t, c: (0, 0, t)),
                pl.BlockSpec((n, 8, PK), lambda t, c: (0, 0, 0)),
            ],
            out_specs=[pl.BlockSpec((columns, 128), lambda t, c: (0, t))]
            + [pl.BlockSpec(s.shape, lambda t, c: (0, 0)) for s in shapes[1:]],
        ),
        out_shape=shapes,
        compiler_params=pltpu.CompilerParams(vmem_limit_bytes=SMALL_VMEM),
        name="layout",
    )(core, gi, gi_sib, small)


def widen_kernel(core_ref, own_ref, sib_ref, out_ref):
    mine = pl.program_id(0) == core_ref[0]
    out_ref[...] = jnp.where(mine, own_ref[...], sib_ref[...][None]).astype(F32).reshape(out_ref.shape)


def widen_call(core, go, go_sib):
    _, n, size, columns = go.shape
    return pl.pallas_call(
        widen_kernel,
        grid_spec=pltpu.PrefetchScalarGridSpec(
            num_scalar_prefetch=1,
            grid=(2, n),
            in_specs=[
                pl.BlockSpec((1, 1, size, columns), lambda h, t, c: (c[0], t, 0, 0)),
                pl.BlockSpec((1, size, columns), lambda h, t, c: (t, 0, 0)),
            ],
            out_specs=pl.BlockSpec((1, 1, size, columns), lambda h, t, c: (t, h, 0, 0)),
        ),
        out_shape=jax.ShapeDtypeStruct((n, 2, size, columns), F32),
        compiler_params=pltpu.CompilerParams(vmem_limit_bytes=SMALL_VMEM),
        name="widen",
    )(core, go, go_sib)


def local(
    tokens, cotangent, norm_gain, w_in, conv_w, conv_b, dt_bias, a_log, skip_d, gate_gain, w_out
):
    n_seq, n_wt = lax.axis_size(SEQ), lax.axis_size(WT)
    here = lax.axis_index(SEQ)
    group = Group(n_seq, n_wt)
    core = lax.axis_index(SECTION).reshape(1)
    G = group.G

    pack = pack_call(
        group, conv_w[0], conv_b, dt_bias, a_log, skip_d, gate_gain, norm_gain
    )
    w_src = jnp.swapaxes(w_in[0], 0, 1)
    if group.runs == n_wt:
        o_src = w_out[0]
    else:
        o_src = lax.all_gather(w_out[0], WT, axis=0, tiled=True)
        o_src = lax.dynamic_slice_in_dim(o_src, here * group.chans, group.chans, 0)
        o_src = jnp.pad(o_src, ((0, G - group.chans), (0, 0)))
    fwd = forward_call(group, n_seq, n_wt, tokens, cotangent, pack, w_src, o_src)
    bwd = backward_call(group, n_seq, n_wt, fwd, tokens, cotangent)
    g_in, g_norm, g_conv, g_bias, g_dtb, g_a, g_skip, g_gate = layout_call(
        group, core, bwd.gi, bwd.gi_sib, bwd.small
    )
    g_out = widen_call(core, bwd.go, bwd.go_sib)
    if group.runs == n_wt:
        g_out = g_out.reshape(INNER // n_wt, D)
    else:
        g_out = g_out.astype(BF).reshape(n_seq, G // n_wt, D)
        g_out = lax.all_gather(g_out, WT, axis=1, tiled=True)[:, : group.chans].reshape(INNER, D)
        mine = INNER // n_wt
        g_out = lax.dynamic_slice_in_dim(g_out, lax.axis_index(WT) * mine, mine, 0).astype(F32)
    return (
        fwd.sec[None, :, None],
        bwd.ig[None, :, None],
        g_norm,
        jnp.swapaxes(g_in, 0, 1)[None],
        g_conv[None],
        g_bias,
        g_dtb,
        g_a,
        g_skip,
        g_gate,
        g_out[None],
    )


def solution(mesh):
    placed = (
        P(None, WT, SEQ, None),
        P(None, WT, SEQ, None),
        P(SECTION, None),
        P(SECTION, WT, None),
        P(SECTION, None, None),
        P(SECTION, None),
        P(SECTION, None),
        P(SECTION, None),
        P(SECTION, None),
        P(SECTION, None),
        P(SECTION, WT, None),
    )
    return jax.shard_map(
        local,
        mesh=mesh,
        in_specs=placed,
        out_specs=(
            P(SECTION, None, WT, SEQ, None),
            P(SECTION, None, WT, SEQ, None),
            P(SECTION, None),
            P(SECTION, WT, None),
            P(SECTION, None, None),
            P(SECTION, None),
            P(SECTION, None),
            P(SECTION, None),
            P(SECTION, None),
            P(SECTION, None),
            P(SECTION, WT, None),
        ),
        check_vma=False,
    )
```

time: 2130 us -> 494 us (0.23)
  waiting for transfers between devices: 1240 us -> 0 us
  Pallas kernels: 0 us -> 478 us
  matrix products: 303 us -> 0 us
  local copies, waits for them, and re-layouts: 256 us -> 14.1 us
  other arithmetic: 174 us -> 0 us
  starting transfers between devices: 70.7 us -> 0 us
  blocking collectives: 52.6 us -> 0 us
    pallas_call x0 -> x5, Pallas kernels: none -> 478 us  [the longest x1 234 us: forward_call(): pl.pallas_call(functools.partial(forward_kernel, g, n, w, rows), out_shap...]
    all_gather x2 -> x0, waiting for transfers between devices: 406 us -> none  [the longest x1 333 us: local(): lax.all_gather(w_in, 'wt', axis=1, tiled=True)]
    unnamed x13 -> x0, waiting for transfers between devices: 393 us -> none
    dot_general x53 -> x0, matrix products: 286 us -> none  [the longest x9 60.4 us: mixer(): jnp.einsum('ctsh,cshp->cthp', mix_weight, x_blocks, precision=EXACT_DOT)]
    psum x2 -> x0, waiting for transfers between devices: 238 us -> none  [the longest x1 133 us: local(): lax.psum(acc_in.astype(jnp.bfloat16), 'seq').astype(jnp.float32)]
    reduce_scatter x1 -> x0, waiting for transfers between devices: 159 us -> none  [local(): lax.psum_scatter(whole_out.astype(jnp.bfloat16), 'wt', scatter_dimension=...]
    all_to_all x16 -> x0, starting transfers between devices: 61.9 us -> none  [the longest x3 13.3 us: local(): lax.all_to_all(projected[:, INNER:2 * INNER], 'seq', split_axis=1, concat...]
    reduce_sum x33 -> x0, other arithmetic: 49.4 us -> none  [the longest x6 14.1 us: conv_silu(): conv_sum = conv_sum + kernel_w[k][None, :] * padded[k:k + length]]
  transfers between devices with their start and end apart: 29 -> 0, of which waited for: 18 -> 0; matrix products, arithmetic and copies ran while one was open for 12% -> 0% of each run, Pallas kernels for 0% -> 0%
where the time goes in v3:
time: 494 us; the launch traced here: 493 us
  Pallas kernels  478 us (97%)
  local copies, waits for them, and re-layouts  14.1 us (3%)
    pallas_call x1, Pallas kernels, forward_call(): pl.pallas_call(functools.partial(forward_kernel, g, n, w, rows), out_shap...  234 us
    pallas_call x1, Pallas kernels, backward_call(): pl.pallas_call(functools.partial(backward_kernel, g, n, w, rows), out_sha...  232 us
    unnamed x32, local copies, waits for them, and re-layouts  14.1 us

profile of v3, /device:TPU:8, one launch (start us, length us, event | category | flops | bytes accessed | tf_op | source)
XLA Modules:
  0.0 493.0 jit_solution(9092445813689876928)
XLA Ops:
  0.6 0.0 copy-start.6
  0.7 0.8 copy-done.6
  1.5 0.7 copy-done.7
  2.2 0.7 copy-done.8
  2.9 0.7 copy-done.9
  3.6 0.7 copy-done.10
  4.2 0.7 copy-done.11
  4.9 0.7 copy-done.12
  5.5 2.1 pack.1.refs_2_
  7.7 0.7 copy-done.4
  8.3 234.1 %forward.1 = (f32[2,128,1536]{2,1,0:T(8,128)}, f32[128,1536]{1,0:T(8,128)}, f32[8,128]{1,0:T(8,128)}, f32[128,1536]{1,0:T(8,128)}, bf16[512,1536]{1,0:T(8,128)(2...) custom-call(f32[2,1,128,1536]{3,2,1,0:T(8,128)} %refs_13_.1, ...), custom_call_target="tpu_custom_call" | custom-call | tf_op jit(solution)/shard_map/forward/pallas_call | solution.py:684
  242.5 232.3 %backward.1 = (f32[2,128,1536]{2,1,0:T(8,128)}, bf16[2,4,928,384]{3,2,1,0:T(8,128)(2,1)}, bf16[2,4,96,1536]{3,2,1,0:T(8,128)(2,1)}, bf16[4,928,384]{2,1,0:T(8,12...) custom-call(f32[2,8,3456]{2,1,0:T(8,128)} %get-tuple-element.40.refs_0_, ...), custom_call_target="tpu_custom_call" | custom-call | tf_op jit(solution)/shard_map/backward/pallas_call | solution.py:1103
  474.7 0.0 copy-start
  474.8 2.6 copy-done
  477.4 1.8 copy-done.1
  479.2 1.0 copy-done.5
  480.2 6.0 %layout.1 = (f32[6448,384]{1,0:T(8,128)}, f32[1,1536]{1,0:T(1,128)}, f32[4,3328]{1,0:T(4,128)}, f32[1,3328]{1,0:T(1,128)}, f32[1,48]{1,0:T(1,128)}, /*index=5*/f...) custom-call(s32[1]{0:T(128)} %bitcast.8.core_ref, bf16[2,4,928,384]{3,2,1,0:T(8,128)(2,1)S(1)} %copy-done, ...), custom_call_target="tpu_custom_call" | custom-call | tf_op jit(solution)/shard_map/layout/pallas_call | solution.py:1260
  486.2 0.0 copy-done.2
  486.2 0.0 copy-done.3
  486.2 3.7 widen.1
  489.9 0.0 copy-done.13
  489.9 1.1 copy.26
  491.0 0.8 copy-done.14
  491.8 1.1 copy.27
  (13 shorter events, 0.0 us)
Async XLA Ops:
  0.6 0.8 copy-start.6
  1.5 0.7 copy-start.7
  2.2 0.7 copy-start.8
  2.9 0.7 copy-start.9
  3.6 0.7 copy-start.10
  4.2 0.7 copy-start.11
  4.9 0.7 copy-start.12
  7.7 0.7 copy-start.4
  474.7 2.6 copy-start
  477.4 1.8 copy-start.1
  479.2 1.0 copy-start.5
  480.2 6.0 %copy-start.2 = (bf16[2,4,96,1536]{3,2,1,0:T(8,128)(2,1)S(1)}, bf16[2,4,96,1536]{3,2,1,0:T(8,128)(2,1)}, u32[]{:S(2)}) copy-start(bf16[2,4,96,1536]{3,2,1,0:T(8,128)(2,1)} %get-tuple-element.65.own_ref) | copy-start | bytes 7077892
  480.2 6.0 %copy-start.3 = (bf16[4,96,1536]{2,1,0:T(8,128)(2,1)S(1)}, bf16[4,96,1536]{2,1,0:T(8,128)(2,1)}, u32[]{:S(2)}) copy-start(bf16[4,96,1536]{2,1,0:T(8,128)(2,1)} %get-tuple-element.66.sib_ref) | copy-start | bytes 3538948
  486.2 3.7 copy-start.13
  489.9 2.0 copy-start.14

commit v4 on v3

--- a/solution.py
+++ b/solution.py
@@ -337,14 +337,33 @@
     def __init__(self, send_sems, recv_sems):
         self.send_sems, self.recv_sems, self.used = send_sems, recv_sems, 0
 
-    def put(self, src, dst, axis, peer):
-        copy = pltpu.make_async_remote_copy(
-            src, dst, self.send_sems.at[self.used], self.recv_sems.at[self.used],
+    def reserve(self):
+        self.used += 1
+        return self.used - 1
+
+    def make(self, src, dst, axis, peer, at_send, at_recv):
+        return pltpu.make_async_remote_copy(
+            src, dst, self.send_sems.at[at_send], self.recv_sems.at[at_recv],
             device_id={axis: peer}, device_id_type=MESH,
         )
+
+    def put(self, src, dst, axis, peer):
+        at = self.reserve()
+        copy = self.make(src, dst, axis, peer, at, at)
         copy.start()
-        self.used += 1
         return copy
+
+
+class Maybe:
+    def __init__(self, condition, copy):
+        self.condition, self.copy = condition, copy
+
+    def start(self):
+        pl.when(self.condition)(self.copy.start)
+        return self
+
+    def wait_send(self):
+        pl.when(self.condition)(self.copy.wait_send)
 
 
 class Mover:
@@ -507,15 +526,38 @@
         lanes = pl.ds(pl.multiple_of(at_shard * lanes_of, 128), lanes_of)
         return wf.at[layer, aligned(first, size), lanes]
 
+    line = w == 4
+
     def fetch(layer, kind):
         mine = part_of(layer, kind, shard, core)
-        return [put(mine, mine, WT, lax.rem(shard + k, w)) for k in range(1, w)]
-
-    def hand_on(copies, layer, kind):
+        at = [wire.reserve() for _ in range(w)]
+        copies = [
+            wire.make(mine, mine, WT, lax.rem(shard + k, w), at[k], at[k]) for k in range(1, w)
+        ]
+        if line:
+            copies[1].start()
+            sends.append(copies[1])
+            sends.append(Maybe(shard != w - 1, copies[0]).start())
+            sends.append(Maybe(shard != 0, copies[2]).start())
+        else:
+            for copy in copies:
+                copy.start()
+            sends.extend(copies)
+        return copies, at
+
+    def hand_on(fetched, layer, kind, then=None):
+        copies, at = fetched
         found = []
-        for k, copy in enumerate(copies, 1):
-            copy.wait_recv()
+        for k in (2, 1, 3) if line else range(1, w):
+            copies[k - 1].wait_recv()
             block = part_of(layer, kind, lax.rem(shard + w - k, w), core)
+            if line and k == 2:
+                up = wire.make(block, block, WT, lax.rem(shard + 1, w), at[0], at[3])
+                down = wire.make(block, block, WT, lax.rem(shard + w - 1, w), at[0], at[1])
+                sends.append(Maybe(shard == 2, up).start())
+                sends.append(Maybe(shard == 1, down).start())
+            if k == 2 and then is not None:
+                then()
             found.append(put(block, block, SECTION, sibling))
         return found
 
@@ -563,8 +605,15 @@
         def project(lanes):
             proj[:, lanes] = dot(normed[...], wf[layer, lanes, :], 1, 1).astype(BF)
 
-        handed = hand_on(pending, layer, REST)
-        pending_gate, pending_o = fetch(layer, GATE), fetch(layer, OUT)
+        coming = []
+
+        def fetch_others():
+            coming.extend([fetch(layer, GATE), fetch(layer, OUT)])
+
+        def fetch_above():
+            coming.append(fetch(1, REST))
+
+        handed = hand_on(pending, layer, REST, fetch_others)
         received(arriving)
         received(handed)
         gathered = arriving
@@ -577,9 +626,9 @@
         save(r.yp, r.yp_o.at[layer])
         save(r.st, r.st_o.at[layer])
         save(normed, r.n_o.at[layer])
-        handed = hand_on(pending_gate, layer, GATE) + hand_on(pending_o, layer, OUT)
-        if layer == 0:
-            pending = fetch(1, REST)
+        handed = hand_on(coming[0], layer, GATE)
+        handed += hand_on(coming[1], layer, OUT, fetch_above if layer == 0 else None)
+        pending = coming[-1]
         received(handed)
         column_tiles(0, G, project)
         save(proj, r.proj_o.at[layer])
@@ -680,7 +729,7 @@
         S((2, rows, D), F32), S((8, 128), F32), S((rows, 128), F32), S((rows, 128), F32),
         S((128, 128), BF),
     ]
-    remote = 4 + 2 * g.runs + 12 * (w - 1) + 8 * (n - 1) + 2
+    remote = 4 + 2 * g.runs + 6 * w + 6 * (w - 1) + 8 * (n - 1) + 2
     outs = pl.pallas_call(
         functools.partial(forward_kernel, g, n, w, rows),
         out_shape=list(shapes),
@@ -763,6 +812,8 @@
     sib_o: Any
     z_w: Any
     z_o: Any
+    relay_w: Any
+    relay_o: Any
     sm: Any
     sm_sib: Any
     sm_z: Any
@@ -798,6 +849,7 @@
     r.sm[...] = jnp.zeros_like(r.sm)
     r.sel[...] = step_select(g, here).astype(BF)
     open_sends, record = [], {}
+    line = w == 4
     arrivals = r.got if r.got.shape[0] == n - 1 else r.far
 
     def put(src, dst, axis, peer):
@@ -875,18 +927,64 @@
             pl.semaphore_signal(
                 r.free.at[kind], inc=1, device_id={SECTION: sibling}, device_id_type=MESH
             )
+        at = [wire.reserve() for _ in range(w)]
         found = []
         for k in range(1, w):
             peer = lax.rem(shard + k, w)
             source = grad.at[block_of(kind, peer, core)]
-            found.append(wire.put(source, z.at[layer, k - 1, kept(kind)], WT, peer))
-        record[kind] += found
-        return found
-
-    def to_plane(layer, kind, copies):
+            found.append(wire.make(source, z.at[layer, k - 1, kept(kind)], WT, peer, at[k], at[k]))
+        if not line:
+            for copy in found:
+                copy.start()
+            record[kind] += found
+            return found, None
+        buffer = (r.relay_o if kind == OUT else r.relay_w).at[layer, kept(kind)]
+        up = wire.make(grad.at[block_of(kind, w - 1, core)], buffer, WT, 1, at[0], at[0])
+        down = wire.make(grad.at[block_of(kind, 0, core)], buffer, WT, w - 2, at[0], at[0])
+        inner = (shard == 1) | (shard == 2)
+        record[kind] += [
+            Maybe(shard == 0, up).start(),
+            Maybe(shard == w - 1, down).start(),
+            Maybe(jnp.logical_not(inner), found[1]).start(),
+            Maybe(shard != w - 1, found[0]).start(),
+            Maybe(shard != 0, found[2]).start(),
+        ]
+        arriving = wire.make(buffer, buffer, WT, lax.rem(shard + 1, w), at[0], at[0])
+        return found, arriving
+
+    def relay(layer, kind, moving):
+        found, arriving = moving
+        if not line:
+            return
+        grad, buffer = (r.gout, r.relay_o) if kind == OUT else (r.gw, r.relay_w)
+        rows_here = kept(kind)
+
+        @pl.when((shard == 1) | (shard == 2))
+        def _():
+            arriving.wait_recv()
+            at_rows, at_lanes = block_of(kind, lax.rem(shard + 2, w), core)
+
+            def add(at):
+                mine = pl.ds(pl.multiple_of(at_rows.start + at.start, TILE), TILE)
+                there = pl.ds(pl.multiple_of(rows_here.start + at.start, TILE), TILE)
+                total = grad[mine, at_lanes].astype(F32) + buffer[layer, there, :].astype(F32)
+                grad[mine, at_lanes] = total.astype(BF)
+
+            rows_loop(rows_here.stop - rows_here.start, add)
+            found[1].start()
+
+        record[kind].append(Maybe((shard == 1) | (shard == 2), found[1]))
+
+    def to_plane(layer, kind, moving):
         grad, _, z, result, _ = buffers(kind)
-        for copy in copies:
-            copy.wait_recv()
+        copies, _ = moving
+        if line:
+            pl.when(shard != 0)(copies[0].wait_recv)
+            copies[1].wait_recv()
+            pl.when(shard != w - 1)(copies[2].wait_recv)
+        else:
+            for copy in copies:
+                copy.wait_recv()
         at_rows, at_lanes = block_of(kind, shard, core)
         here_rows = kept(kind)
 
@@ -896,10 +994,32 @@
             total = grad[mine, at_lanes].astype(F32)
             for k in range(w - 1):
                 total = total + z[layer, k, there, :].astype(F32)
-            z[layer, 0, there, :] = total.astype(BF)
-
-        rows_loop(here_rows.stop - here_rows.start, add)
-        block, target = z.at[layer, 0, here_rows], result.at[layer, here, here_rows]
+            z[layer, 1, there, :] = total.astype(BF)
+
+        def add_end(at, near):
+            mine = pl.ds(pl.multiple_of(at_rows.start + at.start, TILE), TILE)
+            there = pl.ds(pl.multiple_of(here_rows.start + at.start, TILE), TILE)
+            total = grad[mine, at_lanes].astype(F32)
+            total = total + z[layer, 1, there, :].astype(F32) + z[layer, near, there, :].astype(F32)
+            z[layer, 1, there, :] = total.astype(BF)
+
+        count = here_rows.stop - here_rows.start
+        if line:
+
+            @pl.when(shard == 0)
+            def _():
+                rows_loop(count, lambda at: add_end(at, 2))
+
+            @pl.when(shard == w - 1)
+            def _():
+                rows_loop(count, lambda at: add_end(at, 0))
+
+            @pl.when((shard == 1) | (shard == 2))
+            def _():
+                rows_loop(count, add)
+        else:
+            rows_loop(count, add)
+        block, target = z.at[layer, 1, here_rows], result.at[layer, here, here_rows]
         found = [put(block, target, SEQ, lax.rem(here + k, n)) for k in range(1, n)]
         return found, mover.put(block, target)
 
@@ -962,6 +1082,8 @@
             G, r.proj, r.dy, r.yp, r.st, conv, head, wide, r.sel, g_wide, g_conv, g_head,
             r.pad, r.xc, r.dts, r.dstate,
         )
+        relay(layer, OUT, out_z)
+        relay(layer, GATE, gate_z)
         if layer == 1:
             first = load(0, (r.of_i, r.of), (r.mixed_i, r.mixed))
             later = load(0, (r.yp_i, r.yp), (r.st_i, r.st))
@@ -1030,6 +1152,7 @@
                 peer = lax.rem(here + k, n)
                 gathering.append(put(r.gb.at[own], r.gb.at[own], SEQ, peer))
                 gathering.append(put(r.stats.at[here], r.stats.at[here], SEQ, peer))
+            relay(1, REST, rest_z)
             arrived[1, OUT] = to_plane(1, OUT, out_z)
             arrived[1, GATE] = to_plane(1, GATE, gate_z)
             for copy in gathering:
@@ -1037,6 +1160,7 @@
     ends = [put(r.grads.at[sibling], r.ig.at[core], SECTION, sibling)]
     ends.append(put(r.sm.at[sibling], r.sm_sib, SECTION, sibling))
     local_grad = mover.put(r.grads.at[core], r.ig.at[core])
+    relay(0, REST, rest_z)
     arrived[0, OUT] = to_plane(0, OUT, out_z)
     arrived[0, GATE] = to_plane(0, GATE, gate_z)
     ends[1].wait_recv()
@@ -1092,10 +1216,10 @@
         S((n, rows, D), BF), S((1 if spill else n - 1, rows, D), BF), S((8, 128), F32), S((rows, 128), F32), S((2, rows, D), F32),
         S((NC, D), BF), S((G, D), BF), S((g.half, D), BF), S((G // 2, D), BF),
         S((2, w - 1, g.half, lanes_of), BF),
-        S((2, w - 1, o_half, D), BF), S((2, 8, PK), F32), S((8, PK), F32), S((w - 1, 8, PK), F32), S((8, PK), F32),
+        S((2, w - 1, o_half, D), BF), S((2, g.half, lanes_of), BF), S((2, o_half, D), BF), S((2, 8, PK), F32), S((8, PK), F32), S((w - 1, 8, PK), F32), S((8, PK), F32),
         S((128, 128), BF),
     ]
-    remote = 2 * (3 * (w + w - 1 + n - 1) + n - 1) + 2 * (n - 1) + 5 + (w - 1) + (n - 1)
+    remote = 2 * (3 * (w + w + n - 1) + n - 1) + 2 * (n - 1) + 5 + (w - 1) + (n - 1)
     args = [
         fwd.packs_o, fwd.wf_o, fwd.of_o, fwd.n_o, fwd.proj_o, fwd.mixed_o, fwd.yp_o, fwd.st_o,
         fwd.gb_o, fwd.stats, fwd.stat0, fwd.pout, fwd.h1, tokens, cotangent,

time: 494 us -> 440 us (0.89)
  Pallas kernels: 478 us -> 424 us
    pallas_call x1, Pallas kernels: 234 us -> 201 us  [forward_call(): pl.pallas_call(functools.partial(forward_kernel, g, n, w, rows), out_shap...]
    pallas_call x1, Pallas kernels: 232 us -> 211 us  [backward_call(): pl.pallas_call(functools.partial(backward_kernel, g, n, w, rows), out_sha...]
where the time goes in v4:
time: 440 us; the launch traced here: 439 us
  Pallas kernels  424 us (96%)
  local copies, waits for them, and re-layouts  14.1 us (3%)
    pallas_call x1, Pallas kernels, backward_call(): pl.pallas_call(functools.partial(backward_kernel, g, n, w, rows), out_sha...  211 us
    pallas_call x1, Pallas kernels, forward_call(): pl.pallas_call(functools.partial(forward_kernel, g, n, w, rows), out_shap...  201 us
    unnamed x32, local copies, waits for them, and re-layouts  14.1 us

profile of v4, /device:TPU:8, one launch (start us, length us, event | category | flops | bytes accessed | tf_op | source)
XLA Modules:
  0.0 438.9 jit_solution(10456853965828392052)
XLA Ops:
  0.6 0.0 copy-start.6
  0.7 0.8 copy-done.6
  1.5 0.7 copy-done.7
  2.2 0.7 copy-done.8
  2.9 0.7 copy-done.9
  3.6 0.7 copy-done.10
  4.2 0.7 copy-done.11
  4.9 0.7 copy-done.12
  5.5 2.1 pack.1.refs_2_
  7.7 0.7 copy-done.4
  8.3 201.1 %forward.1 = (f32[2,128,1536]{2,1,0:T(8,128)}, f32[128,1536]{1,0:T(8,128)}, f32[8,128]{1,0:T(8,128)}, f32[128,1536]{1,0:T(8,128)}, bf16[512,1536]{1,0:T(8,128)(2...) custom-call(f32[2,1,128,1536]{3,2,1,0:T(8,128)} %refs_13_.1, ...), custom_call_target="tpu_custom_call" | custom-call | tf_op jit(solution)/shard_map/forward/pallas_call | solution.py:733
  209.5 211.2 %backward.1 = (f32[2,128,1536]{2,1,0:T(8,128)}, bf16[2,4,928,384]{3,2,1,0:T(8,128)(2,1)}, bf16[2,4,96,1536]{3,2,1,0:T(8,128)(2,1)}, bf16[4,928,384]{2,1,0:T(8,12...) custom-call(f32[2,8,3456]{2,1,0:T(8,128)} %get-tuple-element.40.refs_0_, ...), custom_call_target="tpu_custom_call" | custom-call | tf_op jit(solution)/shard_map/backward/pallas_call | solution.py:1227
  420.6 0.0 copy-start
  420.7 2.6 copy-done
  423.3 1.8 copy-done.1
  425.1 1.0 copy-done.5
  426.1 6.0 %layout.1 = (f32[6448,384]{1,0:T(8,128)}, f32[1,1536]{1,0:T(1,128)}, f32[4,3328]{1,0:T(4,128)}, f32[1,3328]{1,0:T(1,128)}, f32[1,48]{1,0:T(1,128)}, /*index=5*/f...) custom-call(s32[1]{0:T(128)} %bitcast.8.core_ref, bf16[2,4,928,384]{3,2,1,0:T(8,128)(2,1)S(1)} %copy-done, ...), custom_call_target="tpu_custom_call" | custom-call | tf_op jit(solution)/shard_map/layout/pallas_call | solution.py:1384
  432.1 0.0 copy-done.2
  432.1 0.0 copy-done.3
  432.1 3.7 widen.1
  435.8 0.0 copy-done.13
  435.8 1.1 copy.26
  436.9 0.8 copy-done.14
  437.7 1.1 copy.27
  (13 shorter events, 0.0 us)
Async XLA Ops:
  0.6 0.8 copy-start.6
  1.5 0.7 copy-start.7
  2.2 0.7 copy-start.8
  2.9 0.7 copy-start.9
  3.6 0.7 copy-start.10
  4.2 0.7 copy-start.11
  4.9 0.7 copy-start.12
  7.7 0.7 copy-start.4
  420.6 2.6 copy-start
  423.3 1.8 copy-start.1
  425.1 1.0 copy-start.5
  426.1 6.0 %copy-start.2 = (bf16[2,4,96,1536]{3,2,1,0:T(8,128)(2,1)S(1)}, bf16[2,4,96,1536]{3,2,1,0:T(8,128)(2,1)}, u32[]{:S(2)}) copy-start(bf16[2,4,96,1536]{3,2,1,0:T(8,128)(2,1)} %get-tuple-element.65.own_ref) | copy-start | bytes 7077892
  426.1 6.0 %copy-start.3 = (bf16[4,96,1536]{2,1,0:T(8,128)(2,1)S(1)}, bf16[4,96,1536]{2,1,0:T(8,128)(2,1)}, u32[]{:S(2)}) copy-start(bf16[4,96,1536]{2,1,0:T(8,128)(2,1)} %get-tuple-element.66.sib_ref) | copy-start | bytes 3538948
  432.1 3.7 copy-start.13
  435.7 2.0 copy-start.14

commit v5 on v4

--- a/solution.py
+++ b/solution.py
@@ -22,8 +22,8 @@
 BF = jnp.bfloat16
 SEQ, WT, SECTION = "seq", "wt", "section"
 FORWARD_VMEM = 56 * 2**20
-BACKWARD_VMEM = 60 * 2**20
-SMALL_VMEM = 40 * 2**20
+BACKWARD_VMEM = 62 * 2**20
+SMALL_VMEM = 60 * 2**20
 MESH = pl.DeviceIdType.MESH
 VM = pl.BlockSpec(memory_space=pltpu.VMEM)
 ANY = pl.BlockSpec(memory_space=pl.ANY)
@@ -166,7 +166,7 @@
 
 
 def scan_backward(G, proj_ref, dy_ref, yp_ref, st_ref, cw_ref, hp_ref, gw_ref, sel_ref, gg_ref, gc_ref, gh_ref,
-                  pad, xc, dts, dstate):
+                  pad, xc, dts, dstate, serve):
     L = proj_ref.shape[0]
     nb = L // Q
     mask = lane_mask(Q)
@@ -185,6 +185,7 @@
 
     def chunk(step, _):
         c = nb - 1 - step
+        pl.when(step == nb // 4)(serve)
         at = pl.ds(pl.multiple_of(c * Q, Q), Q)
         dt = dts[at, :]
         rate, cum, causal = chunk_factors(dt, hp_ref)
@@ -366,6 +367,36 @@
         pl.when(self.condition)(self.copy.wait_send)
 
 
+class PlaneGather:
+    def __init__(self, put, n, here, source, block):
+        self.put, self.block, self.plane = put, block, n == 4
+        mine = block(here, None)
+        if not self.plane:
+            self.copies = [put(source, mine, SEQ, lax.rem(here + k, n)) for k in range(1, n)]
+            return
+        self.x = here + 1 - 2 * lax.rem(here, 2)
+        self.y = lax.rem(here + 2, 4)
+        self.copies = [put(source, mine, SEQ, self.x), put(source, mine, SEQ, self.y)]
+
+    def forward(self):
+        if self.plane:
+            for copy, group, half, peer in (
+                (self.copies[0], self.x, 0, self.y),
+                (self.copies[1], self.y, 1, self.x),
+            ):
+                copy.wait_recv()
+                part = self.block(group, half)
+                self.copies.append(self.put(part, part, SEQ, peer))
+
+    def wait_recv(self):
+        for copy in self.copies[2:] if self.plane else self.copies:
+            copy.wait_recv()
+
+    def wait_send(self):
+        for copy in self.copies:
+            copy.wait_send()
+
+
 class Mover:
     def __init__(self, sems):
         self.sems, self.used = sems, 0
@@ -422,7 +453,13 @@
 class ForwardRefs(NamedTuple):
     tokens: Any
     cotangent: Any
-    pack: Any
+    conv_w: Any
+    conv_b: Any
+    dt_bias: Any
+    a_log: Any
+    skip_d: Any
+    gate_gain: Any
+    norm_gain: Any
     w_src: Any
     o_src: Any
     sec: Any
@@ -463,6 +500,7 @@
     cols: Any
     mdots: Any
     sel: Any
+    pack: Any
     ss: Any
     rs: Any
     ls: Any
@@ -490,6 +528,7 @@
             if first < last:
                 wf[layer, first:last, :] = jnp.zeros((last - first, D), BF)
     r.sel[...] = step_select(g, here).astype(BF)
+    pack_small(g, here, r.conv_w, r.conv_b, r.dt_bias, r.a_log, r.skip_d, r.gate_gain, r.norm_gain, r.pack)
     meet_all(((SEQ, n), (WT, w), (SECTION, 2)))
     o_rows = G // w
     lanes_of = D // w
@@ -545,19 +584,23 @@
             sends.extend(copies)
         return copies, at
 
-    def hand_on(fetched, layer, kind, then=None):
-        copies, at = fetched
+    def far_part(fetched, layer, kind):
+        if not line:
+            return []
+        at = fetched[1]
+        fetched[0][1].wait_recv()
+        block = part_of(layer, kind, lax.rem(shard + 2, w), core)
+        up = wire.make(block, block, WT, lax.rem(shard + 1, w), at[0], at[3])
+        down = wire.make(block, block, WT, lax.rem(shard + w - 1, w), at[0], at[1])
+        sends.append(Maybe(shard == 2, up).start())
+        sends.append(Maybe(shard == 1, down).start())
+        return [put(block, block, SECTION, sibling)]
+
+    def near_parts(fetched, layer, kind):
         found = []
-        for k in (2, 1, 3) if line else range(1, w):
-            copies[k - 1].wait_recv()
+        for k in (1, 3) if line else range(1, w):
+            fetched[0][k - 1].wait_recv()
             block = part_of(layer, kind, lax.rem(shard + w - k, w), core)
-            if line and k == 2:
-                up = wire.make(block, block, WT, lax.rem(shard + 1, w), at[0], at[3])
-                down = wire.make(block, block, WT, lax.rem(shard + w - 1, w), at[0], at[1])
-                sends.append(Maybe(shard == 2, up).start())
-                sends.append(Maybe(shard == 1, down).start())
-            if k == 2 and then is not None:
-                then()
             found.append(put(block, block, SECTION, sibling))
         return found
 
@@ -567,11 +610,12 @@
 
     own_rows = aligned(here * rows, rows)
 
-    def gather(layer_ref):
-        return [
-            wire.put(layer_ref.at[own_rows], layer_ref.at[own_rows], SEQ, lax.rem(here + k, n))
-            for k in range(1, n)
-        ]
+    def gather(whole):
+        def block(group, half):
+            size = rows if half is None else rows // 2
+            return whole.at[aligned(group * rows + (half or 0) * size, size)]
+
+        return PlaneGather(wire.put, n, here, block(here, None), block)
 
     def save(source, target):
         saves.append(mover.put(source, target))
@@ -595,6 +639,10 @@
 
     rows_loop(rows, norm)
     arriving = gather(r.normed)
+    handed = far_part(pending, 0, REST)
+    coming = [fetch(0, GATE), fetch(0, OUT)]
+    arriving.forward()
+    handed += near_parts(pending, 0, REST)
 
     for layer in range(2):
         proj, mixed, normed = r.proj, r.mixed, r.normed
@@ -605,16 +653,7 @@
         def project(lanes):
             proj[:, lanes] = dot(normed[...], wf[layer, lanes, :], 1, 1).astype(BF)
 
-        coming = []
-
-        def fetch_others():
-            coming.extend([fetch(layer, GATE), fetch(layer, OUT)])
-
-        def fetch_above():
-            coming.append(fetch(1, REST))
-
-        handed = hand_on(pending, layer, REST, fetch_others)
-        received(arriving)
+        arriving.wait_recv()
         received(handed)
         gathered = arriving
         column_tiles(G, NC, project)
@@ -626,9 +665,10 @@
         save(r.yp, r.yp_o.at[layer])
         save(r.st, r.st_o.at[layer])
         save(normed, r.n_o.at[layer])
-        handed = hand_on(coming[0], layer, GATE)
-        handed += hand_on(coming[1], layer, OUT, fetch_above if layer == 0 else None)
-        pending = coming[-1]
+        handed = far_part(coming[0], layer, GATE) + far_part(coming[1], layer, OUT)
+        handed += near_parts(coming[0], layer, GATE) + near_parts(coming[1], layer, OUT)
+        if layer == 0:
+            pending = fetch(1, REST)
         received(handed)
         column_tiles(0, G, project)
         save(proj, r.proj_o.at[layer])
@@ -643,6 +683,7 @@
             column_tiles(0, D, tile)
 
         saved()
+        gathered.wait_send()
         summing = []
         for k in range(1, n):
             peer = lax.rem(here + k, n)
@@ -652,6 +693,9 @@
         out_product(here)
         for copy in summing:
             copy.wait()
+        if layer == 0:
+            handed = far_part(pending, 1, REST)
+            coming = [fetch(1, GATE), fetch(1, OUT)]
         ssq = r.ssq[here]
         for k in range(n - 1):
             ssq = ssq + r.got_stat[k]
@@ -678,15 +722,15 @@
                 r.mdots[at, :] = jnp.broadcast_to(dots * (1.0 / INNER), (TILE, 128))
                 r.normed[whole, :] = out
 
-        for copy in gathered:
-            copy.wait_send()
         rows_loop(rows, finish)
         if layer == 0:
             arriving = gather(r.normed)
+            arriving.forward()
+            handed += near_parts(pending, 1, REST)
     r.stats[here] = r.own_stat[...]
     r.stats[here, 1:2, :] = r.mdots[...].T[0:1, :]
-    arriving = gather(r.normed)
-    sends.extend(arriving)
+    last_rows = gather(r.normed)
+    arriving = []
     for k in range(1, n):
         block = r.stats.at[here]
         arriving.append(put(block, block, SEQ, lax.rem(here + k, n)))
@@ -695,16 +739,19 @@
     save(packs, r.packs_o)
     save(wf, r.wf_o)
     save(of, r.of_o)
+    last_rows.forward()
+    last_rows.wait_recv()
     received(arriving)
     save(r.normed, r.gb_o)
+    last_rows.wait_send()
     for copy in sends:
         copy.wait_send()
     saved()
 
 
-def forward_call(g, n, w, tokens, cotangent, pack, w_src, o_src):
+def forward_call(g, n, w, tokens, cotangent, small, w_src, o_src):
     rows = tokens.shape[2]
-    L, G, NC, CX, PK = rows * n, g.G, g.NC, g.CX, pack.shape[1]
+    L, G, NC, CX, PK = rows * n, g.G, g.NC, g.CX, g.CX + 128 + g.G + D
     S = jax.ShapeDtypeStruct
     shapes = ForwardOuts(
         sec=S((2, rows, D), F32),
@@ -727,13 +774,13 @@
         S((L, G), F32), S((L // Q, STATE, G), F32), S((8 + L, 128), F32), S((L, CX), F32), S((L, 128), F32), S((STATE, G), F32),
         S((L, G), BF), S((n, 8, 128), F32), S((n, rows, D), BF), S((n - 1, rows, D), BF), S((n - 1, 8, 128), F32),
         S((2, rows, D), F32), S((8, 128), F32), S((rows, 128), F32), S((rows, 128), F32),
-        S((128, 128), BF),
+        S((128, 128), BF), S((8, PK), F32),
     ]
-    remote = 4 + 2 * g.runs + 6 * w + 6 * (w - 1) + 8 * (n - 1) + 2
+    remote = 4 + 2 * g.runs + 6 * w + 6 * (w - 1) + 3 + 8 * (n - 1) + 2
     outs = pl.pallas_call(
         functools.partial(forward_kernel, g, n, w, rows),
         out_shape=list(shapes),
-        in_specs=[ANY, ANY, VM, ANY, ANY],
+        in_specs=[ANY, ANY] + [VM] * len(small) + [ANY, ANY],
         out_specs=[VM] * 4 + [ANY, VM] + [ANY] * 8,
         scratch_shapes=[pltpu.VMEM(s.shape, s.dtype) for s in scratch]
         + [
@@ -745,7 +792,7 @@
             collective_id=0, has_side_effects=True, vmem_limit_bytes=FORWARD_VMEM
         ),
         name="forward",
-    )(tokens, cotangent, pack, w_src, o_src)
+    )(tokens, cotangent, *small, w_src, o_src)
     return ForwardOuts(*outs)
 
 
@@ -757,6 +804,7 @@
     go_sib: Any
     small: Any
     far: Any
+    late: Any
 
 
 class BackwardRefs(NamedTuple):
@@ -782,6 +830,7 @@
     go_sib: Any
     small: Any
     far: Any
+    late: Any
     packs: Any
     wf: Any
     of: Any
@@ -819,6 +868,9 @@
     sm_z: Any
     sm_own: Any
     sel: Any
+    gain: Any
+    gain_z: Any
+    gain_sum: Any
     ss: Any
     rs: Any
     ls: Any
@@ -848,6 +900,7 @@
     meet_all(((SEQ, n), (WT, w), (SECTION, 2)))
     r.sm[...] = jnp.zeros_like(r.sm)
     r.sel[...] = step_select(g, here).astype(BF)
+    r.gain[here] = jnp.zeros((8, D), F32)
     open_sends, record = [], {}
     line = w == 4
     arrivals = r.got if r.got.shape[0] == n - 1 else r.far
@@ -942,13 +995,21 @@
         up = wire.make(grad.at[block_of(kind, w - 1, core)], buffer, WT, 1, at[0], at[0])
         down = wire.make(grad.at[block_of(kind, 0, core)], buffer, WT, w - 2, at[0], at[0])
         inner = (shard == 1) | (shard == 2)
-        record[kind] += [
-            Maybe(shard == 0, up).start(),
-            Maybe(shard == w - 1, down).start(),
-            Maybe(jnp.logical_not(inner), found[1]).start(),
-            Maybe(shard != w - 1, found[0]).start(),
-            Maybe(shard != 0, found[2]).start(),
+        first = [
+            Maybe(shard == 0, up),
+            Maybe(shard == w - 1, down),
+            Maybe(inner, found[0]),
+            Maybe(inner, found[2]),
         ]
+        others = [
+            Maybe(jnp.logical_not(inner), found[1]),
+            Maybe(shard == 0, found[0]),
+            Maybe(shard == w - 1, found[2]),
+        ]
+        record[kind] += [*first, *others, Maybe(inner, found[1])]
+        for copy in first:
+            copy.start()
+        waiting.extend(others)
         arriving = wire.make(buffer, buffer, WT, lax.rem(shard + 1, w), at[0], at[0])
         return found, arriving
 
@@ -972,8 +1033,6 @@
 
             rows_loop(rows_here.stop - rows_here.start, add)
             found[1].start()
-
-        record[kind].append(Maybe((shard == 1) | (shard == 2), found[1]))
 
     def to_plane(layer, kind, moving):
         grad, _, z, result, _ = buffers(kind)
@@ -1019,15 +1078,20 @@
                 rows_loop(count, add)
         else:
             rows_loop(count, add)
-        block, target = z.at[layer, 1, here_rows], result.at[layer, here, here_rows]
-        found = [put(block, target, SEQ, lax.rem(here + k, n)) for k in range(1, n)]
-        return found, mover.put(block, target)
+        def target(group, half):
+            size = here_rows.stop - here_rows.start
+            if half is None:
+                return result.at[layer, group, here_rows]
+            first = here_rows.start + half * (size // 2)
+            return result.at[layer, group, first : first + size // 2]
+
+        block = z.at[layer, 1, here_rows]
+        return PlaneGather(put, n, here, block, target), mover.put(block, target(here, None))
 
     def landed(kind, *arrivals):
         _, _, _, result, target = buffers(kind)
         for found, own in arrivals:
-            for copy in found:
-                copy.wait_recv()
+            found.wait_recv()
             own.wait()
         return put(result.at[sibling, :, kept(kind)], target.at[:, kept(kind)], SECTION, sibling)
 
@@ -1035,7 +1099,7 @@
         for copy in copies:
             copy.wait()
 
-    arrived = {}
+    arrived, waiting = {}, []
     for layer in (1, 0):
         conv = r.packs.at[layer, :, 0:CX]
         head = r.packs.at[layer, :, CX : CX + 128]
@@ -1043,7 +1107,7 @@
         g_conv = r.sm.at[layer, :, 0:CX]
         g_head = r.sm.at[layer, :, CX : CX + 128]
         g_wide = r.sm.at[layer, :, CX + 128 : gain_at]
-        g_gain = r.sm.at[layer, :, gain_at : gain_at + D]
+        g_gain = r.sm.at[layer, :, gain_at : gain_at + D] if layer == 1 else r.gain.at[here]
         done(first)
 
         def d_normed(lanes):
@@ -1077,13 +1141,30 @@
         out_z = to_shards(layer, OUT, out_sib)
         gate_z = to_shards(layer, GATE, gate_sib)
         if layer == 0:
+            arrived[1, OUT][0].forward()
+            arrived[1, GATE][0].forward()
             arrived[1, REST] = to_plane(1, REST, rest_z)
+
+        def serve():
+            for copy in waiting:
+                copy.start()
+
         scan_backward(
             G, r.proj, r.dy, r.yp, r.st, conv, head, wide, r.sel, g_wide, g_conv, g_head,
-            r.pad, r.xc, r.dts, r.dstate,
+            r.pad, r.xc, r.dts, r.dstate, serve,
         )
+        waiting.clear()
         relay(layer, OUT, out_z)
         relay(layer, GATE, gate_z)
+        if layer == 0:
+            small_sib = put(r.sm.at[sibling], r.sm_sib, SECTION, sibling)
+        if layer == 0:
+            arrived[1, REST][0].forward()
+            small_sib.wait_recv()
+            r.sm_own[...] = r.sm[core] + r.sm_sib[...]
+            small_z = [
+                put(r.sm_own, r.sm_z.at[k - 1], WT, lax.rem(shard + k, w)) for k in range(1, w)
+            ]
         if layer == 1:
             first = load(0, (r.of_i, r.of), (r.mixed_i, r.mixed))
             later = load(0, (r.yp_i, r.yp), (r.st_i, r.st))
@@ -1112,6 +1193,8 @@
         rest_sib = to_sibling(layer, REST)
         rest_z = to_shards(layer, REST, rest_sib)
         done(summing)
+        while waiting:
+            waiting.pop(0).start()
         if arrivals is not r.got:
             done(
                 [
@@ -1148,43 +1231,65 @@
             r.stats[here, 1:2, :] = r.mdots[...].T[0:1, :]
             own = aligned(here * rows, rows)
             gathering = []
+
+            def rows_of_group(group, half):
+                size = rows if half is None else rows // 2
+                return r.gb.at[aligned(group * rows + (half or 0) * size, size)]
+
+            grad_rows = PlaneGather(put, n, here, r.gb.at[own], rows_of_group)
             for k in range(1, n):
                 peer = lax.rem(here + k, n)
-                gathering.append(put(r.gb.at[own], r.gb.at[own], SEQ, peer))
                 gathering.append(put(r.stats.at[here], r.stats.at[here], SEQ, peer))
             relay(1, REST, rest_z)
+            grad_rows.forward()
             arrived[1, OUT] = to_plane(1, OUT, out_z)
             arrived[1, GATE] = to_plane(1, GATE, gate_z)
+            grad_rows.wait_recv()
             for copy in gathering:
                 copy.wait_recv()
+    gains = []
     ends = [put(r.grads.at[sibling], r.ig.at[core], SECTION, sibling)]
-    ends.append(put(r.sm.at[sibling], r.sm_sib, SECTION, sibling))
+    for k in range(1, n):
+        gains.append(put(r.gain.at[here], r.gain.at[here], SEQ, lax.rem(here + k, n)))
     local_grad = mover.put(r.grads.at[core], r.ig.at[core])
     relay(0, REST, rest_z)
     arrived[0, OUT] = to_plane(0, OUT, out_z)
     arrived[0, GATE] = to_plane(0, GATE, gate_z)
-    ends[1].wait_recv()
-    r.sm_own[...] = r.sm[core] + r.sm_sib[...]
-    sums = [
-        put(r.sm_own, r.sm_z.at[k - 1], WT, lax.rem(shard + k, w)) for k in range(1, w)
-    ]
-    for copy in sums:
+    arrived[0, OUT][0].forward()
+    arrived[0, GATE][0].forward()
+    for copy in small_z:
         copy.wait_recv()
     total = r.sm_own[...]
     for k in range(w - 1):
         total = total + r.sm_z[k]
     r.small[here] = total
     sums = [
-        put(r.small.at[here], r.small.at[here], SEQ, lax.rem(here + k, n))
-        for k in range(1, n)
+        put(r.small.at[here], r.small.at[here], SEQ, lax.rem(here + k, n)) for k in range(1, n)
     ]
+    for copy in gains:
+        copy.wait_recv()
+    total = r.gain[0]
+    for k in range(1, n):
+        total = total + r.gain[k]
+    r.gain_z[shard] = total
+    gains = [
+        put(r.gain_z.at[shard], r.gain_z.at[shard], WT, lax.rem(shard + k, w)) for k in range(1, w)
+    ]
+    arrived[0, REST] = to_plane(0, REST, rest_z)
     ends.append(landed(OUT, arrived[1, OUT], arrived[0, OUT]))
     ends.append(landed(GATE, arrived[1, GATE], arrived[0, GATE]))
-    arrived[0, REST] = to_plane(0, REST, rest_z)
+    arrived[0, REST][0].forward()
     ends.append(landed(REST, arrived[1, REST], arrived[0, REST]))
-    ends[0].wait_recv()
-    for copy in ends[2:] + sums:
+    for copy in gains:
         copy.wait_recv()
+    total = r.gain_z[0]
+    for k in range(1, w):
+        total = total + r.gain_z[k]
+    r.gain_sum[core] = total
+    ends.append(put(r.gain_sum.at[core], r.gain_sum.at[core], SECTION, sibling))
+    for copy in ends + sums:
+        copy.wait_recv()
+    r.late[...] = r.gain_sum[0] + r.gain_sum[1]
     local_grad.wait()
     for kind in KINDS:
         ready(kind)
@@ -1207,6 +1312,7 @@
         go_sib=S((n, o_half, D), BF),
         small=S((n, 8, PK), F32),
         far=S((n - 1, rows, D) if spill else (8, 128), BF),
+        late=S((8, D), F32),
     )
     scratch = [
         S((2, 8, PK), F32), S((NC, D), BF), S((G, D), BF), S((L, D), BF), S((L, NC), BF), S((L, G), BF),
@@ -1217,9 +1323,9 @@
         S((NC, D), BF), S((G, D), BF), S((g.half, D), BF), S((G // 2, D), BF),
         S((2, w - 1, g.half, lanes_of), BF),
         S((2, w - 1, o_half, D), BF), S((2, g.half, lanes_of), BF), S((2, o_half, D), BF), S((2, 8, PK), F32), S((8, PK), F32), S((w - 1, 8, PK), F32), S((8, PK), F32),
-        S((128, 128), BF),
+        S((128, 128), BF), S((n, 8, D), F32), S((w, 8, D), F32), S((2, 8, D), F32),
     ]
-    remote = 2 * (3 * (w + w + n - 1) + n - 1) + 2 * (n - 1) + 5 + (w - 1) + (n - 1)
+    remote = 2 * (3 * (w + w + n - 1) + n - 1) + 2 * (n - 1) + 6 + 2 * (w - 1) + 2 * (n - 1)
     args = [
         fwd.packs_o, fwd.wf_o, fwd.of_o, fwd.n_o, fwd.proj_o, fwd.mixed_o, fwd.yp_o, fwd.st_o,
         fwd.gb_o, fwd.stats, fwd.stat0, fwd.pout, fwd.h1, tokens, cotangent,
@@ -1228,7 +1334,7 @@
         functools.partial(backward_kernel, g, n, w, rows),
         out_shape=list(outs),
         in_specs=[ANY] * len(args),
-        out_specs=[VM, ANY, ANY, ANY, ANY, VM, ANY],
+        out_specs=[VM, ANY, ANY, ANY, ANY, VM, ANY, VM],
         scratch_shapes=[pltpu.VMEM(s.shape, s.dtype) for s in scratch]
         + [
             pltpu.SemaphoreType.DMA((remote,)),
@@ -1244,9 +1350,9 @@
     return BackwardOuts(*results)
 
 
-def pack_kernel(g, win, conv_ref, bias_ref, dtb_ref, a_ref, skip_ref, gate_ref, norm_ref, pack_ref):
-    here = lax.axis_index(SEQ)
+def pack_small(g, here, conv_ref, bias_ref, dtb_ref, a_ref, skip_ref, gate_ref, norm_ref, pack_ref):
     G, width = g.G, g.run_heads * HEAD_DIM
+    win = -(-(width + 64) // 128) * 128
     start = here * width
     base = pl.multiple_of(start // 128 * 128, 128)
     from_ids = lax.broadcasted_iota(jnp.int32, (win, G), 0)
@@ -1281,18 +1387,6 @@
     pack_ref[0:1, gain_at:] = norm_ref[...]
 
 
-def pack_call(g, *small):
-    win = -(-(g.run_heads * HEAD_DIM + 64) // 128) * 128
-    return pl.pallas_call(
-        functools.partial(pack_kernel, g, win),
-        out_shape=jax.ShapeDtypeStruct((8, g.CX + 128 + g.G + D), F32),
-        in_specs=[VM] * len(small),
-        out_specs=VM,
-        compiler_params=pltpu.CompilerParams(vmem_limit_bytes=SMALL_VMEM),
-        name="pack",
-    )(*small)
-
-
 def halves_of_heads(g, ref_of, column_at, head):
     parts = []
     for h in (head, head + 1):
@@ -1305,7 +1399,7 @@
     return jnp.where(lanes < HEAD_DIM, parts[0], parts[1])
 
 
-def layout_kernel(g, own_ref, sib_ref, small_ref, g_in_ref, norm_ref, conv_ref, bias_ref, dtb_ref, a_ref, skip_ref, gate_ref):
+def layout_kernel(g, own_ref, sib_ref, own_out_ref, sib_out_ref, small_ref, late_ref, g_in_ref, g_out_ref, norm_ref, conv_ref, bias_ref, dtb_ref, a_ref, skip_ref, gate_ref):
     n, G = g.n_seq, g.G
     first_core = lax.axis_index(SECTION) == 0
 
@@ -1323,6 +1417,9 @@
             g_in_ref[target + done : target + done + count, :] = total
             done += count
 
+    own, sib = own_out_ref[0].astype(F32), sib_out_ref[...].astype(F32)
+    g_out_ref[:, 0] = jnp.where(first_core, own, sib)
+    g_out_ref[:, 1] = jnp.where(first_core, sib, own)
     width = g.run_heads * HEAD_DIM
     rest = (G, G // 2, g.rest // 2)
     everyone = range(n)
@@ -1358,7 +1455,7 @@
             norm = norm + small(group, slice(gain_at, gain_at + D))
         conv_ref[:, INNER:] = conv[0:KERNEL]
         bias_ref[:, INNER:] = conv[KERNEL : KERNEL + 1]
-        norm_ref[...] = norm[0:1]
+        norm_ref[...] = jnp.where(first_core, late_ref[0:1, :], norm[0:1])
         heads = jnp.zeros((8, HEADS), F32)
         skips = jnp.zeros((8, HEADS), F32)
         wide_from = lax.broadcasted_iota(jnp.int32, (G, HEADS), 0)
@@ -1372,56 +1469,41 @@
         skip_ref[...] = skips[1:2]
 
 
-def layout_call(g, core, gi, gi_sib, small):
+def layout_call(g, core, gi, gi_sib, go, go_sib, small, late):
     _, n, half, lanes = gi.shape
+    out_half = go.shape[2]
+    steps = lanes // 128
+    out_lanes = D // steps
     PK = small.shape[2]
     columns = 2 * INNER + 2 * STATE + HEADS
     S = jax.ShapeDtypeStruct
     shapes = (
-        S((columns, lanes), F32), S((1, D), F32), S((KERNEL, CONV), F32), S((1, CONV), F32), S((1, HEADS), F32),
-        S((1, HEADS), F32), S((1, HEADS), F32), S((1, INNER), F32),
+        S((columns, lanes), F32), S((n, 2, out_half, D), F32), S((1, D), F32), S((KERNEL, CONV), F32),
+        S((1, CONV), F32), S((1, HEADS), F32), S((1, HEADS), F32), S((1, HEADS), F32), S((1, INNER), F32),
     )
     return pl.pallas_call(
         lambda core_ref, *refs: layout_kernel(g, *refs),
         grid_spec=pltpu.PrefetchScalarGridSpec(
             num_scalar_prefetch=1,
-            grid=(lanes // 128,),
+            grid=(steps,),
             in_specs=[
                 pl.BlockSpec((1, n, half, 128), lambda t, c: (c[0], 0, 0, t)),
                 pl.BlockSpec((n, half, 128), lambda t, c: (0, 0, t)),
+                pl.BlockSpec((1, n, out_half, out_lanes), lambda t, c: (c[0], 0, 0, t)),
+                pl.BlockSpec((n, out_half, out_lanes), lambda t, c: (0, 0, t)),
                 pl.BlockSpec((n, 8, PK), lambda t, c: (0, 0, 0)),
+                pl.BlockSpec((8, D), lambda t, c: (0, 0)),
             ],
-            out_specs=[pl.BlockSpec((columns, 128), lambda t, c: (0, t))]
-            + [pl.BlockSpec(s.shape, lambda t, c: (0, 0)) for s in shapes[1:]],
+            out_specs=[
+                pl.BlockSpec((columns, 128), lambda t, c: (0, t)),
+                pl.BlockSpec((n, 2, out_half, out_lanes), lambda t, c: (0, 0, 0, t)),
+            ]
+            + [pl.BlockSpec(s.shape, lambda t, c: (0, 0)) for s in shapes[2:]],
         ),
         out_shape=shapes,
         compiler_params=pltpu.CompilerParams(vmem_limit_bytes=SMALL_VMEM),
         name="layout",
-    )(core, gi, gi_sib, small)
-
-
-def widen_kernel(core_ref, own_ref, sib_ref, out_ref):
-    mine = pl.program_id(0) == core_ref[0]
-    out_ref[...] = jnp.where(mine, own_ref[...], sib_ref[...][None]).astype(F32).reshape(out_ref.shape)
-
-
-def widen_call(core, go, go_sib):
-    _, n, size, columns = go.shape
-    return pl.pallas_call(
-        widen_kernel,
-        grid_spec=pltpu.PrefetchScalarGridSpec(
-            num_scalar_prefetch=1,
-            grid=(2, n),
-            in_specs=[
-                pl.BlockSpec((1, 1, size, columns), lambda h, t, c: (c[0], t, 0, 0)),
-                pl.BlockSpec((1, size, columns), lambda h, t, c: (t, 0, 0)),
-            ],
-            out_specs=pl.BlockSpec((1, 1, size, columns), lambda h, t, c: (t, h, 0, 0)),
-        ),
-        out_shape=jax.ShapeDtypeStruct((n, 2, size, columns), F32),
-        compiler_params=pltpu.CompilerParams(vmem_limit_bytes=SMALL_VMEM),
-        name="widen",
-    )(core, go, go_sib)
+    )(core, gi, gi_sib, go, go_sib, small, late)
 
 
 def local(
@@ -1433,9 +1515,7 @@
     core = lax.axis_index(SECTION).reshape(1)
     G = group.G
 
-    pack = pack_call(
-        group, conv_w[0], conv_b, dt_bias, a_log, skip_d, gate_gain, norm_gain
-    )
+    small = (conv_w[0], conv_b, dt_bias, a_log, skip_d, gate_gain, norm_gain)
     w_src = jnp.swapaxes(w_in[0], 0, 1)
     if group.runs == n_wt:
         o_src = w_out[0]
@@ -1443,12 +1523,11 @@
         o_src = lax.all_gather(w_out[0], WT, axis=0, tiled=True)
         o_src = lax.dynamic_slice_in_dim(o_src, here * group.chans, group.chans, 0)
         o_src = jnp.pad(o_src, ((0, G - group.chans), (0, 0)))
-    fwd = forward_call(group, n_seq, n_wt, tokens, cotangent, pack, w_src, o_src)
+    fwd = forward_call(group, n_seq, n_wt, tokens, cotangent, small, w_src, o_src)
     bwd = backward_call(group, n_seq, n_wt, fwd, tokens, cotangent)
-    g_in, g_norm, g_conv, g_bias, g_dtb, g_a, g_skip, g_gate = layout_call(
-        group, core, bwd.gi, bwd.gi_sib, bwd.small
+    g_in, g_out, g_norm, g_conv, g_bias, g_dtb, g_a, g_skip, g_gate = layout_call(
+        group, core, bwd.gi, bwd.gi_sib, bwd.go, bwd.go_sib, bwd.small, bwd.late
     )
-    g_out = widen_call(core, bwd.go, bwd.go_sib)
     if group.runs == n_wt:
         g_out = g_out.reshape(INNER // n_wt, D)
     else:

time: 440 us -> 405 us (0.920)
  Pallas kernels: 424 us -> 399 us
  local copies, waits for them, and re-layouts: 14.1 us -> 3.11 us
    pallas_call x1, Pallas kernels: 211 us -> 197 us  [backward_call(): pl.pallas_call(functools.partial(backward_kernel, g, n, w, rows), out_sha...]
    unnamed x32 -> x6, local copies, waits for them, and re-layouts: 14.1 us -> 3.11 us
    pallas_call x1, Pallas kernels: 201 us -> 192 us  [forward_call(): pl.pallas_call(functools.partial(forward_kernel, g, n, w, rows), out_shap...]
    pallas_call x2 -> x0, Pallas kernels: 5.8 us -> none  [the longest x1 3.65 us: widen_call(): pl.pallas_call(widen_kernel, grid_spec=pltpu.PrefetchScalarGridSpec(num_s...]
where the time goes in v5:
time: 405 us; the launch traced here: 402 us
  Pallas kernels  399 us (99%)
    pallas_call x1, Pallas kernels, backward_call(): pl.pallas_call(functools.partial(backward_kernel, g, n, w, rows), out_sha...  197 us
    pallas_call x1, Pallas kernels, forward_call(): pl.pallas_call(functools.partial(forward_kernel, g, n, w, rows), out_shap...  192 us
    pallas_call x1, Pallas kernels, layout_call(): pl.pallas_call(lambda core_ref, *refs: layout_kernel(g, *refs), grid_spec...  10.4 us

profile of v5, /device:TPU:8, one launch (start us, length us, event | category | flops | bytes accessed | tf_op | source)
XLA Modules:
  0.0 402.4 jit_solution(5341951741669575048)
XLA Ops:
  0.6 191.6 %forward.1 = (f32[2,128,1536]{2,1,0:T(8,128)}, f32[128,1536]{1,0:T(8,128)}, f32[8,128]{1,0:T(8,128)}, f32[128,1536]{1,0:T(8,128)}, bf16[512,1536]{1,0:T(8,128)(2...) custom-call(f32[2,1,128,1536]{3,2,1,0:T(8,128)} %refs_13_.1, ...), custom_call_target="tpu_custom_call" | custom-call | tf_op jit(solution)/shard_map/forward/pallas_call | solution.py:780
  192.3 196.6 %backward.1 = (f32[2,128,1536]{2,1,0:T(8,128)}, bf16[2,4,928,384]{3,2,1,0:T(8,128)(2,1)}, bf16[2,4,96,1536]{3,2,1,0:T(8,128)(2,1)}, bf16[4,928,384]{2,1,0:T(8,12...) custom-call(f32[2,8,3456]{2,1,0:T(8,128)} %get-tuple-element.42.refs, ...), custom_call_target="tpu_custom_call" | custom-call | tf_op jit(solution)/shard_map/backward/pallas_call | solution.py:1333
  388.9 0.0 copy-start
  388.9 10.4 %layout.1 = (f32[6448,384]{1,0:T(8,128)}, f32[4,2,96,1536]{3,2,1,0:T(8,128)}, f32[1,1536]{1,0:T(1,128)}, f32[4,3328]{1,0:T(4,128)}, f32[1,3328]{1,0:T(1,128)}, /...) custom-call(s32[1]{0:T(128)} %bitcast.8.core_ref, ...), custom_call_target="tpu_custom_call" | custom-call | tf_op jit(solution)/shard_map/layout/pallas_call | solution.py:1484
  399.2 0.0 copy-start.1
  399.2 0.0 copy-done
  399.3 1.1 copy.26
  400.4 0.8 copy-done.1
  401.2 1.1 copy.27
Async XLA Ops:
  388.9 10.4 %copy-start = (f32[2,128,1536]{2,1,0:T(8,128)S(1)}, f32[2,128,1536]{2,1,0:T(8,128)}, u32[]{:S(2)}) copy-start(f32[2,128,1536]{2,1,0:T(8,128)} %get-tuple-element.41) | copy-start | bytes 4718596
  399.2 2.0 copy-start.1

commit v6 on v5

--- a/solution.py
+++ b/solution.py
@@ -139,6 +139,12 @@
     lax.fori_loop(0, proj_ref.shape[0] // Q, chunk, 0)
 
 
+def lane_sums(values, pick):
+    high = values.astype(BF)
+    low = (values - high.astype(F32)).astype(BF)
+    return dot(high, pick, 1, 0) + dot(low, pick, 1, 0)
+
+
 def gate_backward(G, proj_ref, mixed_ref, dn_ref, sc_ref, gw_ref, dy_ref, gg_ref):
     gg_ref[...] = jnp.zeros_like(gg_ref)
 
@@ -205,6 +211,7 @@
         d_dt = jnp.zeros((Q, 128), F32)
         d_last = jnp.zeros((8, 128), F32)
         lane_ids = lax.broadcasted_iota(jnp.int32, (Q, 128), 1)
+        row_ids = lax.broadcasted_iota(jnp.int32, (Q, 128), 0)
         for p in range(G // 128):
             lanes = slice(p * 128, p * 128 + 128)
             dyb = dy_ref[at, lanes]
@@ -234,14 +241,10 @@
             z3 = jnp.sum(uf * du_out, axis=0, keepdims=True) + e_last_x[0:1, :] * jnp.sum(before * after, axis=0, keepdims=True)
             z1 = d_y * yp_ref[at, lanes] - uf * du
             z2 = x * du
-            zero = jnp.zeros_like(z1)
-            for half, h in ((True, 2 * p), (False, 2 * p + 1)):
-                keep = mask if half else jnp.logical_not(mask)
-                here = lane_ids == h
-                d_cum = jnp.where(here, jnp.sum(jnp.where(keep, z1, zero), axis=1, keepdims=True), d_cum)
-                d_dt = jnp.where(here, jnp.sum(jnp.where(keep, z2, zero), axis=1, keepdims=True), d_dt)
-                s3 = jnp.sum(jnp.where(keep[0:8], jnp.broadcast_to(z3, (8, 128)), 0.0), axis=1, keepdims=True)
-                d_last = jnp.where(here[0:8], s3, d_last)
+            pick = jnp.where(lane_ids == 2 * p + jnp.where(row_ids < HEAD_DIM, 0, 1), 1.0, 0.0).astype(BF)
+            d_cum = d_cum + lane_sums(z1, pick)
+            d_dt = d_dt + lane_sums(z2, pick)
+            d_last = d_last + lane_sums(jnp.broadcast_to(z3, (8, 128)), pick)
             xc[at, lanes] = dt_x * du + gw_ref[1:2, lanes] * d_y
             gg_ref[1:2, lanes] += jnp.sum(d_y * x, axis=0, keepdims=True)
         dsb = d_scores.astype(BF)
@@ -527,8 +530,6 @@
         for first, last in ((g.chans, G), (G + g.chans, 2 * G), (2 * G + 2 * STATE + HEADS, NC)):
             if first < last:
                 wf[layer, first:last, :] = jnp.zeros((last - first, D), BF)
-    r.sel[...] = step_select(g, here).astype(BF)
-    pack_small(g, here, r.conv_w, r.conv_b, r.dt_bias, r.a_log, r.skip_d, r.gate_gain, r.norm_gain, r.pack)
     meet_all(((SEQ, n), (WT, w), (SECTION, 2)))
     o_rows = G // w
     lanes_of = D // w
@@ -544,18 +545,17 @@
             runs.append((source, kind_at + run * width, width))
     runs.append((2 * INNER, 2 * G, 2 * STATE))
     runs.append((2 * INNER + 2 * STATE, 2 * G + 2 * STATE, HEADS))
-    siblings = [put(r.pack, packs.at[core], SECTION, sibling)]
-    locals_ = [
-        mover.put(r.pack, packs.at[core]),
+    siblings, locals_ = [], []
+    for source, target, size in runs:
+        taken = r.w_src.at[aligned(source, size)]
+        siblings.append(put(taken, wf.at[core, target : target + size, mine_lanes], SECTION, sibling))
+        locals_.append(mover.put(taken, wf.at[core, target : target + size, mine_lanes]))
+    others = [put(o_own, of.at[core, mine_o], SECTION, sibling)]
+    locals_later = [
         mover.put(o_own, of.at[core, mine_o]),
         mover.put(r.tokens.at[core, 0], r.h0),
         mover.put(r.cotangent.at[core, 0], r.cot),
     ]
-    for source, target, size in runs:
-        taken = r.w_src.at[aligned(source, size)]
-        siblings.append(put(taken, wf.at[core, target : target + size, mine_lanes], SECTION, sibling))
-        locals_.append(mover.put(taken, wf.at[core, target : target + size, mine_lanes]))
-    siblings.append(put(o_own, of.at[core, mine_o], SECTION, sibling))
 
     def part_of(layer, kind, at_shard, at_core):
         if kind == OUT:
@@ -629,6 +629,13 @@
     received(siblings)
     pending = fetch(0, REST)
     gain_at = g.CX + 128 + G
+    r.sel[...] = step_select(g, here).astype(BF)
+    pack_small(g, here, r.conv_w, r.conv_b, r.dt_bias, r.a_log, r.skip_d, r.gate_gain, r.norm_gain, r.pack)
+    others.append(put(r.pack, packs.at[core], SECTION, sibling))
+    locals_later.append(mover.put(r.pack, packs.at[core]))
+    for copy in locals_later:
+        copy.wait()
+    received(others)
 
     def norm(at):
         h = r.h0[at, :]
@@ -1399,37 +1406,48 @@
     return jnp.where(lanes < HEAD_DIM, parts[0], parts[1])
 
 
-def layout_kernel(g, own_ref, sib_ref, own_out_ref, sib_out_ref, small_ref, late_ref, g_in_ref, g_out_ref, norm_ref, conv_ref, bias_ref, dtb_ref, a_ref, skip_ref, gate_ref):
+def layout_kernel(g, own_ref, sib_ref, own_out_ref, sib_out_ref, small_ref, late_ref, sec_ref, ig_ref, g_in_ref, g_out_ref, sec_out, ig_out, norm_ref, conv_ref, bias_ref, dtb_ref, a_ref, skip_ref, gate_ref):
     n, G = g.n_seq, g.G
     first_core = lax.axis_index(SECTION) == 0
 
-    def copy(groups, kind_at, half_at, half_rows, source, target, size):
-        done = 0
-        while done < size:
-            half, offset = divmod(source + done, half_rows)
-            count = min(size - done, half_rows - offset)
-            at = slice(half_at + offset, half_at + offset + count)
-            total = None
-            for group in groups:
-                own, sib = own_ref[0, group, at, :], sib_ref[group, at, :]
-                value = (jnp.where(first_core, own, sib) if half == 0 else jnp.where(first_core, sib, own)).astype(F32)
-                total = value if total is None else total + value
-            g_in_ref[target + done : target + done + count, :] = total
-            done += count
-
-    own, sib = own_out_ref[0].astype(F32), sib_out_ref[...].astype(F32)
-    g_out_ref[:, 0] = jnp.where(first_core, own, sib)
-    g_out_ref[:, 1] = jnp.where(first_core, sib, own)
-    width = g.run_heads * HEAD_DIM
-    rest = (G, G // 2, g.rest // 2)
-    everyone = range(n)
-    for run in range(g.runs):
-        for group in range(n):
-            target = run * (INNER // g.runs) + group * width
-            copy([group], 0, 0, G // 2, run * width, target, width)
-            copy([group], *rest, run * width, INNER + target, width)
-    copy(everyone, *rest, G, 2 * INNER, 2 * STATE)
-    copy(everyone, *rest, G + 2 * STATE, 2 * INNER + 2 * STATE, HEADS)
+    def all_rows(halves, outs):
+        def copy(groups, kind_at, half_at, half_rows, source, target, size):
+            done = 0
+            while done < size:
+                half, offset = divmod(source + done, half_rows)
+                count = min(size - done, half_rows - offset)
+                at = slice(half_at + offset, half_at + offset + count)
+                total = None
+                for group in groups:
+                    value = halves[half][group, at, :].astype(F32)
+                    total = value if total is None else total + value
+                g_in_ref[target + done : target + done + count, :] = total
+                done += count
+
+        for half in range(2):
+            g_out_ref[:, half] = outs[half][...].astype(F32)
+        width = g.run_heads * HEAD_DIM
+        rest = (G, G // 2, g.rest // 2)
+        everyone = range(n)
+        for run in range(g.runs):
+            for group in range(n):
+                target = run * (INNER // g.runs) + group * width
+                copy([group], 0, 0, G // 2, run * width, target, width)
+                copy([group], *rest, run * width, INNER + target, width)
+        copy(everyone, *rest, G, 2 * INNER, 2 * STATE)
+        copy(everyone, *rest, G + 2 * STATE, 2 * INNER + 2 * STATE, HEADS)
+
+    sec_out[...] = sec_ref[...]
+    ig_out[...] = ig_ref[...]
+    own, own_out = own_ref.at[0], own_out_ref.at[0]
+
+    @pl.when(first_core)
+    def _():
+        all_rows((own, sib_ref), (own_out, sib_out_ref))
+
+    @pl.when(jnp.logical_not(first_core))
+    def _():
+        all_rows((sib_ref, own), (sib_out_ref, own_out))
 
     @pl.when(pl.program_id(0) == 0)
     def _():
@@ -1469,16 +1487,17 @@
         skip_ref[...] = skips[1:2]
 
 
-def layout_call(g, core, gi, gi_sib, go, go_sib, small, late):
+def layout_call(g, core, gi, gi_sib, go, go_sib, small, late, sec, ig):
     _, n, half, lanes = gi.shape
     out_half = go.shape[2]
     steps = lanes // 128
     out_lanes = D // steps
+    rows_spec = pl.BlockSpec(sec.shape[:2] + (out_lanes,), lambda t, c: (0, 0, t))
     PK = small.shape[2]
     columns = 2 * INNER + 2 * STATE + HEADS
     S = jax.ShapeDtypeStruct
     shapes = (
-        S((columns, lanes), F32), S((n, 2, out_half, D), F32), S((1, D), F32), S((KERNEL, CONV), F32),
+        S((columns, lanes), F32), S((n, 2, out_half, D), F32), S(sec.shape, F32), S(ig.shape, F32), S((1, D), F32), S((KERNEL, CONV), F32),
         S((1, CONV), F32), S((1, HEADS), F32), S((1, HEADS), F32), S((1, HEADS), F32), S((1, INNER), F32),
     )
     return pl.pallas_call(
@@ -1493,17 +1512,21 @@
                 pl.BlockSpec((n, out_half, out_lanes), lambda t, c: (0, 0, t)),
                 pl.BlockSpec((n, 8, PK), lambda t, c: (0, 0, 0)),
                 pl.BlockSpec((8, D), lambda t, c: (0, 0)),
+                rows_spec,
+                rows_spec,
             ],
             out_specs=[
                 pl.BlockSpec((columns, 128), lambda t, c: (0, t)),
                 pl.BlockSpec((n, 2, out_half, out_lanes), lambda t, c: (0, 0, 0, t)),
+                rows_spec,
+                rows_spec,
             ]
-            + [pl.BlockSpec(s.shape, lambda t, c: (0, 0)) for s in shapes[2:]],
+            + [pl.BlockSpec(s.shape, lambda t, c: (0, 0)) for s in shapes[4:]],
         ),
         out_shape=shapes,
         compiler_params=pltpu.CompilerParams(vmem_limit_bytes=SMALL_VMEM),
         name="layout",
-    )(core, gi, gi_sib, go, go_sib, small, late)
+    )(core, gi, gi_sib, go, go_sib, small, late, sec, ig)
 
 
 def local(
@@ -1525,8 +1548,8 @@
         o_src = jnp.pad(o_src, ((0, G - group.chans), (0, 0)))
     fwd = forward_call(group, n_seq, n_wt, tokens, cotangent, small, w_src, o_src)
     bwd = backward_call(group, n_seq, n_wt, fwd, tokens, cotangent)
-    g_in, g_out, g_norm, g_conv, g_bias, g_dtb, g_a, g_skip, g_gate = layout_call(
-        group, core, bwd.gi, bwd.gi_sib, bwd.go, bwd.go_sib, bwd.small, bwd.late
+    g_in, g_out, section_out, input_grad, g_norm, g_conv, g_bias, g_dtb, g_a, g_skip, g_gate = layout_call(
+        group, core, bwd.gi, bwd.gi_sib, bwd.go, bwd.go_sib, bwd.small, bwd.late, fwd.sec, bwd.ig
     )
     if group.runs == n_wt:
         g_out = g_out.reshape(INNER // n_wt, D)
@@ -1536,8 +1559,8 @@
         mine = INNER // n_wt
         g_out = lax.dynamic_slice_in_dim(g_out, lax.axis_index(WT) * mine, mine, 0).astype(F32)
     return (
-        fwd.sec[None, :, None],
-        bwd.ig[None, :, None],
+        section_out[None, :, None],
+        input_grad[None, :, None],
         g_norm,
         jnp.swapaxes(g_in, 0, 1)[None],
         g_conv[None],

time: 405 us -> 398 us (0.983)
  Pallas kernels: 399 us -> 394 us
where the time goes in v6:
time: 398 us; the launch traced here: 395 us
  Pallas kernels  394 us (99%)
    pallas_call x1, Pallas kernels, backward_call(): pl.pallas_call(functools.partial(backward_kernel, g, n, w, rows), out_sha...  194 us
    pallas_call x1, Pallas kernels, forward_call(): pl.pallas_call(functools.partial(forward_kernel, g, n, w, rows), out_shap...  188 us
    pallas_call x1, Pallas kernels, layout_call(): pl.pallas_call(lambda core_ref, *refs: layout_kernel(g, *refs), grid_spec...  11.8 us

profile of v6, /device:TPU:8, one launch (start us, length us, event | category | flops | bytes accessed | tf_op | source)
XLA Modules:
  0.0 395.1 jit_solution(16189429640833086865)
XLA Ops:
  0.6 188.4 %forward.1 = (f32[2,128,1536]{2,1,0:T(8,128)}, f32[128,1536]{1,0:T(8,128)}, f32[8,128]{1,0:T(8,128)}, f32[128,1536]{1,0:T(8,128)}, bf16[512,1536]{1,0:T(8,128)(2...) custom-call(f32[2,1,128,1536]{3,2,1,0:T(8,128)} %refs_13_.1, ...), custom_call_target="tpu_custom_call" | custom-call | tf_op jit(solution)/shard_map/forward/pallas_call | solution.py:787
  189.1 194.0 %backward.1 = (f32[2,128,1536]{2,1,0:T(8,128)}, bf16[2,4,928,384]{3,2,1,0:T(8,128)(2,1)}, bf16[2,4,96,1536]{3,2,1,0:T(8,128)(2,1)}, bf16[4,928,384]{2,1,0:T(8,12...) custom-call(f32[2,8,3456]{2,1,0:T(8,128)} %get-tuple-element.43.refs, ...), custom_call_target="tpu_custom_call" | custom-call | tf_op jit(solution)/shard_map/backward/pallas_call | solution.py:1340
  383.1 11.8 %layout.1 = (f32[6448,384]{1,0:T(8,128)}, f32[4,2,96,1536]{3,2,1,0:T(8,128)}, f32[2,128,1536]{2,1,0:T(8,128)}, f32[2,128,1536]{2,1,0:T(8,128)}, f32[1,1536]{1,0:...) custom-call(s32[1]{0:T(128)} %bitcast.core_ref, ...), custom_call_target="tpu_custom_call" | custom-call | tf_op jit(solution)/shard_map/layout/pallas_call | solution.py:1503

commit v7 on v6

--- a/solution.py
+++ b/solution.py
@@ -297,13 +297,6 @@
     lax.fori_loop(0, rows // TILE, step, 0)
 
 
-def total_of(n, part_ref, got, at):
-    total = part_ref[lax.axis_index(SEQ), at, :].astype(F32)
-    for k in range(n - 1):
-        total = total + got[k, at, :].astype(F32)
-    return total
-
-
 class Group:
     def __init__(self, n_seq, n_wt):
         self.n_seq = n_seq
@@ -381,7 +374,7 @@
         self.y = lax.rem(here + 2, 4)
         self.copies = [put(source, mine, SEQ, self.x), put(source, mine, SEQ, self.y)]
 
-    def forward(self):
+    def forward(self, landed=None):
         if self.plane:
             for copy, group, half, peer in (
                 (self.copies[0], self.x, 0, self.y),
@@ -390,6 +383,8 @@
                 copy.wait_recv()
                 part = self.block(group, half)
                 self.copies.append(self.put(part, part, SEQ, peer))
+                if landed is not None:
+                    landed(group)
 
     def wait_recv(self):
         for copy in self.copies[2:] if self.plane else self.copies:
@@ -398,6 +393,67 @@
     def wait_send(self):
         for copy in self.copies:
             copy.wait_send()
+
+
+class PlaneSum:
+    def __init__(self, put, n, here, part, got, mid):
+        self.put, self.n, self.here, self.part, self.got, self.mid = put, n, here, part, got, mid
+        self.plane = n == 4
+        self.half = part.shape[1] // 2
+        self.peers = [lax.rem(here + k, n) for k in range(1, n)]
+        if self.plane:
+            self.x = here + 1 - 2 * lax.rem(here, 2)
+            self.y = lax.rem(here + 2, 4)
+            self.peers = [lax.rem(self.x + 2, 4), self.y, self.x]
+
+    def start(self, product, stat=None, got_stat=None):
+        half, part, got = self.half, self.part, self.got
+        self.copies = []
+        for k, peer in enumerate(self.peers):
+            product(peer)
+            if not self.plane:
+                self.copies.append(self.put(part.at[peer], got.at[k], SEQ, peer))
+            elif k == 0:
+                self.mids = [
+                    self.put(part.at[peer, 0:half], self.mid.at[0], SEQ, self.x),
+                    self.put(part.at[peer, half:], self.mid.at[1], SEQ, self.y),
+                ]
+            elif k == 1:
+                self.copies.append(self.put(part.at[peer, half:], got.at[1, half:], SEQ, peer))
+            else:
+                self.copies.append(self.put(part.at[peer, 0:half], got.at[0, 0:half], SEQ, peer))
+            if stat is not None:
+                self.copies.append(self.put(stat.at[peer], got_stat.at[k], SEQ, peer))
+        product(self.here)
+
+    def middle(self):
+        if not self.plane:
+            return
+        half, part = self.half, self.part
+        for copy in self.mids:
+            copy.wait()
+
+        def add(at):
+            late = pl.ds(pl.multiple_of(at.start + half, TILE), TILE)
+            for peer, rows, slot in ((self.y, at, 0), (self.x, late, 1)):
+                total = part[peer, rows, :].astype(F32) + self.mid[slot, at, :].astype(F32)
+                part[peer, rows, :] = total.astype(BF)
+
+        rows_loop(half, add)
+        self.copies += [
+            self.put(part.at[self.y, 0:half], self.got.at[1, 0:half], SEQ, self.y),
+            self.put(part.at[self.x, half:], self.got.at[0, half:], SEQ, self.x),
+        ]
+
+    def end(self):
+        for copy in self.copies:
+            copy.wait()
+
+    def total(self, at):
+        total = self.part[self.here, at, :].astype(F32)
+        for k in range(2 if self.plane else self.n - 1):
+            total = total + self.got[k, at, :].astype(F32)
+        return total
 
 
 class Mover:
@@ -504,6 +560,7 @@
     mdots: Any
     sel: Any
     pack: Any
+    mid: Any
     ss: Any
     rs: Any
     ls: Any
@@ -691,15 +748,10 @@
 
         saved()
         gathered.wait_send()
-        summing = []
-        for k in range(1, n):
-            peer = lax.rem(here + k, n)
-            out_product(peer)
-            summing.append(wire.put(r.part.at[peer], r.got.at[k - 1], SEQ, peer))
-            summing.append(wire.put(r.ssq.at[peer], r.got_stat.at[k - 1], SEQ, peer))
-        out_product(here)
-        for copy in summing:
-            copy.wait()
+        summing = PlaneSum(wire.put, n, here, r.part, r.got, r.mid)
+        summing.start(out_product, r.ssq, r.got_stat)
+        summing.middle()
+        summing.end()
         if layer == 0:
             handed = far_part(pending, 1, REST)
             coming = [fetch(1, GATE), fetch(1, OUT)]
@@ -713,7 +765,7 @@
             r.stat0[...] = inv2
 
         def finish(at):
-            pout = total_of(n, r.part, r.got, at) * r.cols[at, 0:1]
+            pout = summing.total(at) * r.cols[at, 0:1]
             whole = pl.ds(pl.multiple_of(here * rows + at.start, TILE), TILE)
             h_in = r.h0[at, :] if layer == 0 else r.hbuf[0, at, :]
             h = h_in + pout
@@ -751,6 +803,7 @@
     received(arriving)
     save(r.normed, r.gb_o)
     last_rows.wait_send()
+    assert wire.used <= r.ss.shape[0] and mover.used <= r.ls.shape[0]
     for copy in sends:
         copy.wait_send()
     saved()
@@ -781,9 +834,9 @@
         S((L, G), F32), S((L // Q, STATE, G), F32), S((8 + L, 128), F32), S((L, CX), F32), S((L, 128), F32), S((STATE, G), F32),
         S((L, G), BF), S((n, 8, 128), F32), S((n, rows, D), BF), S((n - 1, rows, D), BF), S((n - 1, 8, 128), F32),
         S((2, rows, D), F32), S((8, 128), F32), S((rows, 128), F32), S((rows, 128), F32),
-        S((128, 128), BF), S((8, PK), F32),
+        S((128, 128), BF), S((8, PK), F32), S((2, rows // 2, D), BF),
     ]
-    remote = 4 + 2 * g.runs + 6 * w + 6 * (w - 1) + 3 + 8 * (n - 1) + 2
+    remote = 4 + 2 * g.runs + 6 * w + 6 * (w - 1) + 24 + 8 * (n - 1)
     outs = pl.pallas_call(
         functools.partial(forward_kernel, g, n, w, rows),
         out_shape=list(shapes),
@@ -878,6 +931,7 @@
     gain: Any
     gain_z: Any
     gain_sum: Any
+    mid: Any
     ss: Any
     rs: Any
     ls: Any
@@ -1184,22 +1238,26 @@
 
             column_tiles(0, D, tile)
 
-        summing = []
-        for k in range(1, n):
-            peer = lax.rem(here + k, n)
-            in_product(peer)
-            summing.append(wire.put(r.part.at[peer], arrivals.at[k - 1], SEQ, peer))
-        in_product(here)
+        summing = PlaneSum(wire.put, n, here, r.part, arrivals, r.mid)
+
+        def rest_gradient():
+            ready(REST)
+            in_rows(G, NC)
+            return to_sibling(layer, REST)
+
+        if layer == 0:
+            rest_sib = rest_gradient()
+            rest_z = to_shards(layer, REST, rest_sib)
+        summing.start(in_product)
         if layer == 1:
             later += load(0, (r.wf_i, r.wf))
-        ready(REST)
-        in_rows(G, NC)
+        summing.middle()
         if layer == 1:
+            rest_sib = rest_gradient()
             first += load(0, (r.proj_i, r.proj))
             later += load(0, (r.n_i, r.n))
-        rest_sib = to_sibling(layer, REST)
-        rest_z = to_shards(layer, REST, rest_sib)
-        done(summing)
+            rest_z = to_shards(layer, REST, rest_sib)
+        summing.end()
         while waiting:
             waiting.pop(0).start()
         if arrivals is not r.got:
@@ -1212,7 +1270,7 @@
 
         def finish(at):
             if arrivals is r.got:
-                d_in = total_of(n, r.part, r.got, at)
+                d_in = summing.total(at)
             else:
                 d_in = r.part[0, at, :].astype(F32)
                 for k in range(1, n):
@@ -1285,8 +1343,24 @@
     arrived[0, REST] = to_plane(0, REST, rest_z)
     ends.append(landed(OUT, arrived[1, OUT], arrived[0, OUT]))
     ends.append(landed(GATE, arrived[1, GATE], arrived[0, GATE]))
-    arrived[0, REST][0].forward()
-    ends.append(landed(REST, arrived[1, REST], arrived[0, REST]))
+    arrived[1, REST][0].wait_recv()
+    arrived[1, REST][1].wait()
+    last, last_own = arrived[0, REST]
+
+    def hand_over(group):
+        source, target = r.gi.at[sibling, group, kept(REST)], r.gi_sib.at[group, kept(REST)]
+        ends.append(put(source, target, SECTION, sibling))
+
+    last_own.wait()
+    hand_over(here)
+    if last.plane:
+        last.forward(hand_over)
+        last.wait_recv()
+        hand_over(lax.rem(last.x + 2, 4))
+    else:
+        last.wait_recv()
+        for k in range(1, n):
+            hand_over(lax.rem(here + k, n))
     for copy in gains:
         copy.wait_recv()
     total = r.gain_z[0]
@@ -1298,6 +1372,7 @@
         copy.wait_recv()
     r.late[...] = r.gain_sum[0] + r.gain_sum[1]
     local_grad.wait()
+    assert wire.used <= r.ss.shape[0] and mover.used <= r.ls.shape[0]
     for kind in KINDS:
         ready(kind)
     for copy in open_sends:
@@ -1331,8 +1406,9 @@
         S((2, w - 1, g.half, lanes_of), BF),
         S((2, w - 1, o_half, D), BF), S((2, g.half, lanes_of), BF), S((2, o_half, D), BF), S((2, 8, PK), F32), S((8, PK), F32), S((w - 1, 8, PK), F32), S((8, PK), F32),
         S((128, 128), BF), S((n, 8, D), F32), S((w, 8, D), F32), S((2, 8, D), F32),
+        S((2, rows // 2, D), BF),
     ]
-    remote = 2 * (3 * (w + w + n - 1) + n - 1) + 2 * (n - 1) + 6 + 2 * (w - 1) + 2 * (n - 1)
+    remote = 2 * (3 * (w + w + n - 1) + n - 1) + 2 * (n - 1) + 40 + 2 * (w - 1) + 2 * (n - 1) + n
     args = [
         fwd.packs_o, fwd.wf_o, fwd.of_o, fwd.n_o, fwd.proj_o, fwd.mixed_o, fwd.yp_o, fwd.st_o,
         fwd.gb_o, fwd.stats, fwd.stat0, fwd.pout, fwd.h1, tokens, cotangent,

time: 398 us -> 384 us (0.965)
  Pallas kernels: 394 us -> 379 us
    pallas_call x1, Pallas kernels: 194 us -> 184 us  [backward_call(): pl.pallas_call(functools.partial(backward_kernel, g, n, w, rows), out_sha...]
    pallas_call x1, Pallas kernels: 188 us -> 183 us  [forward_call(): pl.pallas_call(functools.partial(forward_kernel, g, n, w, rows), out_shap...]
where the time goes in v7:
time: 384 us; the launch traced here: 380 us
  Pallas kernels  379 us (99%)
    pallas_call x1, Pallas kernels, backward_call(): pl.pallas_call(functools.partial(backward_kernel, g, n, w, rows), out_sha...  184 us
    pallas_call x1, Pallas kernels, forward_call(): pl.pallas_call(functools.partial(forward_kernel, g, n, w, rows), out_shap...  183 us
    pallas_call x1, Pallas kernels, layout_call(): pl.pallas_call(lambda core_ref, *refs: layout_kernel(g, *refs), grid_spec...  11.8 us

profile of v7, /device:TPU:8, one launch (start us, length us, event | category | flops | bytes accessed | tf_op | source)
XLA Modules:
  0.0 380.2 jit_solution(16077113984136490230)
XLA Ops:
  0.6 183.4 %forward.1 = (f32[2,128,1536]{2,1,0:T(8,128)}, f32[128,1536]{1,0:T(8,128)}, f32[8,128]{1,0:T(8,128)}, f32[128,1536]{1,0:T(8,128)}, bf16[512,1536]{1,0:T(8,128)(2...) custom-call(f32[2,1,128,1536]{3,2,1,0:T(8,128)} %refs_13_.1, ...), custom_call_target="tpu_custom_call" | custom-call | tf_op jit(solution)/shard_map/forward/pallas_call | solution.py:840
  184.1 184.1 %backward.1 = (f32[2,128,1536]{2,1,0:T(8,128)}, bf16[2,4,928,384]{3,2,1,0:T(8,128)(2,1)}, bf16[2,4,96,1536]{3,2,1,0:T(8,128)(2,1)}, bf16[4,928,384]{2,1,0:T(8,12...) custom-call(f32[2,8,3456]{2,1,0:T(8,128)} %get-tuple-element.43.refs, ...), custom_call_target="tpu_custom_call" | custom-call | tf_op jit(solution)/shard_map/backward/pallas_call | solution.py:1416
  368.2 11.8 %layout.1 = (f32[6448,384]{1,0:T(8,128)}, f32[4,2,96,1536]{3,2,1,0:T(8,128)}, f32[2,128,1536]{2,1,0:T(8,128)}, f32[2,128,1536]{2,1,0:T(8,128)}, f32[1,1536]{1,0:...) custom-call(s32[1]{0:T(128)} %bitcast.core_ref, ...), custom_call_target="tpu_custom_call" | custom-call | tf_op jit(solution)/shard_map/layout/pallas_call | solution.py:1579

commit v8 on v7

--- a/solution.py
+++ b/solution.py
@@ -409,8 +409,8 @@
     def start(self, product, stat=None, got_stat=None):
         half, part, got = self.half, self.part, self.got
         self.copies = []
+        product()
         for k, peer in enumerate(self.peers):
-            product(peer)
             if not self.plane:
                 self.copies.append(self.put(part.at[peer], got.at[k], SEQ, peer))
             elif k == 0:
@@ -424,7 +424,6 @@
                 self.copies.append(self.put(part.at[peer, 0:half], got.at[0, 0:half], SEQ, peer))
             if stat is not None:
                 self.copies.append(self.put(stat.at[peer], got_stat.at[k], SEQ, peer))
-        product(self.here)
 
     def middle(self):
         if not self.plane:
@@ -490,6 +489,23 @@
     lax.fori_loop(0, whole, step, 0)
     if first + whole * 256 < last:
         body(slice(first + whole * 256, last))
+
+
+def four_blocks(part, product):
+    count, rows, columns = part.shape
+
+    def step(q, carry):
+        at = pl.ds(pl.multiple_of(q * 4 * rows, TILE), 4 * rows)
+
+        def tile(lanes):
+            value = product(at, lanes).astype(BF)
+            for b in range(4):
+                part[q * 4 + b, :, lanes] = value[b * rows : (b + 1) * rows]
+
+        column_tiles(0, columns, tile)
+        return carry
+
+    lax.fori_loop(0, count // 4, step, 0)
 
 
 class ForwardOuts(NamedTuple):
@@ -738,13 +754,8 @@
         save(proj, r.proj_o.at[layer])
         gate_forward(G, proj, wide, mixed, r.vg, r.ssq)
 
-        def out_product(block):
-            at = aligned(block * rows, rows)
-
-            def tile(lanes):
-                r.part[block, :, lanes] = dot(r.vg[at, :], of[layer, :, lanes], 1, 0).astype(BF)
-
-            column_tiles(0, D, tile)
+        def out_product():
+            four_blocks(r.part, lambda at, lanes: dot(r.vg[at, :], of[layer, :, lanes], 1, 0))
 
         saved()
         gathered.wait_send()
@@ -1168,7 +1179,6 @@
         g_conv = r.sm.at[layer, :, 0:CX]
         g_head = r.sm.at[layer, :, CX : CX + 128]
         g_wide = r.sm.at[layer, :, CX + 128 : gain_at]
-        g_gain = r.sm.at[layer, :, gain_at : gain_at + D] if layer == 1 else r.gain.at[here]
         done(first)
 
         def d_normed(lanes):
@@ -1179,25 +1189,18 @@
             G, r.proj, r.mixed, r.xc, r.stats, wide, r.dy, g_wide
         )
 
-        def out_rows(t, carry):
-            at = pl.ds(pl.multiple_of(t * 128, 128), 128)
+        def out_rows(at):
             r.gout[at, :] = dot(r.mixed[:, at], r.gb[...], 0, 0).astype(BF)
-            return carry
-
-        def in_rows(first, last):
-            def step(t, carry):
-                at = pl.ds(pl.multiple_of(t * 128, 128), 128)
-                r.gw[at, :] = dot(r.proj[:, at], r.n[...], 0, 0).astype(BF)
-                return carry
-
-            lax.fori_loop(first // 128, last // 128, step, 0)
+
+        def in_rows(at):
+            r.gw[at, :] = dot(r.proj[:, at], r.n[...], 0, 0).astype(BF)
 
         ready(OUT)
-        lax.fori_loop(0, G // 128, out_rows, 0)
+        column_tiles(0, G, out_rows)
         out_sib = to_sibling(layer, OUT)
         done(later)
         ready(GATE)
-        in_rows(0, G)
+        column_tiles(0, G, in_rows)
         gate_sib = to_sibling(layer, GATE)
         out_z = to_shards(layer, OUT, out_sib)
         gate_z = to_shards(layer, GATE, gate_sib)
@@ -1230,32 +1233,28 @@
             first = load(0, (r.of_i, r.of), (r.mixed_i, r.mixed))
             later = load(0, (r.yp_i, r.yp), (r.st_i, r.st))
 
-        def in_product(block):
-            at = aligned(block * rows, rows)
-
-            def tile(lanes):
-                r.part[block, :, lanes] = dot(r.proj[at, :], r.wf[:, lanes], 1, 0).astype(BF)
-
-            column_tiles(0, D, tile)
+        def in_product():
+            four_blocks(r.part, lambda at, lanes: dot(r.proj[at, :], r.wf[:, lanes], 1, 0))
 
         summing = PlaneSum(wire.put, n, here, r.part, arrivals, r.mid)
 
         def rest_gradient():
             ready(REST)
-            in_rows(G, NC)
+            column_tiles(G, NC, in_rows)
             return to_sibling(layer, REST)
 
         if layer == 0:
             rest_sib = rest_gradient()
+            summing.start(in_product)
             rest_z = to_shards(layer, REST, rest_sib)
-        summing.start(in_product)
-        if layer == 1:
+            summing.middle()
+        else:
+            summing.start(in_product)
             later += load(0, (r.wf_i, r.wf))
-        summing.middle()
-        if layer == 1:
             rest_sib = rest_gradient()
             first += load(0, (r.proj_i, r.proj))
             later += load(0, (r.n_i, r.n))
+            summing.middle()
             rest_z = to_shards(layer, REST, rest_sib)
         summing.end()
         while waiting:
@@ -1279,7 +1278,7 @@
             above = r.cot[at, :] if layer == 1 else r.grads[1, at, :]
             inv = lax.rsqrt(jnp.mean(h * h, axis=1, keepdims=True) + EPSILON)
             normed = h * inv
-            g_gain[0:1, :] += jnp.sum(d_in * normed, axis=0, keepdims=True)
+            r.gain[here, layer : layer + 1, :] += jnp.sum(d_in * normed, axis=0, keepdims=True)
             d_s = d_in * r.packs[layer, 0:1, gain_at:]
             d_h = above + inv * (d_s - normed * jnp.mean(d_s * normed, axis=1, keepdims=True))
             r.grads[layer, at, :] = d_h
@@ -1305,8 +1304,8 @@
             for k in range(1, n):
                 peer = lax.rem(here + k, n)
                 gathering.append(put(r.stats.at[here], r.stats.at[here], SEQ, peer))
+            grad_rows.forward()
             relay(1, REST, rest_z)
-            grad_rows.forward()
             arrived[1, OUT] = to_plane(1, OUT, out_z)
             arrived[1, GATE] = to_plane(1, GATE, gate_z)
             grad_rows.wait_recv()
@@ -1392,7 +1391,7 @@
         go=S((2, n, o_half, D), BF),
         gi_sib=S((n, g.half, lanes_of), BF),
         go_sib=S((n, o_half, D), BF),
-        small=S((n, 8, PK), F32),
+        small=S((n, 8, PK - D), F32),
         far=S((n - 1, rows, D) if spill else (8, 128), BF),
         late=S((8, D), F32),
     )
@@ -1404,7 +1403,7 @@
         S((n, rows, D), BF), S((1 if spill else n - 1, rows, D), BF), S((8, 128), F32), S((rows, 128), F32), S((2, rows, D), F32),
         S((NC, D), BF), S((G, D), BF), S((g.half, D), BF), S((G // 2, D), BF),
         S((2, w - 1, g.half, lanes_of), BF),
-        S((2, w - 1, o_half, D), BF), S((2, g.half, lanes_of), BF), S((2, o_half, D), BF), S((2, 8, PK), F32), S((8, PK), F32), S((w - 1, 8, PK), F32), S((8, PK), F32),
+        S((2, w - 1, o_half, D), BF), S((2, g.half, lanes_of), BF), S((2, o_half, D), BF), S((2, 8, PK - D), F32), S((8, PK - D), F32), S((w - 1, 8, PK - D), F32), S((8, PK - D), F32),
         S((128, 128), BF), S((n, 8, D), F32), S((w, 8, D), F32), S((2, 8, D), F32),
         S((2, rows // 2, D), BF),
     ]
@@ -1543,13 +1542,11 @@
             bias_ref[:, at] = conv[KERNEL : KERNEL + 1]
             gate_ref[:, at] = halves_of_heads(g, small, wide_at, head)[0:1]
         conv = small(0, slice(G, head_at))
-        norm = small(0, slice(gain_at, gain_at + D))
         for group in range(1, n):
             conv = conv + small(group, slice(G, head_at))
-            norm = norm + small(group, slice(gain_at, gain_at + D))
         conv_ref[:, INNER:] = conv[0:KERNEL]
         bias_ref[:, INNER:] = conv[KERNEL : KERNEL + 1]
-        norm_ref[...] = jnp.where(first_core, late_ref[0:1, :], norm[0:1])
+        norm_ref[...] = jnp.where(first_core, late_ref[0:1, :], late_ref[1:2, :])
         heads = jnp.zeros((8, HEADS), F32)
         skips = jnp.zeros((8, HEADS), F32)
         wide_from = lax.broadcasted_iota(jnp.int32, (G, HEADS), 0)

time: 384 us -> 378 us (0.984)
    pallas_call x1, Pallas kernels: 184 us -> 180 us  [backward_call(): pl.pallas_call(functools.partial(backward_kernel, g, n, w, rows), out_sha...]
where the time goes in v8:
time: 378 us; the launch traced here: 377 us
  Pallas kernels  376 us (99%)
    pallas_call x1, Pallas kernels, forward_call(): pl.pallas_call(functools.partial(forward_kernel, g, n, w, rows), out_shap...  184 us
    pallas_call x1, Pallas kernels, backward_call(): pl.pallas_call(functools.partial(backward_kernel, g, n, w, rows), out_sha...  180 us
    pallas_call x1, Pallas kernels, layout_call(): pl.pallas_call(lambda core_ref, *refs: layout_kernel(g, *refs), grid_spec...  11.7 us

profile of v8, /device:TPU:8, one launch (start us, length us, event | category | flops | bytes accessed | tf_op | source)
XLA Modules:
  0.0 376.9 jit_solution(16381675314899091984)
XLA Ops:
  0.6 184.4 %forward.1 = (f32[2,128,1536]{2,1,0:T(8,128)}, f32[128,1536]{1,0:T(8,128)}, f32[8,128]{1,0:T(8,128)}, f32[128,1536]{1,0:T(8,128)}, bf16[512,1536]{1,0:T(8,128)(2...) custom-call(f32[2,1,128,1536]{3,2,1,0:T(8,128)} %refs_13_.1, ...), custom_call_target="tpu_custom_call" | custom-call | tf_op jit(solution)/shard_map/forward/pallas_call | solution.py:851
  185.0 179.9 %backward.1 = (f32[2,128,1536]{2,1,0:T(8,128)}, bf16[2,4,928,384]{3,2,1,0:T(8,128)(2,1)}, bf16[2,4,96,1536]{3,2,1,0:T(8,128)(2,1)}, bf16[4,928,384]{2,1,0:T(8,12...) custom-call(f32[2,8,3456]{2,1,0:T(8,128)} %get-tuple-element.43.refs, ...), custom_call_target="tpu_custom_call" | custom-call | tf_op jit(solution)/shard_map/backward/pallas_call | solution.py:1415
  365.0 11.7 %layout.1 = (f32[6448,384]{1,0:T(8,128)}, f32[4,2,96,1536]{3,2,1,0:T(8,128)}, f32[2,128,1536]{2,1,0:T(8,128)}, f32[2,128,1536]{2,1,0:T(8,128)}, f32[1,1536]{1,0:...) custom-call(s32[1]{0:T(128)} %bitcast.core_ref, ...), custom_call_target="tpu_custom_call" | custom-call | tf_op jit(solution)/shard_map/layout/pallas_call | solution.py:1576

commit v9 on v8

--- a/solution.py
+++ b/solution.py
@@ -309,6 +309,7 @@
         self.NC = 2 * self.G + 2 * STATE + 128
         self.rest = self.G + 2 * STATE + 64
         self.half = (self.G + self.rest) // 2
+        self.cut = self.rest // 128 * 64
 
 
 def head_of(g, here, local_head):
@@ -327,7 +328,7 @@
     return one_hot((from_ids == head_of(g, here, to_ids)) & (to_ids < g.heads))
 
 
-OUT, GATE, REST = KINDS = range(3)
+OUT, GATE, REST, LAST = KINDS = range(4)
 
 
 class Wire:
@@ -983,10 +984,11 @@
         return copy
 
     def rows_of(kind):
-        return ((0, G), (0, G), (G, g.rest))[kind]
+        return ((0, G), (0, G), (G, g.cut), (G + g.cut, g.rest - g.cut))[kind]
 
     def kept(kind):
-        return (slice(0, G // (2 * w)), slice(0, G // 2), slice(G // 2, g.half))[kind]
+        middle = (G + g.cut) // 2
+        return (slice(0, G // (2 * w)), slice(0, G // 2), slice(G // 2, middle), slice(middle, g.half))[kind]
 
     def buffers(kind):
         if kind == OUT:
@@ -1207,7 +1209,8 @@
         if layer == 0:
             arrived[1, OUT][0].forward()
             arrived[1, GATE][0].forward()
-            arrived[1, REST] = to_plane(1, REST, rest_z)
+            arrived[1, REST] = to_plane(1, REST, rest_z[0])
+            arrived[1, LAST] = to_plane(1, LAST, rest_z[1])
 
         def serve():
             for copy in waiting:
@@ -1224,6 +1227,7 @@
             small_sib = put(r.sm.at[sibling], r.sm_sib, SECTION, sibling)
         if layer == 0:
             arrived[1, REST][0].forward()
+            arrived[1, LAST][0].forward()
             small_sib.wait_recv()
             r.sm_own[...] = r.sm[core] + r.sm_sib[...]
             small_z = [
@@ -1240,13 +1244,17 @@
 
         def rest_gradient():
             ready(REST)
+            ready(LAST)
             column_tiles(G, NC, in_rows)
-            return to_sibling(layer, REST)
+            return to_sibling(layer, REST), to_sibling(layer, LAST)
+
+        def rest_to_shards(copies):
+            return to_shards(layer, REST, copies[0]), to_shards(layer, LAST, copies[1])
 
         if layer == 0:
             rest_sib = rest_gradient()
             summing.start(in_product)
-            rest_z = to_shards(layer, REST, rest_sib)
+            rest_z = rest_to_shards(rest_sib)
             summing.middle()
         else:
             summing.start(in_product)
@@ -1255,7 +1263,7 @@
             first += load(0, (r.proj_i, r.proj))
             later += load(0, (r.n_i, r.n))
             summing.middle()
-            rest_z = to_shards(layer, REST, rest_sib)
+            rest_z = rest_to_shards(rest_sib)
         summing.end()
         while waiting:
             waiting.pop(0).start()
@@ -1305,7 +1313,8 @@
                 peer = lax.rem(here + k, n)
                 gathering.append(put(r.stats.at[here], r.stats.at[here], SEQ, peer))
             grad_rows.forward()
-            relay(1, REST, rest_z)
+            relay(1, REST, rest_z[0])
+            relay(1, LAST, rest_z[1])
             arrived[1, OUT] = to_plane(1, OUT, out_z)
             arrived[1, GATE] = to_plane(1, GATE, gate_z)
             grad_rows.wait_recv()
@@ -1316,9 +1325,10 @@
     for k in range(1, n):
         gains.append(put(r.gain.at[here], r.gain.at[here], SEQ, lax.rem(here + k, n)))
     local_grad = mover.put(r.grads.at[core], r.ig.at[core])
-    relay(0, REST, rest_z)
+    relay(0, REST, rest_z[0])
     arrived[0, OUT] = to_plane(0, OUT, out_z)
     arrived[0, GATE] = to_plane(0, GATE, gate_z)
+    relay(0, LAST, rest_z[1])
     arrived[0, OUT][0].forward()
     arrived[0, GATE][0].forward()
     for copy in small_z:
@@ -1339,15 +1349,18 @@
     gains = [
         put(r.gain_z.at[shard], r.gain_z.at[shard], WT, lax.rem(shard + k, w)) for k in range(1, w)
     ]
-    arrived[0, REST] = to_plane(0, REST, rest_z)
+    arrived[0, REST] = to_plane(0, REST, rest_z[0])
     ends.append(landed(OUT, arrived[1, OUT], arrived[0, OUT]))
     ends.append(landed(GATE, arrived[1, GATE], arrived[0, GATE]))
-    arrived[1, REST][0].wait_recv()
-    arrived[1, REST][1].wait()
-    last, last_own = arrived[0, REST]
+    arrived[0, LAST] = to_plane(0, LAST, rest_z[1])
+    arrived[0, REST][0].forward()
+    ends.append(landed(REST, arrived[1, REST], arrived[0, REST]))
+    arrived[1, LAST][0].wait_recv()
+    arrived[1, LAST][1].wait()
+    last, last_own = arrived[0, LAST]
 
     def hand_over(group):
-        source, target = r.gi.at[sibling, group, kept(REST)], r.gi_sib.at[group, kept(REST)]
+        source, target = r.gi.at[sibling, group, kept(LAST)], r.gi_sib.at[group, kept(LAST)]
         ends.append(put(source, target, SECTION, sibling))
 
     last_own.wait()
@@ -1407,7 +1420,7 @@
         S((128, 128), BF), S((n, 8, D), F32), S((w, 8, D), F32), S((2, 8, D), F32),
         S((2, rows // 2, D), BF),
     ]
-    remote = 2 * (3 * (w + w + n - 1) + n - 1) + 2 * (n - 1) + 40 + 2 * (w - 1) + 2 * (n - 1) + n
+    remote = 2 * (4 * (w + w + n) + n - 1) + 2 * (n - 1) + 40 + 2 * (w - 1) + 2 * (n - 1) + n
     args = [
         fwd.packs_o, fwd.wf_o, fwd.of_o, fwd.n_o, fwd.proj_o, fwd.mixed_o, fwd.yp_o, fwd.st_o,
         fwd.gb_o, fwd.stats, fwd.stat0, fwd.pout, fwd.h1, tokens, cotangent,
@@ -1421,8 +1434,8 @@
         + [
             pltpu.SemaphoreType.DMA((remote,)),
             pltpu.SemaphoreType.DMA((remote,)),
-            pltpu.SemaphoreType.DMA((36 + 2 * n,)),
-            pltpu.SemaphoreType.REGULAR((3,)),
+            pltpu.SemaphoreType.DMA((40 + 2 * n,)),
+            pltpu.SemaphoreType.REGULAR((4,)),
         ],
         compiler_params=pltpu.CompilerParams(
             collective_id=1, has_side_effects=True, vmem_limit_bytes=BACKWARD_VMEM
@@ -1486,11 +1499,13 @@
     first_core = lax.axis_index(SECTION) == 0
 
     def all_rows(halves, outs):
-        def copy(groups, kind_at, half_at, half_rows, source, target, size):
+        def copy(groups, parts, source, target, size):
             done = 0
             while done < size:
-                half, offset = divmod(source + done, half_rows)
-                count = min(size - done, half_rows - offset)
+                row = source + done
+                first, part_rows, half_at = next(x for x in parts if x[0] <= row < x[0] + x[1])
+                half, offset = divmod(row - first, part_rows // 2)
+                count = min(size - done, part_rows // 2 - offset)
                 at = slice(half_at + offset, half_at + offset + count)
                 total = None
                 for group in groups:
@@ -1502,15 +1517,16 @@
         for half in range(2):
             g_out_ref[:, half] = outs[half][...].astype(F32)
         width = g.run_heads * HEAD_DIM
-        rest = (G, G // 2, g.rest // 2)
+        gate = ((0, G, 0),)
+        rest = ((0, g.cut, G // 2), (g.cut, g.rest - g.cut, (G + g.cut) // 2))
         everyone = range(n)
         for run in range(g.runs):
             for group in range(n):
                 target = run * (INNER // g.runs) + group * width
-                copy([group], 0, 0, G // 2, run * width, target, width)
-                copy([group], *rest, run * width, INNER + target, width)
-        copy(everyone, *rest, G, 2 * INNER, 2 * STATE)
-        copy(everyone, *rest, G + 2 * STATE, 2 * INNER + 2 * STATE, HEADS)
+                copy([group], gate, run * width, target, width)
+                copy([group], rest, run * width, INNER + target, width)
+        copy(everyone, rest, G, 2 * INNER, 2 * STATE)
+        copy(everyone, rest, G + 2 * STATE, 2 * INNER + 2 * STATE, HEADS)
 
     sec_out[...] = sec_ref[...]
     ig_out[...] = ig_ref[...]

time: 378 us -> 375 us (level)
  Pallas kernels: 376 us -> 371 us
    pallas_call x1, Pallas kernels: 180 us -> 175 us  [backward_call(): pl.pallas_call(functools.partial(backward_kernel, g, n, w, rows), out_sha...]
where the time goes in v9:
time: 375 us; the launch traced here: 372 us
  Pallas kernels  371 us (99%)
    pallas_call x1, Pallas kernels, forward_call(): pl.pallas_call(functools.partial(forward_kernel, g, n, w, rows), out_shap...  184 us
    pallas_call x1, Pallas kernels, backward_call(): pl.pallas_call(functools.partial(backward_kernel, g, n, w, rows), out_sha...  175 us
    pallas_call x1, Pallas kernels, layout_call(): pl.pallas_call(lambda core_ref, *refs: layout_kernel(g, *refs), grid_spec...  11.7 us

profile of v9, /device:TPU:8, one launch (start us, length us, event | category | flops | bytes accessed | tf_op | source)
XLA Modules:
  0.0 372.2 jit_solution(12235020697462740772)
XLA Ops:
  0.6 184.4 %forward.1 = (f32[2,128,1536]{2,1,0:T(8,128)}, f32[128,1536]{1,0:T(8,128)}, f32[8,128]{1,0:T(8,128)}, f32[128,1536]{1,0:T(8,128)}, bf16[512,1536]{1,0:T(8,128)(2...) custom-call(f32[2,1,128,1536]{3,2,1,0:T(8,128)} %refs_13_.1, ...), custom_call_target="tpu_custom_call" | custom-call | tf_op jit(solution)/shard_map/forward/pallas_call | solution.py:852
  185.0 175.3 %backward.1 = (f32[2,128,1536]{2,1,0:T(8,128)}, bf16[2,4,928,384]{3,2,1,0:T(8,128)(2,1)}, bf16[2,4,96,1536]{3,2,1,0:T(8,128)(2,1)}, bf16[4,928,384]{2,1,0:T(8,12...) custom-call(f32[2,8,3456]{2,1,0:T(8,128)} %get-tuple-element.43.refs, ...), custom_call_target="tpu_custom_call" | custom-call | tf_op jit(solution)/shard_map/backward/pallas_call | solution.py:1428
  360.3 11.7 %layout.1 = (f32[6448,384]{1,0:T(8,128)}, f32[4,2,96,1536]{3,2,1,0:T(8,128)}, f32[2,128,1536]{2,1,0:T(8,128)}, f32[2,128,1536]{2,1,0:T(8,128)}, f32[1,1536]{1,0:...) custom-call(s32[1]{0:T(128)} %bitcast.core_ref, ...), custom_call_target="tpu_custom_call" | custom-call | tf_op jit(solution)/shard_map/layout/pallas_call | solution.py:1592

commit v10 on v9

--- a/solution.py
+++ b/solution.py
@@ -257,8 +257,8 @@
         d_step = d_dt + d_rate * hp_ref[1:2, :]
         d_raw = d_step * sigmoid(step_inputs(proj_ref, at, hp_ref, sel_ref, dt_at))
         proj_ref[at, dt_at : dt_at + 128] = dot(d_raw.astype(BF), sel_ref[...], 1, 1).astype(BF)
-        gh_ref[0:1, :] += jnp.sum(d_raw, axis=0, keepdims=True)
-        gh_ref[1:2, :] += jnp.sum(d_rate * rate, axis=0, keepdims=True)
+        gh_ref[:, 0:128] += jnp.sum(d_raw, axis=0, keepdims=True)
+        gh_ref[:, 128:256] += jnp.sum(d_rate * rate, axis=0, keepdims=True)
         return 0
 
     lax.fori_loop(0, nb, chunk, 0)
@@ -973,7 +973,7 @@
     meet_all(((SEQ, n), (WT, w), (SECTION, 2)))
     r.sm[...] = jnp.zeros_like(r.sm)
     r.sel[...] = step_select(g, here).astype(BF)
-    r.gain[here] = jnp.zeros((8, D), F32)
+    r.gain[here] = jnp.zeros((8, D // 4), F32)
     open_sends, record = [], {}
     line = w == 4
     arrivals = r.got if r.got.shape[0] == n - 1 else r.far
@@ -1178,9 +1178,9 @@
         conv = r.packs.at[layer, :, 0:CX]
         head = r.packs.at[layer, :, CX : CX + 128]
         wide = r.packs.at[layer, :, CX + 128 : gain_at]
-        g_conv = r.sm.at[layer, :, 0:CX]
-        g_head = r.sm.at[layer, :, CX : CX + 128]
-        g_wide = r.sm.at[layer, :, CX + 128 : gain_at]
+        g_conv = r.sm.at[layer, 0:5, :]
+        g_head = r.sm.at[layer, 7:8, 0:256]
+        g_wide = r.sm.at[layer, 5:7, 0:G]
         done(first)
 
         def d_normed(lanes):
@@ -1286,7 +1286,10 @@
             above = r.cot[at, :] if layer == 1 else r.grads[1, at, :]
             inv = lax.rsqrt(jnp.mean(h * h, axis=1, keepdims=True) + EPSILON)
             normed = h * inv
-            r.gain[here, layer : layer + 1, :] += jnp.sum(d_in * normed, axis=0, keepdims=True)
+            gains_here = jnp.sum(d_in * normed, axis=0, keepdims=True)
+            for q in range(4):
+                row = slice(4 * layer + q, 4 * layer + q + 1)
+                r.gain[here, row, :] += gains_here[:, q * (D // 4) : (q + 1) * (D // 4)]
             d_s = d_in * r.packs[layer, 0:1, gain_at:]
             d_h = above + inv * (d_s - normed * jnp.mean(d_s * normed, axis=1, keepdims=True))
             r.grads[layer, at, :] = d_h
@@ -1404,9 +1407,9 @@
         go=S((2, n, o_half, D), BF),
         gi_sib=S((n, g.half, lanes_of), BF),
         go_sib=S((n, o_half, D), BF),
-        small=S((n, 8, PK - D), F32),
+        small=S((n, 8, CX), F32),
         far=S((n - 1, rows, D) if spill else (8, 128), BF),
-        late=S((8, D), F32),
+        late=S((8, D // 4), F32),
     )
     scratch = [
         S((2, 8, PK), F32), S((NC, D), BF), S((G, D), BF), S((L, D), BF), S((L, NC), BF), S((L, G), BF),
@@ -1416,8 +1419,8 @@
         S((n, rows, D), BF), S((1 if spill else n - 1, rows, D), BF), S((8, 128), F32), S((rows, 128), F32), S((2, rows, D), F32),
         S((NC, D), BF), S((G, D), BF), S((g.half, D), BF), S((G // 2, D), BF),
         S((2, w - 1, g.half, lanes_of), BF),
-        S((2, w - 1, o_half, D), BF), S((2, g.half, lanes_of), BF), S((2, o_half, D), BF), S((2, 8, PK - D), F32), S((8, PK - D), F32), S((w - 1, 8, PK - D), F32), S((8, PK - D), F32),
-        S((128, 128), BF), S((n, 8, D), F32), S((w, 8, D), F32), S((2, 8, D), F32),
+        S((2, w - 1, o_half, D), BF), S((2, g.half, lanes_of), BF), S((2, o_half, D), BF), S((2, 8, CX), F32), S((8, CX), F32), S((w - 1, 8, CX), F32), S((8, CX), F32),
+        S((128, 128), BF), S((n, 8, D // 4), F32), S((w, 8, D // 4), F32), S((2, 8, D // 4), F32),
         S((2, rows // 2, D), BF),
     ]
     remote = 2 * (4 * (w + w + n) + n - 1) + 2 * (n - 1) + 40 + 2 * (w - 1) + 2 * (n - 1) + n
@@ -1546,7 +1549,7 @@
         to_ids = lax.broadcasted_iota(jnp.int32, (128, HEADS), 1)
         picks = [one_hot((to_ids == head_of(g, group, from_ids)) & (from_ids < g.heads)) for group in range(n)]
         exact = lax.Precision.HIGHEST
-        head_at, wide_at, gain_at = g.CX, g.CX + 128, g.CX + 128 + G
+        head_at = g.CX
 
         def small(group, columns):
             return small_ref[group, :, columns]
@@ -1556,24 +1559,28 @@
             conv = halves_of_heads(g, small, 0, head)
             conv_ref[:, at] = conv[0:KERNEL]
             bias_ref[:, at] = conv[KERNEL : KERNEL + 1]
-            gate_ref[:, at] = halves_of_heads(g, small, wide_at, head)[0:1]
+            gate_ref[:, at] = conv[5:6]
         conv = small(0, slice(G, head_at))
         for group in range(1, n):
             conv = conv + small(group, slice(G, head_at))
         conv_ref[:, INNER:] = conv[0:KERNEL]
         bias_ref[:, INNER:] = conv[KERNEL : KERNEL + 1]
-        norm_ref[...] = jnp.where(first_core, late_ref[0:1, :], late_ref[1:2, :])
-        heads = jnp.zeros((8, HEADS), F32)
+        for q in range(4):
+            late = jnp.where(first_core, late_ref[q : q + 1, :], late_ref[4 + q : 5 + q, :])
+            norm_ref[:, q * (D // 4) : (q + 1) * (D // 4)] = late
+        biases = jnp.zeros((8, HEADS), F32)
+        rates = jnp.zeros((8, HEADS), F32)
         skips = jnp.zeros((8, HEADS), F32)
         wide_from = lax.broadcasted_iota(jnp.int32, (G, HEADS), 0)
         wide_to = lax.broadcasted_iota(jnp.int32, (G, HEADS), 1)
         for group in range(n):
-            heads = heads + dot(small(group, slice(head_at, wide_at)), picks[group], 1, 0, exact)
+            biases = biases + dot(small(group, slice(0, 128)), picks[group], 1, 0, exact)
+            rates = rates + dot(small(group, slice(128, 256)), picks[group], 1, 0, exact)
             pick = (wide_to == head_of(g, group, wide_from // HEAD_DIM)) & (wide_from < g.chans)
-            skips = skips + dot(small(group, slice(wide_at, gain_at)), one_hot(pick), 1, 0, exact)
-        dtb_ref[...] = heads[0:1]
-        a_ref[...] = heads[1:2]
-        skip_ref[...] = skips[1:2]
+            skips = skips + dot(small(group, slice(0, G)), one_hot(pick), 1, 0, exact)
+        dtb_ref[...] = biases[7:8]
+        a_ref[...] = rates[7:8]
+        skip_ref[...] = skips[6:7]
 
 
 def layout_call(g, core, gi, gi_sib, go, go_sib, small, late, sec, ig):
@@ -1600,7 +1607,7 @@
                 pl.BlockSpec((1, n, out_half, out_lanes), lambda t, c: (c[0], 0, 0, t)),
                 pl.BlockSpec((n, out_half, out_lanes), lambda t, c: (0, 0, t)),
                 pl.BlockSpec((n, 8, PK), lambda t, c: (0, 0, 0)),
-                pl.BlockSpec((8, D), lambda t, c: (0, 0)),
+                pl.BlockSpec((8, D // 4), lambda t, c: (0, 0)),
                 rows_spec,
                 rows_spec,
             ],

time: 375 us -> 371 us (0.989)
  no operation moved by 1% of the time
where the time goes in v10:
time: 371 us; the launch traced here: 369 us
  Pallas kernels  368 us (99%)
    pallas_call x1, Pallas kernels, forward_call(): pl.pallas_call(functools.partial(forward_kernel, g, n, w, rows), out_shap...  184 us
    pallas_call x1, Pallas kernels, backward_call(): pl.pallas_call(functools.partial(backward_kernel, g, n, w, rows), out_sha...  172 us
    pallas_call x1, Pallas kernels, layout_call(): pl.pallas_call(lambda core_ref, *refs: layout_kernel(g, *refs), grid_spec...  11.7 us

profile of v10, /device:TPU:8, one launch (start us, length us, event | category | flops | bytes accessed | tf_op | source)
XLA Modules:
  0.0 369.0 jit_solution(14695516661659109684)
XLA Ops:
  0.6 184.4 %forward.1 = (f32[2,128,1536]{2,1,0:T(8,128)}, f32[128,1536]{1,0:T(8,128)}, f32[8,128]{1,0:T(8,128)}, f32[128,1536]{1,0:T(8,128)}, bf16[512,1536]{1,0:T(8,128)(2...) custom-call(f32[2,1,128,1536]{3,2,1,0:T(8,128)} %refs_13_.1, ...), custom_call_target="tpu_custom_call" | custom-call | tf_op jit(solution)/shard_map/forward/pallas_call | solution.py:852
  185.0 172.1 %backward.1 = (f32[2,128,1536]{2,1,0:T(8,128)}, bf16[2,4,928,384]{3,2,1,0:T(8,128)(2,1)}, bf16[2,4,96,1536]{3,2,1,0:T(8,128)(2,1)}, bf16[4,928,384]{2,1,0:T(8,12...) custom-call(f32[2,8,3456]{2,1,0:T(8,128)} %get-tuple-element.43.refs_, ...), custom_call_target="tpu_custom_call" | custom-call | tf_op jit(solution)/shard_map/backward/pallas_call | solution.py:1431
  357.1 11.7 %layout.1 = (f32[6448,384]{1,0:T(8,128)}, f32[4,2,96,1536]{3,2,1,0:T(8,128)}, f32[2,128,1536]{2,1,0:T(8,128)}, f32[2,128,1536]{2,1,0:T(8,128)}, f32[1,1536]{1,0:...) custom-call(s32[1]{0:T(128)} %bitcast.core_ref, ...), custom_call_target="tpu_custom_call" | custom-call | tf_op jit(solution)/shard_map/layout/pallas_call | solution.py:1599

commit v11 on v10

--- a/solution.py
+++ b/solution.py
@@ -309,7 +309,7 @@
         self.NC = 2 * self.G + 2 * STATE + 128
         self.rest = self.G + 2 * STATE + 64
         self.half = (self.G + self.rest) // 2
-        self.cut = self.rest // 128 * 64
+        self.cut = self.rest * 3 // 256 * 64
 
 
 def head_of(g, here, local_head):

time: 371 us -> 372 us (level)
  no operation moved by 1% of the time
where the time goes in v11:
time: 372 us; the launch traced here: 371 us
  Pallas kernels  370 us (99%)
    pallas_call x1, Pallas kernels, forward_call(): pl.pallas_call(functools.partial(forward_kernel, g, n, w, rows), out_shap...  184 us
    pallas_call x1, Pallas kernels, backward_call(): pl.pallas_call(functools.partial(backward_kernel, g, n, w, rows), out_sha...  174 us
    pallas_call x1, Pallas kernels, layout_call(): pl.pallas_call(lambda core_ref, *refs: layout_kernel(g, *refs), grid_spec...  11.7 us

profile of v11, /device:TPU:8, one launch (start us, length us, event | category | flops | bytes accessed | tf_op | source)
XLA Modules:
  0.0 371.0 jit_solution(1768524183770313633)
XLA Ops:
  0.6 184.4 %forward.1 = (f32[2,128,1536]{2,1,0:T(8,128)}, f32[128,1536]{1,0:T(8,128)}, f32[8,128]{1,0:T(8,128)}, f32[128,1536]{1,0:T(8,128)}, bf16[512,1536]{1,0:T(8,128)(2...) custom-call(f32[2,1,128,1536]{3,2,1,0:T(8,128)} %refs_13_.1, ...), custom_call_target="tpu_custom_call" | custom-call | tf_op jit(solution)/shard_map/forward/pallas_call | solution.py:852
  185.0 174.1 %backward.1 = (f32[2,128,1536]{2,1,0:T(8,128)}, bf16[2,4,928,384]{3,2,1,0:T(8,128)(2,1)}, bf16[2,4,96,1536]{3,2,1,0:T(8,128)(2,1)}, bf16[4,928,384]{2,1,0:T(8,12...) custom-call(f32[2,8,3456]{2,1,0:T(8,128)} %get-tuple-element.43.refs_, ...), custom_call_target="tpu_custom_call" | custom-call | tf_op jit(solution)/shard_map/backward/pallas_call | solution.py:1431
  359.1 11.7 %layout.1 = (f32[6448,384]{1,0:T(8,128)}, f32[4,2,96,1536]{3,2,1,0:T(8,128)}, f32[2,128,1536]{2,1,0:T(8,128)}, f32[2,128,1536]{2,1,0:T(8,128)}, f32[1,1536]{1,0:...) custom-call(s32[1]{0:T(128)} %bitcast.core_ref, ...), custom_call_target="tpu_custom_call" | custom-call | tf_op jit(solution)/shard_map/layout/pallas_call | solution.py:1599
